TPU v7x, 256 devices: a whole 4x4x8 slice. The times are simulated.
256 devices in a mesh: ctx: 32 (over x, y, core), hg: 8 (over z).
Axes of the slice: x: 4, y: 4, z: 8, core: 2. Of those that a mesh axis runs over, the one named last changes fastest.
Arguments:
- query_states: bfloat16 [8192, 12288], P(('ctx', 'hg')), may hold values from -51 to 51
- key_states: bfloat16 [8192, 1024], P(('ctx', 'hg')), may hold values from -5 to 5
- value_states: bfloat16 [8192, 1024], P(('ctx', 'hg')), may hold values from -6 to 6
- out_grad: bfloat16 [8192, 12288], P(('ctx', 'hg')), may hold values from -6 to 6
- doc_starts: int32 [16], replicated, may hold values from 0 to 8190, as said below
- doc_tenant: int32 [16], replicated, may hold values from 0 to 7
- tenant_weight: float32 [8], replicated, may hold values from 0.25 to 4
Outputs:
- attended: bfloat16 [8192, 12288], P(('ctx', 'hg'))
- query_grad: bfloat16 [8192, 12288], P(('ctx', 'hg'))
- key_grad: bfloat16 [8192, 1024], P(('ctx', 'hg'))
- value_grad: bfloat16 [8192, 1024], P(('ctx', 'hg'))
Inputs may be any that keep to these rules, and one draw needn't show every extreme that they name: `doc_starts`: the documents tile the row in order: the first starts at 0, each later start is greater than the one before, the last document has exactly 2 tokens and ends at 8192; every document has 2 or more tokens, none has more than 1024, and one has exactly 1024.
All inputs are finite; a program needn't handle non-finite values.
Results may differ from a plain program's by a relative error of at most 0.035.
Values may be sent and summed in bfloat16 or wider, within the bound.
No kernel may reach another device: no remote copies, remote signals or barrier semaphores. Data moves between devices by JAX's collectives and lax.ppermute only.
A program may use at most 128 MiB of HBM per device.

v0:
```python
import jax
import jax.numpy as jnp
from jax import lax
from jax.sharding import PartitionSpec as P

HD = 128
SPAN = 4


NEG = -1e30


def passed_along(x, axis, by):
    devices = lax.axis_size(axis)
    pairs = [(i, i + by) for i in range(devices) if 0 <= i + by < devices]
    return lax.ppermute(x, axis, pairs)


def place_rows(start_row, row_count, doc_starts):
    position = start_row + jnp.arange(row_count, dtype=jnp.int32)
    documents = jnp.sum((doc_starts[None, :] <= position[:, None]).astype(jnp.int32), axis=1) - 1
    return (position, documents)


def local(query_states, key_states, value_states, out_grad, doc_starts, doc_tenant, tenant_weight):
    queries, keys_local, values_local, grad_rows = (
        lax.all_to_all(query_states, "hg", split_axis=1, concat_axis=0, tiled=True),
        lax.all_to_all(key_states, "hg", split_axis=1, concat_axis=0, tiled=True),
        lax.all_to_all(value_states, "hg", split_axis=1, concat_axis=0, tiled=True),
        lax.all_to_all(out_grad, "hg", split_axis=1, concat_axis=0, tiled=True),
    )
    row_count = queries.shape[0]
    head_count = queries.shape[1] // HD
    queries = queries.reshape(row_count, head_count, HD)
    grad_rows = grad_rows.reshape(row_count, head_count, HD)
    scale = HD ** (-0.5)
    this_device = lax.axis_index("ctx")
    first_row = this_device * row_count
    query_pos, query_doc = place_rows(first_row, row_count, doc_starts)
    doc_range = jnp.arange(doc_starts.shape[0], dtype=jnp.int32)
    tenants = jnp.sum(
        jnp.where(query_doc[:, None] == doc_range[None, :], doc_tenant[None, :], 0), axis=1
    )
    tenant_range = jnp.arange(tenant_weight.shape[0], dtype=jnp.int32)
    scaling = jnp.sum(
        jnp.where(tenants[:, None] == tenant_range[None, :], tenant_weight[None, :], 0.0), axis=1
    )
    weighted = (scaling[:, None, None] * grad_rows.astype(jnp.float32)).astype(jnp.bfloat16)
    window_rows = (SPAN + 1) * row_count
    key_blocks = []
    value_blocks = []
    carried_keys, carried_values = (keys_local, values_local)
    for offset in range(1, SPAN + 1):
        carried_keys, carried_values = passed_along((carried_keys, carried_values), "ctx", 1)
        key_blocks.insert(0, carried_keys)
        value_blocks.insert(0, carried_values)
    window_keys = jnp.concatenate(key_blocks + [keys_local], axis=0)
    window_values = jnp.concatenate(value_blocks + [values_local], axis=0)
    begin_row = (this_device - SPAN) * row_count
    key_pos, key_doc = place_rows(begin_row, window_rows, doc_starts)
    visible = ((key_pos[None, :] <= query_pos[:, None]) & (key_doc[None, :] == query_doc[:, None]))[
        None
    ]
    scores = (
        jnp.einsum("thd,kd->htk", queries, window_keys, preferred_element_type=jnp.float32) * scale
    )
    row_max = jnp.max(jnp.where(visible, scores, NEG), axis=2, keepdims=True)
    row_total = jnp.sum(jnp.where(visible, jnp.exp(scores - row_max), 0.0), axis=2, keepdims=True)
    log_total = row_max + jnp.log(row_total)
    probability = jnp.where(visible, jnp.exp(scores - log_total), 0.0)
    weights = probability.astype(jnp.bfloat16)
    attended = jnp.einsum(
        "htk,kd->thd", weights, window_values, preferred_element_type=jnp.float32
    ).astype(jnp.bfloat16)
    row_delta = jnp.sum(weighted.astype(jnp.float32) * attended.astype(jnp.float32), axis=2)
    value_push = jnp.einsum(
        "thd,kd->htk", weighted, window_values, preferred_element_type=jnp.float32
    )
    score_grad = (scale * probability * (value_push - row_delta.T[:, :, None])).astype(jnp.bfloat16)
    query_grad = jnp.einsum(
        "htk,kd->thd", score_grad, window_keys, preferred_element_type=jnp.float32
    ).astype(jnp.bfloat16)
    key_part = jnp.einsum("htk,thd->kd", score_grad, queries, preferred_element_type=jnp.float32)
    value_part = jnp.einsum("htk,thd->kd", weights, weighted, preferred_element_type=jnp.float32)
    key_total = key_part[:row_count]
    value_total = value_part[:row_count]
    for offset in range(1, SPAN + 1):
        key_total, value_total = (
            passed_along(key_total.astype(jnp.bfloat16), "ctx", -1).astype(key_total.dtype),
            passed_along(value_total.astype(jnp.bfloat16), "ctx", -1).astype(value_total.dtype),
        )
        lower = offset * row_count
        key_total = key_total + key_part[lower : lower + row_count]
        value_total = value_total + value_part[lower : lower + row_count]
    returned = (
        lax.all_to_all(
            attended.reshape(row_count, head_count * HD),
            "hg",
            split_axis=0,
            concat_axis=1,
            tiled=True,
        ),
        lax.all_to_all(
            query_grad.reshape(row_count, head_count * HD),
            "hg",
            split_axis=0,
            concat_axis=1,
            tiled=True,
        ),
        lax.all_to_all(
            key_total.astype(jnp.bfloat16), "hg", split_axis=0, concat_axis=1, tiled=True
        ),
        lax.all_to_all(
            value_total.astype(jnp.bfloat16), "hg", split_axis=0, concat_axis=1, tiled=True
        ),
    )
    return (returned[0], returned[1], returned[2], returned[3])


def solution(mesh):
    return jax.shard_map(
        local,
        mesh=mesh,
        in_specs=(
            P(("ctx", "hg"), None),
            P(("ctx", "hg"), None),
            P(("ctx", "hg"), None),
            P(("ctx", "hg"), None),
            P(),
            P(),
            P(),
        ),
        out_specs=(
            P(("ctx", "hg"), None),
            P(("ctx", "hg"), None),
            P(("ctx", "hg"), None),
            P(("ctx", "hg"), None),
        ),
        check_vma=False,
    )
```

profile of v0, /device:TPU:25, one launch (start us, length us, event | category | flops | bytes accessed | tf_op | source)
XLA Modules:
  0.0 231.0 jit_solution(10440835719688965157)
XLA Ops:
  2.1 8.2 %all-to-all-start.1 = ((bf16[32,8,128]{2,0,1:T(8,128)(2,1)}), bf16[32,8,128]{2,0,1:T(8,128)(2,1)S(1)}, u32[]{:S(2)}, u32[]{:S(2)}) async-start(bf16[32,8,128]{2,0,1:T(8,128)(2,1)} %copy_bitcast_fusion.4), calls=%async_computation.1 | async-start | bytes 131072 | tf_op jit(solution)/shard_map/all_to_all | solution.py:28
  13.3 4.2 %all-to-all-done.1 = bf16[32,8,128]{2,0,1:T(8,128)(2,1)S(1)} async-done(((bf16[32,8,128]{2,0,1:T(8,128)(2,1)}), bf16[32,8,128]{2,0,1:T(8,128)(2,1)S(1)}, u32[]{:S(2)}, u32[]{:S(2)}) %all-to-all-start.1) | async-done | bytes 65568 | tf_op jit(solution)/shard_map/all_to_all | solution.py:28
  17.5 3.4 %all-to-all-start = ((bf16[32,8,128]{2,0,1:T(8,128)(2,1)}), bf16[32,8,128]{2,0,1:T(8,128)(2,1)S(1)}, u32[]{:S(2)}, u32[]{:S(2)}) async-start(bf16[32,8,128]{2,0,1:T(8,128)(2,1)} %copy_bitcast_fusion.5), calls=%async_computation | async-start | bytes 131072 | tf_op jit(solution)/shard_map/all_to_all | solution.py:29
  20.9 4.8 %collective-permute-start.4 = (bf16[256,128]{1,0:T(8,128)(2,1)S(1)}, bf16[256,128]{1,0:T(8,128)(2,1)S(1)}, u32[]{:S(2)}, u32[]{:S(2)}) collective-permute-start(bf16[256,128]{1,0:T(8,128)(2,1)S(1)} %bitcast.115), channel_id=1, source_target_pairs={{0,8},{8,16},{16,24},{24,32},{32,40},{40,48},{48,56},{56,64},{64,7... | collective-permute-start | bytes 196616 | tf_op jit(solution)/shard_map/ppermute | solution.py:16
  28.0 6.5 %all-to-all-start.2 = ((bf16[32,8,1536]{2,0,1:T(8,128)(2,1)}), bf16[32,8,1536]{2,0,1:T(8,128)(2,1)S(1)}, u32[]{:S(2)}, u32[]{:S(2)}) async-start(bf16[32,8,1536]{2,0,1:T(8,128)(2,1)} %bitcast.105), calls=%async_computation.2 | async-start | bytes 1572864 | tf_op jit(solution)/shard_map/all_to_all | solution.py:27
  49.5 4.3 %collective-permute-start.2 = (bf16[256,128]{0,1:T(8,128)(2,1)S(1)}, bf16[256,128]{0,1:T(8,128)(2,1)S(1)}, u32[]{:S(2)}, u32[]{:S(2)}) collective-permute-start(bf16[256,128]{0,1:T(8,128)(2,1)S(1)} %collective-permute-done.1), channel_id=1, source_target_pairs={{0,8},{8,16},{16,24},{24,32},{32,40},{40,48},{48,56},{56,64},{64,7... | collective-permute-start | bytes 196616 | tf_op jit(solution)/shard_map/ppermute | solution.py:16
  57.7 3.8 %collective-permute-start.3 = (bf16[256,128]{0,1:T(8,128)(2,1)S(1)}, bf16[256,128]{0,1:T(8,128)(2,1)S(1)}, u32[]{:S(2)}, u32[]{:S(2)}) collective-permute-start(bf16[256,128]{0,1:T(8,128)(2,1)S(1)} %collective-permute-done.2), channel_id=1, source_target_pairs={{0,8},{8,16},{16,24},{24,32},{32,40},{40,48},{48,56},{56,64},{64,7... | collective-permute-start | bytes 196616 | tf_op jit(solution)/shard_map/ppermute | solution.py:16
  63.6 6.8 %all-to-all-start.4 = ((bf16[32,8,1536]{2,0,1:T(8,128)(2,1)}), bf16[32,8,1536]{2,0,1:T(8,128)(2,1)S(1)}, u32[]{:S(2)}, u32[]{:S(2)}) async-start(bf16[32,8,1536]{2,0,1:T(8,128)(2,1)} %bitcast.104), calls=%async_computation.4 | async-start | bytes 1572864 | tf_op jit(solution)/shard_map/all_to_all | solution.py:30
  71.0 7.0 %fusion.2 = (f32[12,256]{1,0:T(8,128)S(1)}, f32[1280,256,12]{1,0,2:T(8,128)}) fusion(pred[256,1280]{0,1:T(8,128)(4,1)S(1)} %compare_and_fusion, bf16[256,12,128]{2,1,0:T(8,128)(2,1)S(1)} %reshape.132, bf16[1280,128]{1,0:T(8,128)(2,1)S(1)} %constant_dynamic-update-slice_fusion.5), kind=kOutput, calls=%fused_computation.6 | convolution fusion | flops 1018426368 | bytes 17182720 | tf_op jit(solution)/shard_map/thd,kd->htk/dot_general | solution.py:65
  78.0 8.6 %fusion.5 = f32[12,256]{1,0:T(8,128)S(1)} fusion(f32[1280,256,12]{1,0,2:T(8,128)} %get-tuple-element.7, f32[12,256]{1,0:T(8,128)S(1)} %get-tuple-element.6, pred[256,1280]{0,1:T(8,128)(4,1)S(1)} %compare_and_fusion), kind=kLoop, calls=%fused_computation.9 | loop fusion | flops 15725568 | bytes 16080896 | tf_op jit(solution)/shard_map/reduce_sum | solution.py:68
  86.6 7.4 %all-to-all-done.4 = bf16[32,8,1536]{2,0,1:T(8,128)(2,1)S(1)} async-done(((bf16[32,8,1536]{2,0,1:T(8,128)(2,1)}), bf16[32,8,1536]{2,0,1:T(8,128)(2,1)S(1)}, u32[]{:S(2)}, u32[]{:S(2)}) %all-to-all-start.4) | async-done | bytes 786464 | tf_op jit(solution)/shard_map/all_to_all | solution.py:30
  101.0 10.4 %multiply_reduce_fusion = (f32[256,12]{0,1:T(8,128)S(1)}, bf16[256,12,128]{0,2,1:T(8,128)(2,1)S(1)}, bf16[256,12,128]{0,2,1:T(8,128)(2,1)}) fusion(f32[256,12,128]{0,2,1:T(8,128)} %copy.94, f32[256]{0:T(256)} %select_reduce_fusion.1, f32[1280,256,12]{1,0,2:T(8,128)} %get-tuple-element.7, f32[12,256]{1,0:T(8,128)S(1)} %log_add_fusion, ...), kind=kOutput, calls=%fused_computation.16 | convolution fusion | flops 1025111040 | bytes 19555328 | tf_op jit(solution)/shard_map/htk,kd->thd/dot_general | solution.py:72
  116.8 7.2 %fusion.1 = bf16[12,256,1280]{1,2,0:T(8,128)(2,1)} fusion(f32[1280,256,12]{1,0,2:T(8,128)S(1)} %bitcast.107, bf16[256,12,128]{0,2,1:T(8,128)(2,1)S(1)} %get-tuple-element.5, f32[12,256]{1,0:T(8,128)S(1)} %bitcast.118, f32[12,256]{1,0:T(8,128)S(1)} %log_add_fusion, pred[256,1280]{0,1:T(8,128)(4,1)S(1)} %compare_and_fusion, bf16[1280,128]{0,1:T(8,128)(2,1)S(1)} %copy-done.6), kind=kOutput, calls=%fused_computation.2 | convolution fusion | flops 1034158080 | bytes 25059328 | tf_op jit(solution)/shard_map/thd,kd->htk/dot_general | solution.py:76
  124.1 5.5 %convolution_bitcast_fusion.1 = f32[1280,128]{1,0:T(8,128)S(1)} fusion(bf16[12,256,1280]{1,2,0:T(8,128)(2,1)} %fusion.1, bf16[256,12,128]{2,1,0:T(8,128)(2,1)S(1)} %copy-done.2), kind=kOutput, calls=%fused_computation.14 | convolution fusion | flops 1006632960 | bytes 9306112 | tf_op jit(solution)/shard_map/htk,thd->kd/dot_general | solution.py:83
  133.5 3.7 %collective-permute-done.8 = bf16[256,128]{1,0:T(8,128)(2,1)S(1)} collective-permute-done((bf16[256,128]{1,0:T(8,128)(2,1)S(1)}, bf16[256,128]{1,0:T(8,128)(2,1)S(1)}, u32[]{:S(2)}, u32[]{:S(2)}) %collective-permute-start.8) | collective-permute-done | bytes 65568 | tf_op jit(solution)/shard_map/ppermute | solution.py:16
  141.3 3.7 %collective-permute-done.9 = bf16[256,128]{1,0:T(8,128)(2,1)S(1)} collective-permute-done((bf16[256,128]{1,0:T(8,128)(2,1)S(1)}, bf16[256,128]{1,0:T(8,128)(2,1)S(1)}, u32[]{:S(2)}, u32[]{:S(2)}) %collective-permute-start.9) | collective-permute-done | bytes 65568 | tf_op jit(solution)/shard_map/ppermute | solution.py:16
  149.0 3.7 %collective-permute-done.10 = bf16[256,128]{1,0:T(8,128)(2,1)S(1)} collective-permute-done((bf16[256,128]{1,0:T(8,128)(2,1)S(1)}, bf16[256,128]{1,0:T(8,128)(2,1)S(1)}, u32[]{:S(2)}, u32[]{:S(2)}) %collective-permute-start.10) | collective-permute-done | bytes 65568 | tf_op jit(solution)/shard_map/ppermute | solution.py:16
  161.3 4.6 %all-to-all-done.7 = bf16[8,32,128]{2,1,0:T(8,128)(2,1)S(1)} async-done(((bf16[8,32,128]{2,1,0:T(8,128)(2,1)}), bf16[8,32,128]{2,1,0:T(8,128)(2,1)S(1)}, u32[]{:S(2)}, u32[]{:S(2)}) %all-to-all-start.7) | async-done | bytes 65568 | tf_op jit(solution)/shard_map/all_to_all | solution.py:113
  165.9 3.4 %all-to-all-start.6 = ((bf16[8,32,128]{2,1,0:T(8,128)(2,1)}), bf16[8,32,128]{2,1,0:T(8,128)(2,1)S(1)}, u32[]{:S(2)}, u32[]{:S(2)}) async-start(bf16[8,32,128]{2,1,0:T(8,128)(2,1)} %bitcast.19), calls=%async_computation.6 | async-start | bytes 131072 | tf_op jit(solution)/shard_map/all_to_all | solution.py:110
  169.3 4.6 %fusion.10 = bf16[256,12,128]{0,2,1:T(8,128)(2,1)S(1)} fusion(bf16[12,256,1280]{1,2,0:T(8,128)(2,1)} %fusion.1, bf16[1280,128]{1,0:T(8,128)(2,1)} %copy-done.3), kind=kOutput, calls=%fused_computation.22 | convolution fusion | flops 1007026176 | bytes 8978432 | tf_op jit(solution)/shard_map/htk,kd->thd/dot_general | solution.py:80
  176.4 6.5 %all-to-all-start.5 = ((bf16[8,32,1536]{2,1,0:T(8,128)(2,1)}), bf16[8,32,1536]{2,1,0:T(8,128)(2,1)S(1)}, u32[]{:S(2)}, u32[]{:S(2)}) async-start(bf16[8,32,1536]{2,1,0:T(8,128)(2,1)} %all_to_all.123), calls=%async_computation.5 | async-start | bytes 1572864 | tf_op jit(solution)/shard_map/all_to_all | solution.py:103
  185.3 18.6 %all-to-all-done.5 = bf16[8,32,1536]{2,1,0:T(8,128)(2,1)S(1)} async-done(((bf16[8,32,1536]{2,1,0:T(8,128)(2,1)}), bf16[8,32,1536]{2,1,0:T(8,128)(2,1)S(1)}, u32[]{:S(2)}, u32[]{:S(2)}) %all-to-all-start.5) | async-done | bytes 786464 | tf_op jit(solution)/shard_map/all_to_all | solution.py:103
  203.9 3.5 %all-to-all-start.3 = ((bf16[8,32,1536]{2,1,0:T(8,128)(2,1)}), bf16[8,32,1536]{2,1,0:T(8,128)(2,1)S(1)}, u32[]{:S(2)}, u32[]{:S(2)}) async-start(bf16[8,32,1536]{2,1,0:T(8,128)(2,1)} %all_to_all.117), calls=%async_computation.3 | async-start | bytes 1572864 | tf_op jit(solution)/shard_map/all_to_all | solution.py:96
  209.7 20.4 %all-to-all-done.3 = bf16[8,32,1536]{2,1,0:T(8,128)(2,1)S(1)} async-done(((bf16[8,32,1536]{2,1,0:T(8,128)(2,1)}), bf16[8,32,1536]{2,1,0:T(8,128)(2,1)S(1)}, u32[]{:S(2)}, u32[]{:S(2)}) %all-to-all-start.3) | async-done | bytes 786464 | tf_op jit(solution)/shard_map/all_to_all | solution.py:96
  (101 shorter events, 68.9 us)
Async XLA Ops:
  2.1 15.4 %all-to-all-start.1 = ((bf16[32,8,128]{2,0,1:T(8,128)(2,1)}), bf16[32,8,128]{2,0,1:T(8,128)(2,1)S(1)}, u32[]{:S(2)}, u32[]{:S(2)}) async-start(bf16[32,8,128]{2,0,1:T(8,128)(2,1)} %copy_bitcast_fusion.4), calls=%async_computation.1 | async-start | bytes 131072 | tf_op jit(solution)/shard_map/all_to_all | solution.py:28
  17.5 10.5 %all-to-all-start = ((bf16[32,8,128]{2,0,1:T(8,128)(2,1)}), bf16[32,8,128]{2,0,1:T(8,128)(2,1)S(1)}, u32[]{:S(2)}, u32[]{:S(2)}) async-start(bf16[32,8,128]{2,0,1:T(8,128)(2,1)} %copy_bitcast_fusion.5), calls=%async_computation | async-start | bytes 131072 | tf_op jit(solution)/shard_map/all_to_all | solution.py:29
  20.9 16.7 %collective-permute-start.4 = (bf16[256,128]{1,0:T(8,128)(2,1)S(1)}, bf16[256,128]{1,0:T(8,128)(2,1)S(1)}, u32[]{:S(2)}, u32[]{:S(2)}) collective-permute-start(bf16[256,128]{1,0:T(8,128)(2,1)S(1)} %bitcast.115), channel_id=1, source_target_pairs={{0,8},{8,16},{16,24},{24,32},{32,40},{40,48},{48,56},{56,64},{64,7... | collective-permute-start | bytes 196616 | tf_op jit(solution)/shard_map/ppermute | solution.py:16
  28.0 34.8 %all-to-all-start.2 = ((bf16[32,8,1536]{2,0,1:T(8,128)(2,1)}), bf16[32,8,1536]{2,0,1:T(8,128)(2,1)S(1)}, u32[]{:S(2)}, u32[]{:S(2)}) async-start(bf16[32,8,1536]{2,0,1:T(8,128)(2,1)} %bitcast.105), calls=%async_computation.2 | async-start | bytes 1572864 | tf_op jit(solution)/shard_map/all_to_all | solution.py:27
  34.7 8.5 %collective-permute-start = (bf16[256,128]{0,1:T(8,128)(2,1)S(1)}, bf16[256,128]{0,1:T(8,128)(2,1)S(1)}, u32[]{:S(2)}, u32[]{:S(2)}) collective-permute-start(bf16[256,128]{0,1:T(8,128)(2,1)S(1)} %copy.85), channel_id=1, source_target_pairs={{0,8},{8,16},{16,24},{24,32},{32,40},{40,48},{48,56},{56,64},{64,7... | collective-permute-start | bytes 196616 | tf_op jit(solution)/shard_map/ppermute | solution.py:16
  37.6 8.5 %collective-permute-start.5 = (bf16[256,128]{1,0:T(8,128)(2,1)S(1)}, bf16[256,128]{1,0:T(8,128)(2,1)S(1)}, u32[]{:S(2)}, u32[]{:S(2)}) collective-permute-start(bf16[256,128]{1,0:T(8,128)(2,1)S(1)} %collective-permute-done.4), channel_id=1, source_target_pairs={{0,8},{8,16},{16,24},{24,32},{32,40},{40,48},{48,56},{56,64},{64,7... | collective-permute-start | bytes 196616 | tf_op jit(solution)/shard_map/ppermute | solution.py:16
  43.2 6.3 %collective-permute-start.1 = (bf16[256,128]{0,1:T(8,128)(2,1)S(1)}, bf16[256,128]{0,1:T(8,128)(2,1)S(1)}, u32[]{:S(2)}, u32[]{:S(2)}) collective-permute-start(bf16[256,128]{0,1:T(8,128)(2,1)S(1)} %collective-permute-done), channel_id=1, source_target_pairs={{0,8},{8,16},{16,24},{24,32},{32,40},{40,48},{48,56},{56,64},{64,7... | collective-permute-start | bytes 196616 | tf_op jit(solution)/shard_map/ppermute | solution.py:16
  46.2 7.7 %collective-permute-start.6 = (bf16[256,128]{1,0:T(8,128)(2,1)S(1)}, bf16[256,128]{1,0:T(8,128)(2,1)S(1)}, u32[]{:S(2)}, u32[]{:S(2)}) collective-permute-start(bf16[256,128]{1,0:T(8,128)(2,1)S(1)} %collective-permute-done.5), channel_id=1, source_target_pairs={{0,8},{8,16},{16,24},{24,32},{32,40},{40,48},{48,56},{56,64},{64,7... | collective-permute-start | bytes 196616 | tf_op jit(solution)/shard_map/ppermute | solution.py:16
  49.5 8.2 %collective-permute-start.2 = (bf16[256,128]{0,1:T(8,128)(2,1)S(1)}, bf16[256,128]{0,1:T(8,128)(2,1)S(1)}, u32[]{:S(2)}, u32[]{:S(2)}) collective-permute-start(bf16[256,128]{0,1:T(8,128)(2,1)S(1)} %collective-permute-done.1), channel_id=1, source_target_pairs={{0,8},{8,16},{16,24},{24,32},{32,40},{40,48},{48,56},{56,64},{64,7... | collective-permute-start | bytes 196616 | tf_op jit(solution)/shard_map/ppermute | solution.py:16
  53.8 7.7 %collective-permute-start.7 = (bf16[256,128]{1,0:T(8,128)(2,1)S(1)}, bf16[256,128]{1,0:T(8,128)(2,1)S(1)}, u32[]{:S(2)}, u32[]{:S(2)}) collective-permute-start(bf16[256,128]{1,0:T(8,128)(2,1)S(1)} %collective-permute-done.6), channel_id=1, source_target_pairs={{0,8},{8,16},{16,24},{24,32},{32,40},{40,48},{48,56},{56,64},{64,7... | collective-permute-start | bytes 196616 | tf_op jit(solution)/shard_map/ppermute | solution.py:16
  57.7 5.1 %collective-permute-start.3 = (bf16[256,128]{0,1:T(8,128)(2,1)S(1)}, bf16[256,128]{0,1:T(8,128)(2,1)S(1)}, u32[]{:S(2)}, u32[]{:S(2)}) collective-permute-start(bf16[256,128]{0,1:T(8,128)(2,1)S(1)} %collective-permute-done.2), channel_id=1, source_target_pairs={{0,8},{8,16},{16,24},{24,32},{32,40},{40,48},{48,56},{56,64},{64,7... | collective-permute-start | bytes 196616 | tf_op jit(solution)/shard_map/ppermute | solution.py:16
  63.6 30.4 %all-to-all-start.4 = ((bf16[32,8,1536]{2,0,1:T(8,128)(2,1)}), bf16[32,8,1536]{2,0,1:T(8,128)(2,1)S(1)}, u32[]{:S(2)}, u32[]{:S(2)}) async-start(bf16[32,8,1536]{2,0,1:T(8,128)(2,1)} %bitcast.104), calls=%async_computation.4 | async-start | bytes 1572864 | tf_op jit(solution)/shard_map/all_to_all | solution.py:30
  114.2 17.4 %collective-permute-start.12 = (bf16[256,128]{1,0:T(8,128)(2,1)S(1)}, bf16[256,128]{1,0:T(8,128)(2,1)S(1)}, u32[]{:S(2)}, u32[]{:S(2)}) collective-permute-start(bf16[256,128]{1,0:T(8,128)(2,1)S(1)} %slice.78), channel_id=1, source_target_pairs={{8,0},{16,8},{24,16},{32,24},{40,32},{48,40},{56,48},{64,56},{72,6... | collective-permute-start | bytes 196616 | tf_op jit(solution)/shard_map/ppermute | solution.py:16
  129.6 7.7 %collective-permute-start.8 = (bf16[256,128]{1,0:T(8,128)(2,1)S(1)}, bf16[256,128]{1,0:T(8,128)(2,1)S(1)}, u32[]{:S(2)}, u32[]{:S(2)}) collective-permute-start(bf16[256,128]{1,0:T(8,128)(2,1)S(1)} %slice.79), channel_id=1, source_target_pairs={{8,0},{16,8},{24,16},{32,24},{40,32},{48,40},{56,48},{64,56},{72,6... | collective-permute-start | bytes 196616 | tf_op jit(solution)/shard_map/ppermute | solution.py:16
  131.6 7.7 %collective-permute-start.13 = (bf16[256,128]{1,0:T(8,128)(2,1)S(1)}, bf16[256,128]{1,0:T(8,128)(2,1)S(1)}, u32[]{:S(2)}, u32[]{:S(2)}) collective-permute-start(bf16[256,128]{1,0:T(8,128)(2,1)S(1)} %fusion.21), channel_id=1, source_target_pairs={{8,0},{16,8},{24,16},{32,24},{40,32},{48,40},{56,48},{64,56},{72,6... | collective-permute-start | bytes 196616 | tf_op jit(solution)/shard_map/ppermute | solution.py:16
  137.3 7.7 %collective-permute-start.9 = (bf16[256,128]{1,0:T(8,128)(2,1)S(1)}, bf16[256,128]{1,0:T(8,128)(2,1)S(1)}, u32[]{:S(2)}, u32[]{:S(2)}) collective-permute-start(bf16[256,128]{1,0:T(8,128)(2,1)S(1)} %fusion.25), channel_id=1, source_target_pairs={{8,0},{16,8},{24,16},{32,24},{40,32},{48,40},{56,48},{64,56},{72,6... | collective-permute-start | bytes 196616 | tf_op jit(solution)/shard_map/ppermute | solution.py:16
  139.3 7.7 %collective-permute-start.14 = (bf16[256,128]{1,0:T(8,128)(2,1)S(1)}, bf16[256,128]{1,0:T(8,128)(2,1)S(1)}, u32[]{:S(2)}, u32[]{:S(2)}) collective-permute-start(bf16[256,128]{1,0:T(8,128)(2,1)S(1)} %fusion.20), channel_id=1, source_target_pairs={{8,0},{16,8},{24,16},{32,24},{40,32},{48,40},{56,48},{64,56},{72,6... | collective-permute-start | bytes 196616 | tf_op jit(solution)/shard_map/ppermute | solution.py:16
  145.0 7.7 %collective-permute-start.10 = (bf16[256,128]{1,0:T(8,128)(2,1)S(1)}, bf16[256,128]{1,0:T(8,128)(2,1)S(1)}, u32[]{:S(2)}, u32[]{:S(2)}) collective-permute-start(bf16[256,128]{1,0:T(8,128)(2,1)S(1)} %fusion.24), channel_id=1, source_target_pairs={{8,0},{16,8},{24,16},{32,24},{40,32},{48,40},{56,48},{64,56},{72,6... | collective-permute-start | bytes 196616 | tf_op jit(solution)/shard_map/ppermute | solution.py:16
  147.1 7.7 %collective-permute-start.15 = (bf16[256,128]{1,0:T(8,128)(2,1)S(1)}, bf16[256,128]{1,0:T(8,128)(2,1)S(1)}, u32[]{:S(2)}, u32[]{:S(2)}) collective-permute-start(bf16[256,128]{1,0:T(8,128)(2,1)S(1)} %fusion.19), channel_id=1, source_target_pairs={{8,0},{16,8},{24,16},{32,24},{40,32},{48,40},{56,48},{64,56},{72,6... | collective-permute-start | bytes 196616 | tf_op jit(solution)/shard_map/ppermute | solution.py:16
  152.7 7.9 %collective-permute-start.11 = (bf16[256,128]{1,0:T(8,128)(2,1)S(1)}, bf16[256,128]{1,0:T(8,128)(2,1)S(1)}, u32[]{:S(2)}, u32[]{:S(2)}) collective-permute-start(bf16[256,128]{1,0:T(8,128)(2,1)S(1)} %fusion.23), channel_id=1, source_target_pairs={{8,0},{16,8},{24,16},{32,24},{40,32},{48,40},{56,48},{64,56},{72,6... | collective-permute-start | bytes 196616 | tf_op jit(solution)/shard_map/ppermute | solution.py:16
  155.4 10.5 %all-to-all-start.7 = ((bf16[8,32,128]{2,1,0:T(8,128)(2,1)}), bf16[8,32,128]{2,1,0:T(8,128)(2,1)S(1)}, u32[]{:S(2)}, u32[]{:S(2)}) async-start(bf16[8,32,128]{2,1,0:T(8,128)(2,1)} %bitcast.22), calls=%async_computation.7 | async-start | bytes 131072 | tf_op jit(solution)/shard_map/all_to_all | solution.py:113
  165.9 10.5 %all-to-all-start.6 = ((bf16[8,32,128]{2,1,0:T(8,128)(2,1)}), bf16[8,32,128]{2,1,0:T(8,128)(2,1)S(1)}, u32[]{:S(2)}, u32[]{:S(2)}) async-start(bf16[8,32,128]{2,1,0:T(8,128)(2,1)} %bitcast.19), calls=%async_computation.6 | async-start | bytes 131072 | tf_op jit(solution)/shard_map/all_to_all | solution.py:110
  176.4 27.5 %all-to-all-start.5 = ((bf16[8,32,1536]{2,1,0:T(8,128)(2,1)}), bf16[8,32,1536]{2,1,0:T(8,128)(2,1)S(1)}, u32[]{:S(2)}, u32[]{:S(2)}) async-start(bf16[8,32,1536]{2,1,0:T(8,128)(2,1)} %all_to_all.123), calls=%async_computation.5 | async-start | bytes 1572864 | tf_op jit(solution)/shard_map/all_to_all | solution.py:103
  203.9 26.1 %all-to-all-start.3 = ((bf16[8,32,1536]{2,1,0:T(8,128)(2,1)}), bf16[8,32,1536]{2,1,0:T(8,128)(2,1)S(1)}, u32[]{:S(2)}, u32[]{:S(2)}) async-start(bf16[8,32,1536]{2,1,0:T(8,128)(2,1)} %all_to_all.117), calls=%async_computation.3 | async-start | bytes 1572864 | tf_op jit(solution)/shard_map/all_to_all | solution.py:96
  (11 other events, 161.0 us)
where the time goes:
time: 232 us; the launch traced here: 231 us
  starting transfers between devices  84.2 us (36%)
  waiting for transfers between devices  70.2 us (30%)
  matrix products  37.4 us (16%)
  local copies, waits for them, and re-layouts  22.3 us (10%)
  other arithmetic  15.8 us (7%)
    ppermute x16, starting transfers between devices, passed_along(): return lax.ppermute(x, axis, pairs)  42.5 us
    all_to_all x1, waiting for transfers between devices, local(): lax.all_to_all(attended.reshape(row_count, head_count * HD), 'hg', split_...  20.4 us
    all_to_all x1, waiting for transfers between devices, local(): lax.all_to_all(query_grad.reshape(row_count, head_count * HD), 'hg', spli...  18.6 us
    ppermute x16, waiting for transfers between devices, passed_along(): return lax.ppermute(x, axis, pairs)  14.5 us
    dot_general x1, matrix products, local(): jnp.einsum('htk,kd->thd', weights, window_values, preferred_element_type=...  10.4 us
    reduce_sum x1, other arithmetic, local(): jnp.sum(jnp.where(visible, jnp.exp(scores - row_max), 0.0), axis=2, keepd...  8.61 us
    all_to_all x1, starting transfers between devices, local(): lax.all_to_all(key_states, 'hg', split_axis=1, concat_axis=0, tiled=True)  8.19 us
    all_to_all x1, waiting for transfers between devices, local(): lax.all_to_all(out_grad, 'hg', split_axis=1, concat_axis=0, tiled=True)  7.41 us
  transfers between devices with their start and end apart: 24, of which 15 were waited for; matrix products, arithmetic and copies ran while one was open for 21% of the time, Pallas kernels for 0%

commit v1 on v0

v1 whole, which is shorter than its diff:
```python
import functools

import jax
import jax.numpy as jnp
from jax import lax
from jax.experimental import pallas as pl
from jax.experimental.pallas import tpu as pltpu
from jax.sharding import PartitionSpec as P

HD = 128
QPK = 12
TB = 32
GROUP = 4
ROWS = QPK * TB
CHUNK = 256
SCALE = HD ** (-0.5)
LOG2E = 1.4426950408889634
NEG = -1e30
GATHER_PHASE = (0, 0)
REDUCE_PHASE = (0, 1)
HW = 2 * QPK * HD
KW = 2 * HD

ANY = pl.BlockSpec(memory_space=pl.ANY)
SMEM = pl.BlockSpec(memory_space=pltpu.SMEM)
VMEM = pl.BlockSpec(memory_space=pltpu.VMEM)
NT = (((1,), (1,)), ((), ()))
NN = (((1,), (0,)), ((), ()))


def bf16(*shape):
    return jax.ShapeDtypeStruct(shape, jnp.bfloat16)


def columns(start, width):
    return pl.ds(pl.multiple_of(start, 128), width)


def run_copies(copies):
    for copy in copies:
        copy.start()
    for copy in copies:
        copy.wait()


def split_kv_body(meta, keys, values, *refs):
    outs, sem = refs[:GROUP], refs[GROUP]
    group_at = meta[0]
    copies = []
    for d in range(GROUP):
        for n, source in enumerate((keys, values)):
            for head in range(2):
                at = (group_at ^ d) * KW + head * HD
                copies.append(
                    pltpu.make_async_copy(
                        source.at[:, columns(at, HD)], outs[d].at[n, head], sem.at[len(copies)]
                    )
                )
    run_copies(copies)


def split_kv(meta, keys, values):
    return pl.pallas_call(
        split_kv_body,
        in_specs=[SMEM, ANY, ANY],
        out_specs=[VMEM] * GROUP,
        out_shape=[bf16(2, 2, TB, HD)] * GROUP,
        scratch_shapes=[pltpu.SemaphoreType.DMA((4 * GROUP,))],
    )(meta, keys, values)


def split_queries_body(meta, queries, grads, *refs):
    outs, sem = refs[: GROUP - 1], refs[GROUP - 1]
    group_at = meta[0]
    copies = []
    for d in range(1, GROUP):
        for n, source in enumerate((queries, grads)):
            copies.append(
                pltpu.make_async_copy(
                    source.at[:, columns((group_at ^ d) * HW, HW)],
                    outs[d - 1].at[n],
                    sem.at[len(copies)],
                )
            )
    run_copies(copies)


def split_queries(meta, queries, grads):
    return pl.pallas_call(
        split_queries_body,
        in_specs=[SMEM, ANY, ANY],
        out_specs=[VMEM] * (GROUP - 1),
        out_shape=[bf16(2, TB, HW)] * (GROUP - 1),
        scratch_shapes=[pltpu.SemaphoreType.DMA((2 * GROUP,))],
    )(meta, queries, grads)


def attention_body(
    meta, doc_starts, doc_tenant, tenant_weight, queries, grads, qg1, qg2, qg3, *refs
):
    gathered, refs = refs[:10], refs[10:]
    partials, refs = refs[:8], refs[8:]
    outs, refs = refs[:4], refs[4:]
    kv, acc, qg, scores, weights_ref, head_q, head_w, attended_t, query_t, sem_kv, sem_q = refs
    group_at, z_at, pair_at = meta[0], meta[1], meta[2]
    n_docs = doc_starts.shape[0]

    side = 1 - 2 * (z_at & 1)

    def offsets(phase):
        s = side if phase == 0 else -side
        return ((0,), (s,), (-s, -2 * s), (2 * s, 3 * s), (-3 * s, -4 * s))

    copies = []
    for chain in range(2):
        base = 4 if chain == 0 else 0
        for part in range(5):
            source = gathered[chain * 5 + part]
            for j, off in enumerate(offsets(GATHER_PHASE[chain])[part]):
                z_from = (z_at + off + 8) & 7
                for d in range(4):
                    copies.append(
                        pltpu.make_async_copy(
                            source.at[j, d], kv.at[base + (group_at ^ d), z_from], sem_kv
                        )
                    )
    q_copies = [
        pltpu.make_async_copy(queries.at[:, columns(group_at * HW, HW)], qg.at[0, 0], sem_q),
        pltpu.make_async_copy(grads.at[:, columns(group_at * HW, HW)], qg.at[0, 1], sem_q),
    ] + [
        pltpu.make_async_copy(source, qg.at[d + 1], sem_q) for d, source in enumerate((qg1, qg2, qg3))
    ]
    for copy in copies + q_copies:
        copy.start()
    acc[...] = jnp.zeros_like(acc)
    rows_at = lax.broadcasted_iota(jnp.int32, (128, 128), 0)
    cols_at = lax.broadcasted_iota(jnp.int32, (128, 128), 1)
    eye = jnp.where(rows_at == cols_at, 1.0, 0.0).astype(jnp.bfloat16)
    for copy in copies + q_copies:
        copy.wait()

    def dot(a, b, dims):
        return lax.dot_general(a, b, dims, preferred_element_type=jnp.float32)

    def flip(x):
        return jnp.concatenate(
            [dot(eye, x[:, i * 128 : (i + 1) * 128], NT) for i in range(x.shape[1] // 128)], axis=0
        )

    window_at = 1024 * (pair_at - 1)
    c_scale = SCALE * LOG2E

    def block(d, carry):
        sub = group_at ^ d
        first = 1024 * pair_at + CHUNK * sub + TB * z_at
        lowest = jnp.int32(0)
        for n in range(n_docs):
            lowest = jnp.where(doc_starts[n] <= first, doc_starts[n], lowest)
        chunk_lo = jnp.maximum((lowest - window_at) >> 8, 0)
        chunk_hi = 4 + sub + 1
        lane = lax.broadcasted_iota(jnp.int32, (1, 128), 1)
        token = first + (lane & (TB - 1))
        start = jnp.zeros((1, 128), jnp.int32)
        scaling = jnp.zeros((1, 128), jnp.float32)
        for n in range(n_docs):
            inside = doc_starts[n] <= token
            start = jnp.where(inside, doc_starts[n], start)
            scaling = jnp.where(inside, tenant_weight[doc_tenant[n]], scaling)
        scaling = jnp.concatenate([scaling] * 3, axis=1)

        for h in range(2):
            for m in range(QPK):
                cols = slice((h * QPK + m) * HD, (h * QPK + m + 1) * HD)
                head_q[h, m * TB : (m + 1) * TB, :] = qg[d, 0, :, cols]
            raw = jnp.concatenate(
                [qg[d, 1, :, (h * QPK + m) * HD : (h * QPK + m + 1) * HD] for m in range(QPK)], axis=0
            )
            raw_t = jnp.concatenate(
                [dot(eye, raw[i * 128 : (i + 1) * 128], NT) for i in range(3)], axis=1
            )
            head_w[h] = (raw_t * scaling).astype(jnp.bfloat16)

        def first_pass(c, tops):
            key_at = window_at + c * CHUNK + lax.broadcasted_iota(jnp.int32, (CHUNK, 128), 0)
            bias = jnp.where((key_at >= start) & (key_at <= token), 0.0, NEG)
            bias = jnp.concatenate([bias] * 3, axis=1)
            new = []
            for h in range(2):
                k = kv[c, :, 0, h].reshape(CHUNK, HD)
                s = dot(k, head_q[h], NT) + bias
                scores[c, h] = s
                new.append(jnp.maximum(tops[h], jnp.max(s.reshape(CHUNK // 8, 8, ROWS), axis=0)))
            return tuple(new)

        top = jnp.full((8, ROWS), NEG, jnp.float32)
        tops = lax.fori_loop(chunk_lo, chunk_hi, first_pass, (top, top))
        tops = [jnp.max(t, axis=0, keepdims=True) for t in tops]

        attended_t[...] = jnp.zeros_like(attended_t)
        query_t[...] = jnp.zeros_like(query_t)

        def second_pass(c, sums):
            new = []
            for h in range(2):
                p = jnp.exp2((scores[c, h] - tops[h]) * c_scale)
                scores[c, h] = p
                new.append(sums[h] + jnp.sum(p.reshape(CHUNK // 8, 8, ROWS), axis=0))
                v = kv[c, :, 1, h].reshape(CHUNK, HD)
                v_t = jnp.concatenate(
                    [dot(eye, v[i * 128 : (i + 1) * 128], NT) for i in range(CHUNK // 128)], axis=1
                ).astype(jnp.bfloat16)
                attended_t[h] += dot(v_t, p.astype(jnp.bfloat16), NN)
            return tuple(new)

        zero = jnp.zeros((8, ROWS), jnp.float32)
        sums = lax.fori_loop(chunk_lo, chunk_hi, second_pass, (zero, zero))
        inverse = [1.0 / jnp.sum(s, axis=0, keepdims=True) for s in sums]
        deltas = []
        for h in range(2):
            rounded = (attended_t[h] * inverse[h]).astype(jnp.bfloat16)
            deltas.append(
                jnp.sum(
                    rounded.astype(jnp.float32) * head_w[h].astype(jnp.float32), axis=0, keepdims=True
                )
            )
            out = flip(rounded).astype(jnp.bfloat16)
            for m in range(QPK):
                cols = slice((h * QPK + m) * HD, (h * QPK + m + 1) * HD)
                weights_ref[d, 0, :, cols] = out[m * TB : (m + 1) * TB]

        def third_pass(c, carry):
            for h in range(2):
                k = kv[c, :, 0, h].reshape(CHUNK, HD)
                v = kv[c, :, 1, h].reshape(CHUNK, HD)
                p = scores[c, h] * inverse[h]
                push = dot(v, head_w[h], NN)
                ds = (p * (push - deltas[h])).astype(jnp.bfloat16)
                acc[c, :, 1, h] += dot(p.astype(jnp.bfloat16), head_w[h], NT).reshape(8, TB, HD)
                acc[c, :, 0, h] += dot(ds, head_q[h], NN).reshape(8, TB, HD)
                k_t = jnp.concatenate(
                    [dot(eye, k[i * 128 : (i + 1) * 128], NT) for i in range(CHUNK // 128)], axis=1
                ).astype(jnp.bfloat16)
                query_t[h] += dot(k_t, ds, NN)
            return carry

        lax.fori_loop(chunk_lo, chunk_hi, third_pass, 0)
        for h in range(2):
            out = flip((query_t[h] * SCALE).astype(jnp.bfloat16)).astype(jnp.bfloat16)
            for m in range(QPK):
                cols = slice((h * QPK + m) * HD, (h * QPK + m + 1) * HD)
                weights_ref[d, 1, :, cols] = out[m * TB : (m + 1) * TB]
        return carry

    lax.fori_loop(0, 4, block, 0)

    out_copies = [pltpu.make_async_copy(weights_ref.at[d], outs[d], sem_q) for d in range(4)]
    for copy in out_copies:
        copy.start()
    for chain in range(2):
        base = 4 if chain == 0 else 0
        for part in range(4):
            offs = offsets(REDUCE_PHASE[chain])
            offs = offs[part + 1] if part else offs[0] + offs[1]
            target = partials[chain * 4 + part]
            for j, off in enumerate(offs):
                z_to = (z_at + off + 8) & 7
                for d in range(4):
                    part_sum = acc[base + (group_at ^ d), z_to]
                    target[j, d, 0] = (part_sum[0] * SCALE).astype(jnp.bfloat16)
                    target[j, d, 1] = part_sum[1].astype(jnp.bfloat16)
    for copy in out_copies:
        copy.wait()


def attention(meta, doc_starts, doc_tenant, tenant_weight, queries, grads, received, gathered):
    part = bf16(2, 4, 2, 2, TB, HD)
    return pl.pallas_call(
        attention_body,
        in_specs=[SMEM] * 4 + [ANY] * 2 + [VMEM] * 13,
        out_specs=[VMEM] * 12,
        out_shape=[part] * 8 + [bf16(2, TB, HW)] * 4,
        scratch_shapes=[
            pltpu.VMEM((8, 8, 2, 2, TB, HD), jnp.bfloat16),
            pltpu.VMEM((8, 8, 2, 2, TB, HD), jnp.float32),
            pltpu.VMEM((4, 2, TB, HW), jnp.bfloat16),
            pltpu.VMEM((8, 2, CHUNK, ROWS), jnp.float32),
            pltpu.VMEM((4, 2, TB, HW), jnp.bfloat16),
            pltpu.VMEM((2, ROWS, HD), jnp.bfloat16),
            pltpu.VMEM((2, HD, ROWS), jnp.bfloat16),
            pltpu.VMEM((2, HD, ROWS), jnp.float32),
            pltpu.VMEM((2, HD, ROWS), jnp.float32),
            pltpu.SemaphoreType.DMA,
            pltpu.SemaphoreType.DMA,
        ],
        compiler_params=pltpu.CompilerParams(vmem_limit_bytes=40 * 1024 * 1024),
        cost_estimate=pl.CostEstimate(flops=3 * 10**9, bytes_accessed=10**7, transcendentals=10**6),
    )(meta, doc_starts, doc_tenant, tenant_weight, queries, grads, *received, *gathered)


def join_body(meta, *refs):
    ins, refs = refs[:8], refs[8:]
    attended, query_grad, key_grad, value_grad, sem = refs
    group_at = meta[0]
    copies = []
    for d in range(GROUP):
        for n, target in enumerate((attended, query_grad)):
            copies.append(
                pltpu.make_async_copy(
                    ins[d].at[n], target.at[:, columns((group_at ^ d) * HW, HW)], sem.at[len(copies)]
                )
            )
        for n, target in enumerate((key_grad, value_grad)):
            for head in range(2):
                at = (group_at ^ d) * KW + head * HD
                copies.append(
                    pltpu.make_async_copy(
                        ins[4 + d].at[n, head], target.at[:, columns(at, HD)], sem.at[len(copies)]
                    )
                )
    run_copies(copies)


def join(meta, wide, narrow):
    return pl.pallas_call(
        join_body,
        in_specs=[SMEM] + [VMEM] * 8,
        out_specs=[ANY] * 4,
        out_shape=[bf16(TB, 96 * HD)] * 2 + [bf16(TB, 8 * HD)] * 2,
        scratch_shapes=[pltpu.SemaphoreType.DMA((6 * GROUP,))],
    )(meta, *wide, *narrow)


def swap_in_group(x, d):
    return lax.ppermute(x, "ctx", [(i, i ^ d) for i in range(lax.axis_size("ctx"))])


def swap_on_z(x, phase):
    if phase == 0:
        pairs = [(i, i ^ 1) for i in range(8)]
    else:
        pairs = [(i, (i - 1) % 8 if i % 2 == 0 else (i + 1) % 8) for i in range(8)]
    return lax.ppermute(x, "hg", pairs)


def gather_on_z(x, phase, beside=None):
    own = x[None]
    first = swap_on_z(own, phase)
    second = swap_on_z(jnp.concatenate([own, first]), 1 - phase)
    third = swap_on_z(second, phase)
    if beside is not None:
        third, beside = lax.optimization_barrier((third, beside))
    fourth = swap_on_z(third, 1 - phase)
    return [own, first, second, third, fourth], beside


def add(a, b):
    return a.astype(jnp.float32) + b.astype(jnp.float32)


def reduce_on_z(parts, phase, beside=None):
    moved = swap_on_z(parts[3], 1 - phase)
    moved = swap_on_z(add(parts[2], moved).astype(jnp.bfloat16), phase)
    moved = add(parts[1], moved).astype(jnp.bfloat16)
    if beside is not None:
        moved, beside = lax.optimization_barrier((moved, beside))
    moved = swap_on_z(moved, 1 - phase)
    last = add(parts[0], moved)
    total = last[0] + swap_on_z(last[1:].astype(jnp.bfloat16), phase)[0].astype(jnp.float32)
    return total, beside


def shift_pairs(x, by):
    devices = lax.axis_size("ctx")
    pairs = [(i, i + by) for i in range(devices) if 0 <= i + by < devices]
    return lax.ppermute(x, "ctx", pairs)


def local(query_states, key_states, value_states, out_grad, doc_starts, doc_tenant, tenant_weight):
    ctx_at = lax.axis_index("ctx")
    z_at = lax.axis_index("hg")
    meta = jnp.stack([ctx_at & 3, z_at, ctx_at >> 2]).astype(jnp.int32)

    kv = split_kv(meta, key_states, value_states)
    own = jnp.stack([kv[0]] + [swap_in_group(kv[d], d) for d in range(1, GROUP)])
    sent = split_queries(meta, query_states, out_grad)
    own, sent = lax.optimization_barrier((own, sent))
    received = [swap_in_group(x, d + 1) for d, x in enumerate(sent)]
    own_all, received = gather_on_z(own, GATHER_PHASE[0], received)
    earlier_all, _ = gather_on_z(shift_pairs(own, GROUP), GATHER_PHASE[1])

    results = attention(
        meta,
        doc_starts,
        doc_tenant,
        tenant_weight,
        query_states,
        out_grad,
        received,
        own_all + earlier_all,
    )
    own_parts, earlier_parts, wide = results[:4], results[4:8], results[8:]

    moved = [swap_in_group(wide[d], d) for d in range(1, GROUP)]
    own_sum, moved = reduce_on_z(own_parts, REDUCE_PHASE[0], moved)
    earlier_sum, _ = reduce_on_z(earlier_parts, REDUCE_PHASE[1])
    earlier_sum = shift_pairs(earlier_sum.astype(jnp.bfloat16), -GROUP)
    total = (own_sum + earlier_sum.astype(jnp.float32)).astype(jnp.bfloat16)
    narrow = [total[0]] + [swap_in_group(total[d], d) for d in range(1, GROUP)]
    return tuple(join(meta, [wide[0]] + moved, narrow))


def solution(mesh):
    row = P(("ctx", "hg"), None)
    return jax.shard_map(
        local,
        mesh=mesh,
        in_specs=(row, row, row, row, P(), P(), P()),
        out_specs=(row, row, row, row),
        check_vma=False,
    )
```

time: 232 us -> 156 us (0.67)
  starting transfers between devices: 84.2 us -> 37.5 us
  Pallas kernels: 0 us -> 40.6 us
  matrix products: 37.4 us -> 0 us
  local copies, waits for them, and re-layouts: 22.3 us -> 1.32 us
  other arithmetic: 15.8 us -> 1.27 us
  waiting for transfers between devices: 70.2 us -> 74.1 us
    ppermute x16 -> x30, waiting for transfers between devices: 14.5 us -> 74.1 us  [the longest x16 33.3 us: swap_on_z(): return lax.ppermute(x, 'hg', pairs)]
    all_to_all x8 -> x0, waiting for transfers between devices: 55.6 us -> none  [the longest x1 20.4 us: local(): lax.all_to_all(attended.reshape(row_count, head_count * HD), 'hg', split_...]
    all_to_all x8 -> x0, starting transfers between devices: 41.6 us -> none  [the longest x1 8.19 us: local(): lax.all_to_all(key_states, 'hg', split_axis=1, concat_axis=0, tiled=True)]
    pallas_call x0 -> x4, Pallas kernels: none -> 40.6 us  [the longest x1 32.3 us: attention(): pl.pallas_call(attention_body, in_specs=[SMEM] * 4 + [ANY] * 2 + [VMEM] *...]
    dot_general x6 -> x0, matrix products: 37.4 us -> none  [the longest x1 10.4 us: local(): jnp.einsum('htk,kd->thd', weights, window_values, preferred_element_type=...]
    all_to_all x11 -> x0, local copies, waits for them, and re-layouts: 12.4 us -> none  [the longest x2 2.36 us: local(): lax.all_to_all(query_grad.reshape(row_count, head_count * HD), 'hg', spli...]
    reduce_sum x5 -> x0, other arithmetic: 12.1 us -> none  [the longest x1 8.61 us: local(): jnp.sum(jnp.where(visible, jnp.exp(scores - row_max), 0.0), axis=2, keepd...]
    convert_element_type x4 -> x0, local copies, waits for them, and re-layouts: 7.67 us -> none  [the longest x2 5.6 us: local(): grad_rows.astype(jnp.float32)]
  transfers between devices with their start and end apart: 24 -> 30, of which waited for: 15 -> 17; matrix products, arithmetic and copies ran while one was open for 21% -> 0% of each run, Pallas kernels for 0% -> 2%
where the time goes in v1:
time: 156 us
  waiting for transfers between devices  74.1 us (47%)
  Pallas kernels  40.6 us (26%)
  starting transfers between devices  37.5 us (24%)
    ppermute x16, waiting for transfers between devices, swap_on_z(): return lax.ppermute(x, 'hg', pairs)  33.3 us
    pallas_call x1, Pallas kernels, attention(): pl.pallas_call(attention_body, in_specs=[SMEM] * 4 + [ANY] * 2 + [VMEM] *...  32.3 us
    ppermute x12, waiting for transfers between devices, swap_in_group(): lax.ppermute(x, 'ctx', [(i, i ^ d) for i in range(lax.axis_size('ctx'))])  31.9 us
    ppermute x16, starting transfers between devices, swap_on_z(): return lax.ppermute(x, 'hg', pairs)  17.6 us
    ppermute x12, starting transfers between devices, swap_in_group(): lax.ppermute(x, 'ctx', [(i, i ^ d) for i in range(lax.axis_size('ctx'))])  14.1 us
    ppermute x2, waiting for transfers between devices, shift_pairs(): return lax.ppermute(x, 'ctx', pairs)  9 us
    ppermute x2, starting transfers between devices, shift_pairs(): return lax.ppermute(x, 'ctx', pairs)  5.84 us
    pallas_call x1, Pallas kernels, split_queries(): pl.pallas_call(split_queries_body, in_specs=[SMEM, ANY, ANY], out_specs=[...  3.2 us
  transfers between devices with their start and end apart: 30, of which 17 were waited for; matrix products, arithmetic and copies ran while one was open for 0% of the time, Pallas kernels for 2%

profile of v1, /device:TPU:25, one launch (start us, length us, event | category | flops | bytes accessed | tf_op | source)
XLA Modules:
  0.0 155.9 jit_solution(9534176145909221372)
XLA Ops:
  1.3 2.3 %shard_map.102 = (bf16[2,2,32,128]{3,2,1,0:T(8,128)(2,1)}, bf16[2,2,32,128]{3,2,1,0:T(8,128)(2,1)}, bf16[2,2,32,128]{3,2,1,0:T(8,128)(2,1)}, bf16[2,2,32,128]{3,2,1,0:T(8,128)(2,1)}) custom-call(s32[3]{0:T(128)} %pad_add_fusion.meta, bf16[32,1024]{1,0:T(8,128)(2,1)} %keys.1, bf16[32,1024]{1,0:T(8,128)(2,1)} %values.1), custom_call_target="tpu_custom_call" | custom-call | tf_op jit(solution)/shard_map/pallas_call | solution.py:63
  6.1 3.2 %shard_map.103 = (bf16[2,32,3072]{2,1,0:T(8,128)(2,1)}, bf16[2,32,3072]{2,1,0:T(8,128)(2,1)}, bf16[2,32,3072]{2,1,0:T(8,128)(2,1)}) custom-call(s32[3]{0:T(128)} %pad_add_fusion.meta, bf16[32,12288]{1,0:T(8,128)(2,1)} %queries.3, bf16[32,12288]{1,0:T(8,128)(2,1)} %grads.3), custom_call_target="tpu_custom_call" | custom-call | tf_op jit(solution)/shard_map/pallas_call | solution.py:89
  9.4 3.9 %collective-permute-start.10 = (bf16[4,2,2,32,128]{4,3,2,1,0:T(8,128)(2,1)S(1)}, bf16[4,2,2,32,128]{4,3,2,1,0:T(8,128)(2,1)S(1)}, u32[]{:S(2)}, u32[]{:S(2)}) collective-permute-start(bf16[4,2,2,32,128]{4,3,2,1,0:T(8,128)(2,1)S(1)} %pad_maximum_fusion.2), channel_id=1, source_target_pairs={{0,32},{8,40},{16,48},{24,56},{32,64},{40,72},{48,80},{56,88},{64,... | collective-permute-start | bytes 393224 | tf_op jit(solution)/shard_map/ppermute | solution.py:375
  15.1 2.8 %collective-permute-done.10 = bf16[4,2,2,32,128]{4,3,2,1,0:T(8,128)(2,1)S(1)} collective-permute-done((bf16[4,2,2,32,128]{4,3,2,1,0:T(8,128)(2,1)S(1)}, bf16[4,2,2,32,128]{4,3,2,1,0:T(8,128)(2,1)S(1)}, u32[]{:S(2)}, u32[]{:S(2)}) %collective-permute-start.10) | collective-permute-done | bytes 131104 | tf_op jit(solution)/shard_map/ppermute | solution.py:375
  19.6 4.8 %collective-permute-start.4 = (bf16[2,4,2,2,32,128]{5,4,3,2,1,0:T(8,128)(2,1)S(1)}, bf16[2,4,2,2,32,128]{5,4,3,2,1,0:T(8,128)(2,1)S(1)}, u32[]{:S(2)}, u32[]{:S(2)}) collective-permute-start(bf16[2,4,2,2,32,128]{5,4,3,2,1,0:T(8,128)(2,1)S(1)} %pad_maximum_fusion), channel_id=1, source_target_pairs={{0,7},{1,2},{2,1},{3,4},{4,3},{5,6},{6,5},{7,0},{8,15},{9,10},{10,... | collective-permute-start | bytes 786440 | tf_op jit(solution)/shard_map/ppermute | solution.py:342
  24.4 3.0 %collective-permute-start.12 = (bf16[2,4,2,2,32,128]{5,4,3,2,1,0:T(8,128)(2,1)S(1)}, bf16[2,4,2,2,32,128]{5,4,3,2,1,0:T(8,128)(2,1)S(1)}, u32[]{:S(2)}, u32[]{:S(2)}) collective-permute-start(bf16[2,4,2,2,32,128]{5,4,3,2,1,0:T(8,128)(2,1)S(1)} %pad_maximum_fusion.1), channel_id=1, source_target_pairs={{0,7},{1,2},{2,1},{3,4},{4,3},{5,6},{6,5},{7,0},{8,15},{9,10},{10,... | collective-permute-start | bytes 786440 | tf_op jit(solution)/shard_map/ppermute | solution.py:342
  27.4 2.4 %collective-permute-start.6 = (bf16[2,32,3072]{2,1,0:T(8,128)(2,1)}, bf16[2,32,3072]{2,1,0:T(8,128)(2,1)S(1)}, u32[]{:S(2)}, u32[]{:S(2)}) collective-permute-start(bf16[2,32,3072]{2,1,0:T(8,128)(2,1)} %get-tuple-element.43), channel_id=1, source_target_pairs={{0,8},{8,0},{16,24},{24,16},{32,40},{40,32},{48,56},{56,48},{64,72... | collective-permute-start | bytes 1179656 | tf_op jit(solution)/shard_map/ppermute | solution.py:334
  31.4 3.9 %collective-permute-done.12.refs_7_ = bf16[2,4,2,2,32,128]{5,4,3,2,1,0:T(8,128)(2,1)S(1)} collective-permute-done((bf16[2,4,2,2,32,128]{5,4,3,2,1,0:T(8,128)(2,1)S(1)}, bf16[2,4,2,2,32,128]{5,4,3,2,1,0:T(8,128)(2,1)S(1)}, u32[]{:S(2)}, u32[]{:S(2)}) %collective-permute-start.12) | collective-permute-done | bytes 262176 | tf_op jit(solution)/shard_map/ppermute | solution.py:342
  35.4 5.4 %collective-permute-done.7.qg2 = bf16[2,32,3072]{2,1,0:T(8,128)(2,1)S(1)} collective-permute-done((bf16[2,32,3072]{2,1,0:T(8,128)(2,1)}, bf16[2,32,3072]{2,1,0:T(8,128)(2,1)S(1)}, u32[]{:S(2)}, u32[]{:S(2)}) %collective-permute-start.7) | collective-permute-done | bytes 393248 | tf_op jit(solution)/shard_map/ppermute | solution.py:334
  40.8 8.5 %collective-permute-done.8.qg3 = bf16[2,32,3072]{2,1,0:T(8,128)(2,1)S(1)} collective-permute-done((bf16[2,32,3072]{2,1,0:T(8,128)(2,1)S(1)}, bf16[2,32,3072]{2,1,0:T(8,128)(2,1)S(1)}, u32[]{:S(2)}, u32[]{:S(2)}) %collective-permute-start.8) | collective-permute-done | bytes 393248 | tf_op jit(solution)/shard_map/ppermute | solution.py:334
  49.3 2.7 %collective-permute-start.14 = (bf16[2,4,2,2,32,128]{5,4,3,2,1,0:T(8,128)(2,1)S(1)}, bf16[2,4,2,2,32,128]{5,4,3,2,1,0:T(8,128)(2,1)S(1)}, u32[]{:S(2)}, u32[]{:S(2)}) collective-permute-start(bf16[2,4,2,2,32,128]{5,4,3,2,1,0:T(8,128)(2,1)S(1)} %collective-permute-done.13.refs_8_), channel_id=1, source_target_pairs={{0,7},{1,2},{2,1},{3,4},{4,3},{5,6},{6,5},{7,0},{8,15},{9,10},{10,... | collective-permute-start | bytes 786440 | tf_op jit(solution)/shard_map/ppermute | solution.py:342
  52.0 6.1 %collective-permute-done.9.refs_4_ = bf16[2,4,2,2,32,128]{5,4,3,2,1,0:T(8,128)(2,1)S(1)} collective-permute-done((bf16[2,4,2,2,32,128]{5,4,3,2,1,0:T(8,128)(2,1)S(1)}, bf16[2,4,2,2,32,128]{5,4,3,2,1,0:T(8,128)(2,1)S(1)}, u32[]{:S(2)}, u32[]{:S(2)}) %collective-permute-start.9) | collective-permute-done | bytes 262176 | tf_op jit(solution)/shard_map/ppermute | solution.py:342
  58.1 5.6 %collective-permute-done.14.refs_9_ = bf16[2,4,2,2,32,128]{5,4,3,2,1,0:T(8,128)(2,1)S(1)} collective-permute-done((bf16[2,4,2,2,32,128]{5,4,3,2,1,0:T(8,128)(2,1)S(1)}, bf16[2,4,2,2,32,128]{5,4,3,2,1,0:T(8,128)(2,1)S(1)}, u32[]{:S(2)}, u32[]{:S(2)}) %collective-permute-start.14) | collective-permute-done | bytes 262176 | tf_op jit(solution)/shard_map/ppermute | solution.py:342
  63.8 32.3 %shard_map.104 = (bf16[2,4,2,2,32,128]{5,4,3,2,1,0:T(8,128)(2,1)S(1)}, bf16[2,4,2,2,32,128]{5,4,3,2,1,0:T(8,128)(2,1)S(1)}, bf16[2,4,2,2,32,128]{5,4,3,2,1,0:T(8...) custom-call(s32[3]{0:T(128)S(1)} %copy-done.3, ...), custom_call_target="tpu_custom_call" | custom-call | flops 3000000000 | bytes 10000000 | tf_op jit(solution)/shard_map/pallas_call | solution.py:277
  96.4 6.4 %collective-permute-done.22 = bf16[2,4,2,2,32,128]{5,4,3,2,1,0:T(8,128)(2,1)S(1)} collective-permute-done((bf16[2,4,2,2,32,128]{5,4,3,2,1,0:T(8,128)(2,1)S(1)}, bf16[2,4,2,2,32,128]{5,4,3,2,1,0:T(8,128)(2,1)S(1)}, u32[]{:S(2)}, u32[]{:S(2)}) %collective-permute-start.22) | collective-permute-done | bytes 262176 | tf_op jit(solution)/shard_map/ppermute | solution.py:342
  104.5 2.3 %collective-permute-start.17 = (bf16[2,32,3072]{2,1,0:T(8,128)(2,1)S(1)}, bf16[2,32,3072]{2,1,0:T(8,128)(2,1)S(1)}, u32[]{:S(2)}, u32[]{:S(2)}) collective-permute-start(bf16[2,32,3072]{2,1,0:T(8,128)(2,1)S(1)} %get-tuple-element.54), channel_id=1, source_target_pairs={{0,8},{8,0},{16,24},{24,16},{32,40},{40,32},{48,56},{56,48},{64,72... | collective-permute-start | bytes 1179656 | tf_op jit(solution)/shard_map/ppermute | solution.py:334
  110.3 7.2 %collective-permute-done.18.refs_2_ = bf16[2,32,3072]{2,1,0:T(8,128)(2,1)S(1)} collective-permute-done((bf16[2,32,3072]{2,1,0:T(8,128)(2,1)S(1)}, bf16[2,32,3072]{2,1,0:T(8,128)(2,1)S(1)}, u32[]{:S(2)}, u32[]{:S(2)}) %collective-permute-start.18) | collective-permute-done | bytes 393248 | tf_op jit(solution)/shard_map/ppermute | solution.py:334
  117.5 8.5 %collective-permute-done.19.refs_3_ = bf16[2,32,3072]{2,1,0:T(8,128)(2,1)S(1)} collective-permute-done((bf16[2,32,3072]{2,1,0:T(8,128)(2,1)S(1)}, bf16[2,32,3072]{2,1,0:T(8,128)(2,1)S(1)}, u32[]{:S(2)}, u32[]{:S(2)}) %collective-permute-start.19) | collective-permute-done | bytes 393248 | tf_op jit(solution)/shard_map/ppermute | solution.py:334
  128.9 5.9 %collective-permute-done.20 = bf16[2,4,2,2,32,128]{5,4,3,2,1,0:T(8,128)(2,1)S(1)} collective-permute-done((bf16[2,4,2,2,32,128]{5,4,3,2,1,0:T(8,128)(2,1)S(1)}, bf16[2,4,2,2,32,128]{5,4,3,2,1,0:T(8,128)(2,1)S(1)}, u32[]{:S(2)}, u32[]{:S(2)}) %collective-permute-start.20) | collective-permute-done | bytes 262176 | tf_op jit(solution)/shard_map/ppermute | solution.py:342
  135.3 2.3 %collective-permute-done.25 = bf16[1,4,2,2,32,128]{5,4,3,2,1,0:T(8,128)(2,1)S(1)} collective-permute-done((bf16[1,4,2,2,32,128]{5,4,3,2,1,0:T(8,128)(2,1)S(1)}, bf16[1,4,2,2,32,128]{5,4,3,2,1,0:T(8,128)(2,1)S(1)}, u32[]{:S(2)}, u32[]{:S(2)}) %collective-permute-start.25) | collective-permute-done | bytes 131104 | tf_op jit(solution)/shard_map/ppermute | solution.py:342
  137.7 1.9 %collective-permute-start.26 = (bf16[4,2,2,32,128]{4,3,2,1,0:T(8,128)(2,1)S(1)}, bf16[4,2,2,32,128]{4,3,2,1,0:T(8,128)(2,1)S(1)}, u32[]{:S(2)}, u32[]{:S(2)}) collective-permute-start(bf16[4,2,2,32,128]{4,3,2,1,0:T(8,128)(2,1)S(1)} %fusion.4), channel_id=1, source_target_pairs={{32,0},{40,8},{48,16},{56,24},{64,32},{72,40},{80,48},{88,56},{96,... | collective-permute-start | bytes 393224 | tf_op jit(solution)/shard_map/ppermute | solution.py:375
  139.6 6.2 %collective-permute-done.26 = bf16[4,2,2,32,128]{4,3,2,1,0:T(8,128)(2,1)S(1)} collective-permute-done((bf16[4,2,2,32,128]{4,3,2,1,0:T(8,128)(2,1)S(1)}, bf16[4,2,2,32,128]{4,3,2,1,0:T(8,128)(2,1)S(1)}, u32[]{:S(2)}, u32[]{:S(2)}) %collective-permute-start.26) | collective-permute-done | bytes 131104 | tf_op jit(solution)/shard_map/ppermute | solution.py:375
  146.5 2.6 %collective-permute-start.29 = (bf16[2,2,32,128]{3,2,1,0:T(8,128)(2,1)S(1)}, bf16[2,2,32,128]{3,2,1,0:T(8,128)(2,1)S(1)}, u32[]{:S(2)}, u32[]{:S(2)}) collective-permute-start(bf16[2,2,32,128]{3,2,1,0:T(8,128)(2,1)S(1)} %get-tuple-element.66), channel_id=1, source_target_pairs={{0,24},{8,16},{16,8},{24,0},{32,56},{40,48},{48,40},{56,32},{64,88... | collective-permute-start | bytes 98312 | tf_op jit(solution)/shard_map/ppermute | solution.py:334
  153.0 2.8 %shard_map.105 = (bf16[32,12288]{1,0:T(8,128)(2,1)}, bf16[32,12288]{1,0:T(8,128)(2,1)}, bf16[32,1024]{1,0:T(8,128)(2,1)}, bf16[32,1024]{1,0:T(8,128)(2,1)}) custom-call(s32[3]{0:T(128)} %pad_add_fusion.meta, bf16[2,32,3072]{2,1,0:T(8,128)(2,1)} %copy-done.2, bf16[2,32,3072]{2,1,0:T(8,128)(2,1)} %copy-done.7, bf16[2,32,3072]{2,1,0:T(8,128)(2,1)} %copy-done.8, ...), custom_call_target="tpu_custom_call" | custom-call | tf_op jit(solution)/shard_map/pallas_call | solution.py:324
  (85 shorter events, 21.7 us)
Async XLA Ops:
  3.6 5.7 %collective-permute-start = (bf16[2,2,32,128]{3,2,1,0:T(8,128)(2,1)}, bf16[2,2,32,128]{3,2,1,0:T(8,128)(2,1)S(1)}, u32[]{:S(2)}, u32[]{:S(2)}) collective-permute-start(bf16[2,2,32,128]{3,2,1,0:T(8,128)(2,1)} %get-tuple-element.36), channel_id=1, source_target_pairs={{0,8},{8,0},{16,24},{24,16},{32,40},{40,32},{48,56},{56,48},{64,72... | collective-permute-start | bytes 98312 | tf_op jit(solution)/shard_map/ppermute | solution.py:334
  9.4 8.5 %collective-permute-start.10 = (bf16[4,2,2,32,128]{4,3,2,1,0:T(8,128)(2,1)S(1)}, bf16[4,2,2,32,128]{4,3,2,1,0:T(8,128)(2,1)S(1)}, u32[]{:S(2)}, u32[]{:S(2)}) collective-permute-start(bf16[4,2,2,32,128]{4,3,2,1,0:T(8,128)(2,1)S(1)} %pad_maximum_fusion.2), channel_id=1, source_target_pairs={{0,32},{8,40},{16,48},{24,56},{32,64},{40,72},{48,80},{56,88},{64,... | collective-permute-start | bytes 393224 | tf_op jit(solution)/shard_map/ppermute | solution.py:375
  13.3 6.2 %collective-permute-start.3 = (bf16[1,4,2,2,32,128]{5,4,3,2,1,0:T(8,128)(2,1)S(1)}, bf16[1,4,2,2,32,128]{5,4,3,2,1,0:T(8,128)(2,1)S(1)}, u32[]{:S(2)}, u32[]{:S(2)}) collective-permute-start(bf16[1,4,2,2,32,128]{5,4,3,2,1,0:T(8,128)(2,1)S(1)} %bitcast.25), channel_id=1, source_target_pairs={{0,1},{1,0},{2,3},{3,2},{4,5},{5,4},{6,7},{7,6},{8,9},{9,8},{10,11... | collective-permute-start | bytes 393224 | tf_op jit(solution)/shard_map/ppermute | solution.py:342
  17.9 6.5 %collective-permute-start.11 = (bf16[1,4,2,2,32,128]{5,4,3,2,1,0:T(8,128)(2,1)S(1)}, bf16[1,4,2,2,32,128]{5,4,3,2,1,0:T(8,128)(2,1)S(1)}, u32[]{:S(2)}, u32[]{:S(2)}) collective-permute-start(bf16[1,4,2,2,32,128]{5,4,3,2,1,0:T(8,128)(2,1)S(1)} %bitcast.28), channel_id=1, source_target_pairs={{0,1},{1,0},{2,3},{3,2},{4,5},{5,4},{6,7},{7,6},{8,9},{9,8},{10,11... | collective-permute-start | bytes 393224 | tf_op jit(solution)/shard_map/ppermute | solution.py:342
  19.6 11.8 %collective-permute-start.4 = (bf16[2,4,2,2,32,128]{5,4,3,2,1,0:T(8,128)(2,1)S(1)}, bf16[2,4,2,2,32,128]{5,4,3,2,1,0:T(8,128)(2,1)S(1)}, u32[]{:S(2)}, u32[]{:S(2)}) collective-permute-start(bf16[2,4,2,2,32,128]{5,4,3,2,1,0:T(8,128)(2,1)S(1)} %pad_maximum_fusion), channel_id=1, source_target_pairs={{0,7},{1,2},{2,1},{3,4},{4,3},{5,6},{6,5},{7,0},{8,15},{9,10},{10,... | collective-permute-start | bytes 786440 | tf_op jit(solution)/shard_map/ppermute | solution.py:342
  24.4 11.0 %collective-permute-start.12 = (bf16[2,4,2,2,32,128]{5,4,3,2,1,0:T(8,128)(2,1)S(1)}, bf16[2,4,2,2,32,128]{5,4,3,2,1,0:T(8,128)(2,1)S(1)}, u32[]{:S(2)}, u32[]{:S(2)}) collective-permute-start(bf16[2,4,2,2,32,128]{5,4,3,2,1,0:T(8,128)(2,1)S(1)} %pad_maximum_fusion.1), channel_id=1, source_target_pairs={{0,7},{1,2},{2,1},{3,4},{4,3},{5,6},{6,5},{7,0},{8,15},{9,10},{10,... | collective-permute-start | bytes 786440 | tf_op jit(solution)/shard_map/ppermute | solution.py:342
  27.4 8.0 %collective-permute-start.6 = (bf16[2,32,3072]{2,1,0:T(8,128)(2,1)}, bf16[2,32,3072]{2,1,0:T(8,128)(2,1)S(1)}, u32[]{:S(2)}, u32[]{:S(2)}) collective-permute-start(bf16[2,32,3072]{2,1,0:T(8,128)(2,1)} %get-tuple-element.43), channel_id=1, source_target_pairs={{0,8},{8,0},{16,24},{24,16},{32,40},{40,32},{48,56},{56,48},{64,72... | collective-permute-start | bytes 1179656 | tf_op jit(solution)/shard_map/ppermute | solution.py:334
  29.8 11.0 %collective-permute-start.7 = (bf16[2,32,3072]{2,1,0:T(8,128)(2,1)}, bf16[2,32,3072]{2,1,0:T(8,128)(2,1)S(1)}, u32[]{:S(2)}, u32[]{:S(2)}) collective-permute-start(bf16[2,32,3072]{2,1,0:T(8,128)(2,1)} %get-tuple-element.44), channel_id=1, source_target_pairs={{0,16},{8,24},{16,0},{24,8},{32,48},{40,56},{48,32},{56,40},{64,80... | collective-permute-start | bytes 1179656 | tf_op jit(solution)/shard_map/ppermute | solution.py:334
  30.3 19.0 %collective-permute-start.8 = (bf16[2,32,3072]{2,1,0:T(8,128)(2,1)S(1)}, bf16[2,32,3072]{2,1,0:T(8,128)(2,1)S(1)}, u32[]{:S(2)}, u32[]{:S(2)}) collective-permute-start(bf16[2,32,3072]{2,1,0:T(8,128)(2,1)S(1)} %copy-done.14), channel_id=1, source_target_pairs={{0,24},{8,16},{16,8},{24,0},{32,56},{40,48},{48,40},{56,32},{64,88... | collective-permute-start | bytes 1179656 | tf_op jit(solution)/shard_map/ppermute | solution.py:334
  31.4 17.8 %collective-permute-start.5 = (bf16[2,4,2,2,32,128]{5,4,3,2,1,0:T(8,128)(2,1)S(1)}, bf16[2,4,2,2,32,128]{5,4,3,2,1,0:T(8,128)(2,1)S(1)}, u32[]{:S(2)}, u32[]{:S(2)}) collective-permute-start(bf16[2,4,2,2,32,128]{5,4,3,2,1,0:T(8,128)(2,1)S(1)} %collective-permute-done.4.refs_2_), channel_id=1, source_target_pairs={{0,1},{1,0},{2,3},{3,2},{4,5},{5,4},{6,7},{7,6},{8,9},{9,8},{10,11... | collective-permute-start | bytes 786440 | tf_op jit(solution)/shard_map/ppermute | solution.py:342
  35.4 13.9 %collective-permute-start.13 = (bf16[2,4,2,2,32,128]{5,4,3,2,1,0:T(8,128)(2,1)S(1)}, bf16[2,4,2,2,32,128]{5,4,3,2,1,0:T(8,128)(2,1)S(1)}, u32[]{:S(2)}, u32[]{:S(2)}) collective-permute-start(bf16[2,4,2,2,32,128]{5,4,3,2,1,0:T(8,128)(2,1)S(1)} %collective-permute-done.12.refs_7_), channel_id=1, source_target_pairs={{0,1},{1,0},{2,3},{3,2},{4,5},{5,4},{6,7},{7,6},{8,9},{9,8},{10,11... | collective-permute-start | bytes 786440 | tf_op jit(solution)/shard_map/ppermute | solution.py:342
  49.3 8.8 %collective-permute-start.9 = (bf16[2,4,2,2,32,128]{5,4,3,2,1,0:T(8,128)(2,1)S(1)}, bf16[2,4,2,2,32,128]{5,4,3,2,1,0:T(8,128)(2,1)S(1)}, u32[]{:S(2)}, u32[]{:S(2)}) collective-permute-start(bf16[2,4,2,2,32,128]{5,4,3,2,1,0:T(8,128)(2,1)S(1)} %collective-permute-done.5.refs_3_), channel_id=1, source_target_pairs={{0,7},{1,2},{2,1},{3,4},{4,3},{5,6},{6,5},{7,0},{8,15},{9,10},{10,... | collective-permute-start | bytes 786440 | tf_op jit(solution)/shard_map/ppermute | solution.py:342
  49.3 14.4 %collective-permute-start.14 = (bf16[2,4,2,2,32,128]{5,4,3,2,1,0:T(8,128)(2,1)S(1)}, bf16[2,4,2,2,32,128]{5,4,3,2,1,0:T(8,128)(2,1)S(1)}, u32[]{:S(2)}, u32[]{:S(2)}) collective-permute-start(bf16[2,4,2,2,32,128]{5,4,3,2,1,0:T(8,128)(2,1)S(1)} %collective-permute-done.13.refs_8_), channel_id=1, source_target_pairs={{0,7},{1,2},{2,1},{3,4},{4,3},{5,6},{6,5},{7,0},{8,15},{9,10},{10,... | collective-permute-start | bytes 786440 | tf_op jit(solution)/shard_map/ppermute | solution.py:342
  96.0 6.8 %collective-permute-start.22 = (bf16[2,4,2,2,32,128]{5,4,3,2,1,0:T(8,128)(2,1)S(1)}, bf16[2,4,2,2,32,128]{5,4,3,2,1,0:T(8,128)(2,1)S(1)}, u32[]{:S(2)}, u32[]{:S(2)}) collective-permute-start(bf16[2,4,2,2,32,128]{5,4,3,2,1,0:T(8,128)(2,1)S(1)} %get-tuple-element.65), channel_id=1, source_target_pairs={{0,1},{1,0},{2,3},{3,2},{4,5},{5,4},{6,7},{7,6},{8,9},{9,8},{10,11... | collective-permute-start | bytes 786440 | tf_op jit(solution)/shard_map/ppermute | solution.py:342
  96.1 8.2 %collective-permute-start.15 = (bf16[2,4,2,2,32,128]{5,4,3,2,1,0:T(8,128)(2,1)S(1)}, bf16[2,4,2,2,32,128]{5,4,3,2,1,0:T(8,128)(2,1)S(1)}, u32[]{:S(2)}, u32[]{:S(2)}) collective-permute-start(bf16[2,4,2,2,32,128]{5,4,3,2,1,0:T(8,128)(2,1)S(1)} %get-tuple-element.53), channel_id=1, source_target_pairs={{0,7},{1,2},{2,1},{3,4},{4,3},{5,6},{6,5},{7,0},{8,15},{9,10},{10,... | collective-permute-start | bytes 786440 | tf_op jit(solution)/shard_map/ppermute | solution.py:342
  102.9 7.1 %collective-permute-start.23 = (bf16[2,4,2,2,32,128]{5,4,3,2,1,0:T(8,128)(2,1)S(1)}, bf16[2,4,2,2,32,128]{5,4,3,2,1,0:T(8,128)(2,1)S(1)}, u32[]{:S(2)}, u32[]{:S(2)}) collective-permute-start(bf16[2,4,2,2,32,128]{5,4,3,2,1,0:T(8,128)(2,1)S(1)} %add_convert_fusion.1), channel_id=1, source_target_pairs={{0,7},{1,2},{2,1},{3,4},{4,3},{5,6},{6,5},{7,0},{8,15},{9,10},{10,... | collective-permute-start | bytes 786440 | tf_op jit(solution)/shard_map/ppermute | solution.py:342
  104.4 5.9 %collective-permute-start.16 = (bf16[2,4,2,2,32,128]{5,4,3,2,1,0:T(8,128)(2,1)S(1)}, bf16[2,4,2,2,32,128]{5,4,3,2,1,0:T(8,128)(2,1)S(1)}, u32[]{:S(2)}, u32[]{:S(2)}) collective-permute-start(bf16[2,4,2,2,32,128]{5,4,3,2,1,0:T(8,128)(2,1)S(1)} %add_convert_fusion.3), channel_id=1, source_target_pairs={{0,1},{1,0},{2,3},{3,2},{4,5},{5,4},{6,7},{7,6},{8,9},{9,8},{10,11... | collective-permute-start | bytes 786440 | tf_op jit(solution)/shard_map/ppermute | solution.py:342
  104.5 5.8 %collective-permute-start.17 = (bf16[2,32,3072]{2,1,0:T(8,128)(2,1)S(1)}, bf16[2,32,3072]{2,1,0:T(8,128)(2,1)S(1)}, u32[]{:S(2)}, u32[]{:S(2)}) collective-permute-start(bf16[2,32,3072]{2,1,0:T(8,128)(2,1)S(1)} %get-tuple-element.54), channel_id=1, source_target_pairs={{0,8},{8,0},{16,24},{24,16},{32,40},{40,32},{48,56},{56,48},{64,72... | collective-permute-start | bytes 1179656 | tf_op jit(solution)/shard_map/ppermute | solution.py:334
  106.8 10.7 %collective-permute-start.18 = (bf16[2,32,3072]{2,1,0:T(8,128)(2,1)S(1)}, bf16[2,32,3072]{2,1,0:T(8,128)(2,1)S(1)}, u32[]{:S(2)}, u32[]{:S(2)}) collective-permute-start(bf16[2,32,3072]{2,1,0:T(8,128)(2,1)S(1)} %get-tuple-element.55), channel_id=1, source_target_pairs={{0,16},{8,24},{16,0},{24,8},{32,48},{40,56},{48,32},{56,40},{64,80... | collective-permute-start | bytes 1179656 | tf_op jit(solution)/shard_map/ppermute | solution.py:334
  107.2 18.8 %collective-permute-start.19 = (bf16[2,32,3072]{2,1,0:T(8,128)(2,1)S(1)}, bf16[2,32,3072]{2,1,0:T(8,128)(2,1)S(1)}, u32[]{:S(2)}, u32[]{:S(2)}) collective-permute-start(bf16[2,32,3072]{2,1,0:T(8,128)(2,1)S(1)} %get-tuple-element.56), channel_id=1, source_target_pairs={{0,24},{8,16},{16,8},{24,0},{32,56},{40,48},{48,40},{56,32},{64,88... | collective-permute-start | bytes 1179656 | tf_op jit(solution)/shard_map/ppermute | solution.py:334
  110.1 17.5 %collective-permute-start.24 = (bf16[2,4,2,2,32,128]{5,4,3,2,1,0:T(8,128)(2,1)S(1)}, bf16[2,4,2,2,32,128]{5,4,3,2,1,0:T(8,128)(2,1)S(1)}, u32[]{:S(2)}, u32[]{:S(2)}) collective-permute-start(bf16[2,4,2,2,32,128]{5,4,3,2,1,0:T(8,128)(2,1)S(1)} %add_convert_fusion), channel_id=1, source_target_pairs={{0,1},{1,0},{2,3},{3,2},{4,5},{5,4},{6,7},{7,6},{8,9},{9,8},{10,11... | collective-permute-start | bytes 786440 | tf_op jit(solution)/shard_map/ppermute | solution.py:342
  126.0 8.8 %collective-permute-start.20 = (bf16[2,4,2,2,32,128]{5,4,3,2,1,0:T(8,128)(2,1)S(1)}, bf16[2,4,2,2,32,128]{5,4,3,2,1,0:T(8,128)(2,1)S(1)}, u32[]{:S(2)}, u32[]{:S(2)}) collective-permute-start(bf16[2,4,2,2,32,128]{5,4,3,2,1,0:T(8,128)(2,1)S(1)} %add_convert_fusion.2), channel_id=1, source_target_pairs={{0,7},{1,2},{2,1},{3,4},{4,3},{5,6},{6,5},{7,0},{8,15},{9,10},{10,... | collective-permute-start | bytes 786440 | tf_op jit(solution)/shard_map/ppermute | solution.py:342
  127.7 10.0 %collective-permute-start.25 = (bf16[1,4,2,2,32,128]{5,4,3,2,1,0:T(8,128)(2,1)S(1)}, bf16[1,4,2,2,32,128]{5,4,3,2,1,0:T(8,128)(2,1)S(1)}, u32[]{:S(2)}, u32[]{:S(2)}) collective-permute-start(bf16[1,4,2,2,32,128]{5,4,3,2,1,0:T(8,128)(2,1)S(1)} %slice.60), channel_id=1, source_target_pairs={{0,7},{1,2},{2,1},{3,4},{4,3},{5,6},{6,5},{7,0},{8,15},{9,10},{10,... | collective-permute-start | bytes 393224 | tf_op jit(solution)/shard_map/ppermute | solution.py:342
  137.7 8.1 %collective-permute-start.26 = (bf16[4,2,2,32,128]{4,3,2,1,0:T(8,128)(2,1)S(1)}, bf16[4,2,2,32,128]{4,3,2,1,0:T(8,128)(2,1)S(1)}, u32[]{:S(2)}, u32[]{:S(2)}) collective-permute-start(bf16[4,2,2,32,128]{4,3,2,1,0:T(8,128)(2,1)S(1)} %fusion.4), channel_id=1, source_target_pairs={{32,0},{40,8},{48,16},{56,24},{64,32},{72,40},{80,48},{88,56},{96,... | collective-permute-start | bytes 393224 | tf_op jit(solution)/shard_map/ppermute | solution.py:375
  (21 other events, 375.4 us)

commit v2 on v1

v2 whole, which is shorter than its diff:
```python
import functools

import jax
import jax.numpy as jnp
from jax import lax
from jax.experimental import pallas as pl
from jax.experimental.pallas import tpu as pltpu
from jax.sharding import PartitionSpec as P

HD = 128
QPK = 12
TB = 32
GROUP = 4
ROWS = QPK * TB
CHUNK = 256
SCALE = HD ** (-0.5)
LOG2E = 1.4426950408889634
NEG = -1e30
GATHERED = (0, 1, -1, -2, 2, 3, -3, 4)
HW = 2 * QPK * HD
KW = 2 * HD

ANY = pl.BlockSpec(memory_space=pl.ANY)
SMEM = pl.BlockSpec(memory_space=pltpu.SMEM)
VMEM = pl.BlockSpec(memory_space=pltpu.VMEM)
NT = (((1,), (1,)), ((), ()))
TN = (((0,), (0,)), ((), ()))
NN = (((1,), (0,)), ((), ()))


def bf16(*shape):
    return jax.ShapeDtypeStruct(shape, jnp.bfloat16)


def columns(start, width):
    return pl.ds(pl.multiple_of(start, 128), width)


def run_copies(copies):
    for copy in copies:
        copy.start()
    for copy in copies:
        copy.wait()


def split_kv_body(meta, keys, values, *refs):
    outs, sem = refs[:GROUP], refs[GROUP]
    group_at = meta[0]
    copies = []
    for d in range(GROUP):
        for n, source in enumerate((keys, values)):
            for head in range(2):
                at = (group_at ^ d) * KW + head * HD
                copies.append(
                    pltpu.make_async_copy(
                        source.at[:, columns(at, HD)], outs[d].at[n, head], sem.at[len(copies)]
                    )
                )
    run_copies(copies)


def split_kv(meta, keys, values):
    return pl.pallas_call(
        split_kv_body,
        in_specs=[SMEM, ANY, ANY],
        out_specs=[VMEM] * GROUP,
        out_shape=[bf16(2, 2, TB, HD)] * GROUP,
        scratch_shapes=[pltpu.SemaphoreType.DMA((4 * GROUP,))],
    )(meta, keys, values)


def split_queries_body(meta, queries, grads, *refs):
    outs, sem = refs[: 2 * (GROUP - 1)], refs[2 * (GROUP - 1)]
    group_at = meta[0]
    copies = []
    for d in range(1, GROUP):
        for n, source in enumerate((queries, grads)):
            copies.append(
                pltpu.make_async_copy(
                    source.at[:, columns((group_at ^ d) * HW, HW)],
                    outs[n * (GROUP - 1) + d - 1],
                    sem.at[len(copies)],
                )
            )
    run_copies(copies)


def split_queries(meta, queries, grads):
    return pl.pallas_call(
        split_queries_body,
        in_specs=[SMEM, ANY, ANY],
        out_specs=[VMEM] * (2 * (GROUP - 1)),
        out_shape=[bf16(TB, HW)] * (2 * (GROUP - 1)),
        scratch_shapes=[pltpu.SemaphoreType.DMA((2 * GROUP,))],
    )(meta, queries, grads)


def attention_body(meta, doc_starts, doc_tenant, tenant_weight, queries, grads, *refs):
    sent, refs = refs[:6], refs[6:]
    gathered, refs = refs[:5], refs[5:]
    partials, refs = refs[:4], refs[4:]
    outs, refs = refs[:8], refs[8:]
    kv, acc_k, acc_v, scores, head_q, head_w, attended_t, query_t = (refs[0],) + tuple(
        refs[1 + 2 * i : 3 + 2 * i] for i in range(7)
    )
    head_qt, head_wn = refs[15:17], refs[17:19]
    qs, gs, wide, sem_kv, sem_q, sem_out = refs[19:]
    group_at, z_at, pair_at = meta[0], meta[1], meta[2]
    n_docs = doc_starts.shape[0]
    side = (1 - 2 * (z_at & 1)) * (1 - 2 * (group_at & 1))

    copies = []
    at = 0
    for part in gathered:
        blocks = part.shape[0]
        copies.append(pltpu.make_async_copy(part, kv.at[pl.ds(at, blocks)], sem_kv))
        at += blocks
    own = columns(group_at * HW, HW)
    copies += [
        pltpu.make_async_copy(queries.at[:, own], qs.at[0], sem_q),
        pltpu.make_async_copy(grads.at[:, own], gs.at[0], sem_q),
    ]
    for d in range(3):
        copies.append(pltpu.make_async_copy(sent[d], qs.at[d + 1], sem_q))
        copies.append(pltpu.make_async_copy(sent[3 + d], gs.at[d + 1], sem_q))
    for copy in copies:
        copy.start()
    for h in range(2):
        acc_k[h][...] = jnp.zeros_like(acc_k[h])
        acc_v[h][...] = jnp.zeros_like(acc_v[h])
    rows_at = lax.broadcasted_iota(jnp.int32, (128, 128), 0)
    cols_at = lax.broadcasted_iota(jnp.int32, (128, 128), 1)
    eye = jnp.where(rows_at == cols_at, 1.0, 0.0).astype(jnp.bfloat16)
    for copy in copies:
        copy.wait()

    def dot(a, b, dims):
        return lax.dot_general(a, b, dims, preferred_element_type=jnp.float32)

    def flip(x):
        return jnp.concatenate(
            [x[:, i * 128 : (i + 1) * 128].T for i in range(x.shape[1] // 128)], axis=0
        )

    def flip_back(x):
        return jnp.concatenate(
            [x[i * 128 : (i + 1) * 128].T for i in range(x.shape[0] // 128)], axis=1
        )

    window_at = 1024 * (pair_at - 1)
    c_scale = SCALE * LOG2E

    def block(d, carry):
        sub = group_at ^ d
        first = 1024 * pair_at + CHUNK * sub + TB * z_at
        lowest = jnp.int32(0)
        for n in range(n_docs):
            lowest = jnp.where(doc_starts[n] <= first, doc_starts[n], lowest)
        chunk_lo = jnp.maximum((lowest - window_at) >> 8, 0)
        chunk_hi = 4 + sub + 1
        lane = lax.broadcasted_iota(jnp.int32, (1, 128), 1)
        token = first + (lane & (TB - 1))
        start = jnp.zeros((1, 128), jnp.int32)
        scaling = jnp.zeros((1, 128), jnp.float32)
        for n in range(n_docs):
            inside = doc_starts[n] <= token
            start = jnp.where(inside, doc_starts[n], start)
            scaling = jnp.where(inside, tenant_weight[doc_tenant[n]], scaling)
        scaling = jnp.concatenate([scaling] * 3, axis=1)

        def head_columns(h, m):
            return slice((h * QPK + m) * HD, (h * QPK + m + 1) * HD)

        for h in range(2):
            for m in range(QPK):
                head_q[h][m * TB : (m + 1) * TB, :] = qs[d, :, head_columns(h, m)]
            raw = jnp.concatenate([gs[d, :, head_columns(h, m)] for m in range(QPK)], axis=0)
            head_w[h][...] = (flip_back(raw) * scaling).astype(jnp.bfloat16)
            head_wn[h][...] = flip(head_w[h][...]).astype(jnp.bfloat16)
            head_qt[h][...] = flip_back(head_q[h][...]).astype(jnp.bfloat16)

        def first_pass(c, tops):
            base = window_at + c * CHUNK
            row = lax.broadcasted_iota(jnp.int32, (TB, 128), 0)
            bias = []
            for off in GATHERED:
                key = base + TB * ((z_at + side * off + 8) & 7) + row
                bias.append(jnp.where((key >= start) & (key <= token), 0.0, NEG))
            bias = jnp.concatenate(bias, axis=0)
            bias = jnp.concatenate([bias] * 3, axis=1)
            new = []
            for h in range(2):
                k = kv[:, c >> 2, (c & 3) ^ group_at, 0, h].reshape(CHUNK, HD)
                s = dot(k, head_qt[h][...], NN) + bias
                scores[h][c] = s
                new.append(jnp.maximum(tops[h], jnp.max(s.reshape(CHUNK // 8, 8, ROWS), axis=0)))
            return tuple(new)

        def work(chunks):
            def static_loop(f, carry):
                for i in range(chunks):
                    carry = f(chunk_lo + i, carry)
                return carry

            top = jnp.full((8, ROWS), NEG, jnp.float32)
            tops = static_loop(first_pass, (top, top))
            tops = [jnp.max(t, axis=0, keepdims=True) for t in tops]

            for h in range(2):
                attended_t[h][...] = jnp.zeros_like(attended_t[h])
                query_t[h][...] = jnp.zeros_like(query_t[h])

            def second_pass(c, sums):
                new = []
                for h in range(2):
                    p = jnp.exp2((scores[h][c] - tops[h]) * c_scale)
                    scores[h][c] = p
                    new.append(sums[h] + jnp.sum(p.reshape(CHUNK // 8, 8, ROWS), axis=0))
                    v = kv[:, c >> 2, (c & 3) ^ group_at, 1, h].reshape(CHUNK, HD)
                    attended_t[h][...] += dot(v, p.astype(jnp.bfloat16), TN)
                return tuple(new)

            zero = jnp.zeros((8, ROWS), jnp.float32)
            sums = static_loop(second_pass, (zero, zero))
            inverse = [1.0 / jnp.sum(s, axis=0, keepdims=True) for s in sums]
            deltas = []
            for h in range(2):
                rounded = (attended_t[h][...] * inverse[h]).astype(jnp.bfloat16)
                product = rounded.astype(jnp.float32) * head_w[h][...].astype(jnp.float32)
                deltas.append(jnp.sum(product, axis=0, keepdims=True))
                out = flip(rounded).astype(jnp.bfloat16)
                for m in range(QPK):
                    wide[d, 0, :, head_columns(h, m)] = out[m * TB : (m + 1) * TB]

            def third_pass(c, carry):
                for h in range(2):
                    k = kv[:, c >> 2, (c & 3) ^ group_at, 0, h].reshape(CHUNK, HD)
                    v = kv[:, c >> 2, (c & 3) ^ group_at, 1, h].reshape(CHUNK, HD)
                    p = scores[h][c] * inverse[h]
                    push = dot(v, head_w[h][...], NN)
                    ds = (p * (push - deltas[h])).astype(jnp.bfloat16)
                    at = (slice(None), c >> 2, (c & 3) ^ group_at)
                    acc_v[h][at] += dot(p.astype(jnp.bfloat16), head_wn[h][...], NN).reshape(8, TB, HD)
                    acc_k[h][at] += dot(ds, head_q[h][...], NN).reshape(8, TB, HD)
                    query_t[h][...] += dot(k, ds, TN)
                return carry

            static_loop(third_pass, 0)
            for h in range(2):
                out = flip((query_t[h][...] * SCALE).astype(jnp.bfloat16)).astype(jnp.bfloat16)
                for m in range(QPK):
                    wide[d, 1, :, head_columns(h, m)] = out[m * TB : (m + 1) * TB]

        for chunks in range(1, 6):
            pl.when(chunk_hi - chunk_lo == chunks)(functools.partial(work, chunks))
        for n in range(4):

            @pl.when(d == n)
            def _():
                for i in range(2):
                    pltpu.make_async_copy(wide.at[n, i], outs[2 * n + i], sem_out).start()

        return carry

    lax.fori_loop(0, 4, block, 0)

    for at in range(8):
        target = partials[at // 2]
        for h in range(2):
            target[at % 2, :, :, 0, h] = (acc_k[h][at] * SCALE).astype(jnp.bfloat16)
            target[at % 2, :, :, 1, h] = acc_v[h][at].astype(jnp.bfloat16)
    for n in range(4):
        for i in range(2):
            pltpu.make_async_copy(wide.at[n, i], outs[2 * n + i], sem_out).wait()


def attention(meta, doc_starts, doc_tenant, tenant_weight, queries, grads, sent, gathered):
    def vmem(dtype, *shape):
        return pltpu.VMEM(shape, dtype)

    part = bf16(2, 2, 4, 2, 2, TB, HD)
    return pl.pallas_call(
        attention_body,
        in_specs=[SMEM] * 4 + [ANY] * 2 + [VMEM] * 11,
        out_specs=[VMEM] * 12,
        out_shape=[part] * 4 + [bf16(TB, HW)] * 8,
        scratch_shapes=[vmem(jnp.bfloat16, 8, 2, 4, 2, 2, TB, HD)]
        + [vmem(jnp.float32, 8, 2, 4, TB, HD)] * 4
        + [vmem(jnp.float32, 8, CHUNK, ROWS)] * 2
        + [vmem(jnp.bfloat16, ROWS, HD)] * 2
        + [vmem(jnp.bfloat16, HD, ROWS)] * 2
        + [vmem(jnp.float32, HD, ROWS)] * 4
        + [vmem(jnp.bfloat16, HD, ROWS)] * 2
        + [vmem(jnp.bfloat16, ROWS, HD)] * 2
        + [vmem(jnp.bfloat16, 4, TB, HW)] * 2
        + [vmem(jnp.bfloat16, 4, 2, TB, HW)]
        + [pltpu.SemaphoreType.DMA] * 3,
        compiler_params=pltpu.CompilerParams(vmem_limit_bytes=40 * 1024 * 1024),
        cost_estimate=pl.CostEstimate(flops=3 * 10**9, bytes_accessed=10**7, transcendentals=10**6),
    )(meta, doc_starts, doc_tenant, tenant_weight, queries, grads, *sent, *gathered)


def join_body(meta, *refs):
    ins, refs = refs[: 3 * GROUP], refs[3 * GROUP :]
    attended, query_grad, key_grad, value_grad, sem = refs
    group_at = meta[0]
    copies = []
    for d in range(GROUP):
        for n, target in enumerate((attended, query_grad)):
            copies.append(
                pltpu.make_async_copy(
                    ins[2 * d + n], target.at[:, columns((group_at ^ d) * HW, HW)], sem.at[len(copies)]
                )
            )
        for n, target in enumerate((key_grad, value_grad)):
            for head in range(2):
                at = (group_at ^ d) * KW + head * HD
                copies.append(
                    pltpu.make_async_copy(
                        ins[2 * GROUP + d].at[n, head], target.at[:, columns(at, HD)], sem.at[len(copies)]
                    )
                )
    run_copies(copies)


def join(meta, wide, narrow):
    return pl.pallas_call(
        join_body,
        in_specs=[SMEM] + [VMEM] * (3 * GROUP),
        out_specs=[ANY] * 4,
        out_shape=[bf16(TB, 96 * HD)] * 2 + [bf16(TB, 8 * HD)] * 2,
        scratch_shapes=[pltpu.SemaphoreType.DMA((6 * GROUP,))],
    )(meta, *wide, *narrow)


def swap_in_group(x, d):
    return lax.ppermute(x, "ctx", [(i, i ^ d) for i in range(lax.axis_size("ctx"))])


def swap_on_z(x, phase):
    pairs = []
    for i in range(lax.axis_size("ctx")):
        for z in range(8):
            up = (z + phase + i) % 2 == 0
            pairs.append((8 * i + z, 8 * i + (z + 1 if up else z - 1) % 8))
    return lax.ppermute(x, ("ctx", "hg"), pairs)


def arrived(x, *beside):
    return lax.optimization_barrier((x, *beside))


def add(a, b):
    return (a.astype(jnp.float32) + b.astype(jnp.float32)).astype(jnp.bfloat16)


def shift_pairs(x, by):
    devices = lax.axis_size("ctx")
    pairs = [(i, i + by) for i in range(devices) if 0 <= i + by < devices]
    return lax.ppermute(x, "ctx", pairs)


def local(query_states, key_states, value_states, out_grad, doc_starts, doc_tenant, tenant_weight):
    ctx_at = lax.axis_index("ctx")
    z_at = lax.axis_index("hg")
    meta = jnp.stack([ctx_at & 3, z_at, ctx_at >> 2]).astype(jnp.int32)

    kv = split_kv(meta, key_states, value_states)
    own = jnp.stack([kv[0]] + [swap_in_group(kv[d], d) for d in range(1, GROUP)])
    sent = split_queries(meta, query_states, out_grad)
    own, sent = lax.optimization_barrier((own, sent))
    q1, q2, q3, g1, g2, g3 = [swap_in_group(x, i % 3 + 1) for i, x in enumerate(sent)]
    first = jnp.stack([shift_pairs(own, GROUP), own])[None]
    first, q1, g1 = arrived(first, q1, g1)
    second = swap_on_z(first, 0)
    third = swap_on_z(jnp.concatenate([first, second]), 1)
    third, q2 = arrived(third, q2)
    fourth = swap_on_z(third, 0)
    fourth, q3 = arrived(fourth, q3)
    fifth = swap_on_z(fourth, 1)

    results = attention(
        meta,
        doc_starts,
        doc_tenant,
        tenant_weight,
        query_states,
        out_grad,
        (q1, q2, q3, g1, g2, g3),
        (first, second, third, fourth, fifth),
    )
    parts, wide = results[:4], list(results[4:])

    for d in range(1, GROUP):
        for i in range(2):
            wide[2 * d + i] = swap_in_group(wide[2 * d + i], d)
    moved = swap_on_z(parts[3], 1)
    moved, wide[2], wide[3], wide[4] = arrived(add(parts[2], moved), wide[2], wide[3], wide[4])
    moved = swap_on_z(moved, 0)
    moved, wide[6] = arrived(add(parts[1], moved), wide[6])
    moved = swap_on_z(moved, 1)
    passed, wide[5] = arrived(add(parts[0][1], moved[1]), wide[5])
    passed = swap_on_z(passed, 0).astype(jnp.float32)
    passed = passed + parts[0][0].astype(jnp.float32) + moved[0].astype(jnp.float32)
    earlier_sum, wide[7] = arrived(passed[0].astype(jnp.bfloat16), wide[7])
    earlier_sum = shift_pairs(earlier_sum, -GROUP)
    total = (passed[1] + earlier_sum.astype(jnp.float32)).astype(jnp.bfloat16)
    narrow = [total[0]] + [swap_in_group(total[d], d) for d in range(1, GROUP)]
    return tuple(join(meta, wide, narrow))


def solution(mesh):
    row = P(("ctx", "hg"), None)
    return jax.shard_map(
        local,
        mesh=mesh,
        in_specs=(row, row, row, row, P(), P(), P()),
        out_specs=(row, row, row, row),
        check_vma=False,
    )
```

time: 156 us -> 133 us (0.85)
  Pallas kernels: 40.6 us -> 25.2 us
  waiting for transfers between devices: 74.1 us -> 66.3 us
    pallas_call x1, Pallas kernels: 32.3 us -> 16.9 us  [attention(): pl.pallas_call(attention_body, in_specs=[SMEM] * 4 + [ANY] * 2 + [VMEM] *...]
    ppermute x16 -> x8, starting transfers between devices: 17.6 us -> 9.17 us  [swap_on_z(): return lax.ppermute(x, ('ctx', 'hg'), pairs)]
    ppermute x12 -> x18, waiting for transfers between devices: 31.9 us -> 24 us  [swap_in_group(): lax.ppermute(x, 'ctx', [(i, i ^ d) for i in range(lax.axis_size('ctx'))])]
    ppermute x12 -> x18, starting transfers between devices: 14.1 us -> 21.2 us  [swap_in_group(): lax.ppermute(x, 'ctx', [(i, i ^ d) for i in range(lax.axis_size('ctx'))])]
    ppermute x2, waiting for transfers between devices: 9 us -> 10.7 us  [shift_pairs(): return lax.ppermute(x, 'ctx', pairs)]
    ppermute x16 -> x8, waiting for transfers between devices: 33.3 us -> 31.6 us  [swap_on_z(): return lax.ppermute(x, ('ctx', 'hg'), pairs)]
  transfers between devices with their start and end apart: 30 -> 28, of which waited for: 17 -> 14; matrix products, arithmetic and copies ran while one was open for 0% -> 0% of each run, Pallas kernels for 2% -> 2%
where the time goes in v2:
time: 133 us; the launch traced here: 132 us
  waiting for transfers between devices  66.3 us (50%)
  starting transfers between devices  36.2 us (27%)
  Pallas kernels  25.2 us (19%)
  other arithmetic  1.33 us (1%)
  local copies, waits for them, and re-layouts  1.33 us (1%)
    ppermute x8, waiting for transfers between devices, swap_on_z(): return lax.ppermute(x, ('ctx', 'hg'), pairs)  31.6 us
    ppermute x18, waiting for transfers between devices, swap_in_group(): lax.ppermute(x, 'ctx', [(i, i ^ d) for i in range(lax.axis_size('ctx'))])  24 us
    ppermute x18, starting transfers between devices, swap_in_group(): lax.ppermute(x, 'ctx', [(i, i ^ d) for i in range(lax.axis_size('ctx'))])  21.2 us
    pallas_call x1, Pallas kernels, attention(): pl.pallas_call(attention_body, in_specs=[SMEM] * 4 + [ANY] * 2 + [VMEM] *...  16.9 us
    ppermute x2, waiting for transfers between devices, shift_pairs(): return lax.ppermute(x, 'ctx', pairs)  10.7 us
    ppermute x8, starting transfers between devices, swap_on_z(): return lax.ppermute(x, ('ctx', 'hg'), pairs)  9.17 us
    ppermute x2, starting transfers between devices, shift_pairs(): return lax.ppermute(x, 'ctx', pairs)  5.83 us
    pallas_call x1, Pallas kernels, split_queries(): pl.pallas_call(split_queries_body, in_specs=[SMEM, ANY, ANY], out_specs=[...  3.08 us
  transfers between devices with their start and end apart: 28, of which 14 were waited for; matrix products, arithmetic and copies ran while one was open for 0% of the time, Pallas kernels for 2%

profile of v2, /device:TPU:25, one launch (start us, length us, event | category | flops | bytes accessed | tf_op | source)
XLA Modules:
  0.0 131.6 jit_solution(12713842684128501028)
XLA Ops:
  1.2 2.3 %shard_map.102 = (bf16[2,2,32,128]{3,2,1,0:T(8,128)(2,1)}, bf16[2,2,32,128]{3,2,1,0:T(8,128)(2,1)}, bf16[2,2,32,128]{3,2,1,0:T(8,128)(2,1)}, bf16[2,2,32,128]{3,2,1,0:T(8,128)(2,1)}) custom-call(s32[3]{0:T(128)} %pad_add_fusion.meta, bf16[32,1024]{1,0:T(8,128)(2,1)} %keys.1, bf16[32,1024]{1,0:T(8,128)(2,1)} %values.1), custom_call_target="tpu_custom_call" | custom-call | tf_op jit(solution)/shard_map/pallas_call | solution.py:63
  6.1 3.1 %shard_map.103 = (bf16[32,3072]{1,0:T(8,128)(2,1)}, bf16[32,3072]{1,0:T(8,128)(2,1)}, bf16[32,3072]{1,0:T(8,128)(2,1)}, bf16[32,3072]{1,0:T(8,128)(2,1)}, bf16[3...) custom-call(s32[3]{0:T(128)} %pad_add_fusion.meta, bf16[32,12288]{1,0:T(8,128)(2,1)} %queries.3, bf16[32,12288]{1,0:T(8,128)(2,1)} %grads.3), custom_call_target="tpu_custom_call" | custom-call | tf_op jit(solution)/shard_map/pallas_call | solution.py:89
  9.2 3.9 %collective-permute-start.3 = (bf16[4,2,2,32,128]{4,3,2,1,0:T(8,128)(2,1)S(1)}, bf16[4,2,2,32,128]{4,3,2,1,0:T(8,128)(2,1)S(1)}, u32[]{:S(2)}, u32[]{:S(2)}) collective-permute-start(bf16[4,2,2,32,128]{4,3,2,1,0:T(8,128)(2,1)S(1)} %pad_maximum_fusion.1), channel_id=1, source_target_pairs={{0,32},{8,40},{16,48},{24,56},{32,64},{40,72},{48,80},{56,88},{64,... | collective-permute-start | bytes 393224 | tf_op jit(solution)/shard_map/ppermute | solution.py:360
  13.8 3.9 %collective-permute-done.3 = bf16[4,2,2,32,128]{4,3,2,1,0:T(8,128)(2,1)S(1)} collective-permute-done((bf16[4,2,2,32,128]{4,3,2,1,0:T(8,128)(2,1)S(1)}, bf16[4,2,2,32,128]{4,3,2,1,0:T(8,128)(2,1)S(1)}, u32[]{:S(2)}, u32[]{:S(2)}) %collective-permute-start.3) | collective-permute-done | bytes 131104 | tf_op jit(solution)/shard_map/ppermute | solution.py:360
  17.8 5.7 %collective-permute-start.6 = (bf16[1,2,4,2,2,32,128]{6,5,4,3,2,1,0:T(8,128)(2,1)S(1)}, bf16[1,2,4,2,2,32,128]{6,5,4,3,2,1,0:T(8,128)(2,1)S(1)}, u32[]{:S(2)}, u32[]{:S(2)}) collective-permute-start(bf16[1,2,4,2,2,32,128]{6,5,4,3,2,1,0:T(8,128)(2,1)S(1)} %maximum_bitcast_fusion.refs_6_), channel_id=1, source_target_pairs={{0,1},{1,0},{2,3},{3,2},{4,5},{5,4},{6,7},{7,6},{8,15},{9,10},{10,... | collective-permute-start | bytes 786440 | tf_op jit(solution)/shard_map/ppermute | solution.py:346
  23.5 3.8 %collective-permute-done.6.refs_7_ = bf16[1,2,4,2,2,32,128]{6,5,4,3,2,1,0:T(8,128)(2,1)S(1)} collective-permute-done((bf16[1,2,4,2,2,32,128]{6,5,4,3,2,1,0:T(8,128)(2,1)S(1)}, bf16[1,2,4,2,2,32,128]{6,5,4,3,2,1,0:T(8,128)(2,1)S(1)}, u32[]{:S(2)}, u32[]{:S(2)}) %collective-permute-start.6) | collective-permute-done | bytes 262176 | tf_op jit(solution)/shard_map/ppermute | solution.py:346
  27.9 4.6 %collective-permute-done.8.refs_1_ = bf16[32,3072]{1,0:T(8,128)(2,1)S(1)} collective-permute-done((bf16[32,3072]{1,0:T(8,128)(2,1)}, bf16[32,3072]{1,0:T(8,128)(2,1)S(1)}, u32[]{:S(2)}, u32[]{:S(2)}) %collective-permute-start.8) | collective-permute-done | bytes 196640 | tf_op jit(solution)/shard_map/ppermute | solution.py:337
  32.5 3.2 %collective-permute-done.7.refs_8_ = bf16[2,2,4,2,2,32,128]{6,5,4,3,2,1,0:T(8,128)(2,1)S(1)} collective-permute-done((bf16[2,2,4,2,2,32,128]{6,5,4,3,2,1,0:T(8,128)(2,1)S(1)}, bf16[2,2,4,2,2,32,128]{6,5,4,3,2,1,0:T(8,128)(2,1)S(1)}, u32[]{:S(2)}, u32[]{:S(2)}) %collective-permute-start.7) | collective-permute-done | bytes 524320 | tf_op jit(solution)/shard_map/ppermute | solution.py:346
  35.7 2.7 %collective-permute-start.9 = (bf16[2,2,4,2,2,32,128]{6,5,4,3,2,1,0:T(8,128)(2,1)S(1)}, bf16[2,2,4,2,2,32,128]{6,5,4,3,2,1,0:T(8,128)(2,1)S(1)}, u32[]{:S(2)}, u32[]{:S(2)}) collective-permute-start(bf16[2,2,4,2,2,32,128]{6,5,4,3,2,1,0:T(8,128)(2,1)S(1)} %collective-permute-done.7.refs_8_), channel_id=1, source_target_pairs={{0,1},{1,0},{2,3},{3,2},{4,5},{5,4},{6,7},{7,6},{8,15},{9,10},{10,... | collective-permute-start | bytes 1572872 | tf_op jit(solution)/shard_map/ppermute | solution.py:346
  38.7 6.7 %collective-permute-done.10.refs_2_ = bf16[32,3072]{1,0:T(8,128)(2,1)S(1)} collective-permute-done((bf16[32,3072]{1,0:T(8,128)(2,1)}, bf16[32,3072]{1,0:T(8,128)(2,1)S(1)}, u32[]{:S(2)}, u32[]{:S(2)}) %collective-permute-start.10) | collective-permute-done | bytes 196640 | tf_op jit(solution)/shard_map/ppermute | solution.py:337
  47.3 5.1 %collective-permute-start.12 = (bf16[32,3072]{1,0:T(8,128)(2,1)S(1)}, bf16[32,3072]{1,0:T(8,128)(2,1)S(1)}, u32[]{:S(2)}, u32[]{:S(2)}) collective-permute-start(bf16[32,3072]{1,0:T(8,128)(2,1)S(1)} %copy-done.18), channel_id=1, source_target_pairs={{0,24},{8,16},{16,8},{24,0},{32,56},{40,48},{48,40},{56,32},{64,88... | collective-permute-start | bytes 589832 | tf_op jit(solution)/shard_map/ppermute | solution.py:337
  52.4 7.7 %collective-permute-done.12.refs_5_ = bf16[32,3072]{1,0:T(8,128)(2,1)S(1)} collective-permute-done((bf16[32,3072]{1,0:T(8,128)(2,1)S(1)}, bf16[32,3072]{1,0:T(8,128)(2,1)S(1)}, u32[]{:S(2)}, u32[]{:S(2)}) %collective-permute-start.12) | collective-permute-done | bytes 196640 | tf_op jit(solution)/shard_map/ppermute | solution.py:337
  60.2 16.9 %shard_map.104 = (bf16[2,2,4,2,2,32,128]{6,5,4,3,2,1,0:T(8,128)(2,1)S(1)}, bf16[2,2,4,2,2,32,128]{6,5,4,3,2,1,0:T(8,128)(2,1)S(1)}, bf16[2,2,4,2,2,32,128]{6,5,4...) custom-call(s32[3]{0:T(128)S(1)} %copy-done.4, ...), custom_call_target="tpu_custom_call" | custom-call | flops 3000000000 | bytes 10000000 | tf_op jit(solution)/shard_map/pallas_call | solution.py:282
  78.4 7.2 %collective-permute-done.14 = bf16[2,2,4,2,2,32,128]{6,5,4,3,2,1,0:T(8,128)(2,1)S(1)} collective-permute-done((bf16[2,2,4,2,2,32,128]{6,5,4,3,2,1,0:T(8,128)(2,1)S(1)}, bf16[2,2,4,2,2,32,128]{6,5,4,3,2,1,0:T(8,128)(2,1)S(1)}, u32[]{:S(2)}, u32[]{:S(2)}) %collective-permute-start.14) | collective-permute-done | bytes 524320 | tf_op jit(solution)/shard_map/ppermute | solution.py:346
  86.0 2.0 %collective-permute-start.19 = (bf16[32,3072]{1,0:T(8,128)(2,1)S(1)}, bf16[32,3072]{1,0:T(8,128)(2,1)S(1)}, u32[]{:S(2)}, u32[]{:S(2)}) collective-permute-start(bf16[32,3072]{1,0:T(8,128)(2,1)S(1)} %get-tuple-element.87), channel_id=1, source_target_pairs={{0,24},{8,16},{16,8},{24,0},{32,56},{40,48},{48,40},{56,32},{64,88... | collective-permute-start | bytes 589832 | tf_op jit(solution)/shard_map/ppermute | solution.py:337
  87.9 7.2 %collective-permute-done.18 = bf16[2,2,4,2,2,32,128]{6,5,4,3,2,1,0:T(8,128)(2,1)S(1)} collective-permute-done((bf16[2,2,4,2,2,32,128]{6,5,4,3,2,1,0:T(8,128)(2,1)S(1)}, bf16[2,2,4,2,2,32,128]{6,5,4,3,2,1,0:T(8,128)(2,1)S(1)}, u32[]{:S(2)}, u32[]{:S(2)}) %collective-permute-start.18) | collective-permute-done | bytes 524320 | tf_op jit(solution)/shard_map/ppermute | solution.py:346
  96.1 7.7 %collective-permute-done.20 = bf16[2,2,4,2,2,32,128]{6,5,4,3,2,1,0:T(8,128)(2,1)S(1)} collective-permute-done((bf16[2,2,4,2,2,32,128]{6,5,4,3,2,1,0:T(8,128)(2,1)S(1)}, bf16[2,2,4,2,2,32,128]{6,5,4,3,2,1,0:T(8,128)(2,1)S(1)}, u32[]{:S(2)}, u32[]{:S(2)}) %collective-permute-start.20) | collective-permute-done | bytes 524320 | tf_op jit(solution)/shard_map/ppermute | solution.py:346
  104.1 4.0 %collective-permute-start.23 = (bf16[32,3072]{1,0:T(8,128)(2,1)S(1)}, bf16[32,3072]{1,0:T(8,128)(2,1)S(1)}, u32[]{:S(2)}, u32[]{:S(2)}) collective-permute-start(bf16[32,3072]{1,0:T(8,128)(2,1)S(1)} %get-tuple-element.93), channel_id=1, source_target_pairs={{0,24},{8,16},{16,8},{24,0},{32,56},{40,48},{48,40},{56,32},{64,88... | collective-permute-start | bytes 589832 | tf_op jit(solution)/shard_map/ppermute | solution.py:337
  108.1 2.4 %collective-permute-done.22 = bf16[2,4,2,2,32,128]{5,4,3,2,1,0:T(8,128)(2,1)S(1)} collective-permute-done((bf16[2,4,2,2,32,128]{5,4,3,2,1,0:T(8,128)(2,1)S(1)}, bf16[2,4,2,2,32,128]{5,4,3,2,1,0:T(8,128)(2,1)S(1)}, u32[]{:S(2)}, u32[]{:S(2)}) %collective-permute-start.22) | collective-permute-done | bytes 262176 | tf_op jit(solution)/shard_map/ppermute | solution.py:346
  110.7 3.0 %collective-permute-done.23.refs_7_ = bf16[32,3072]{1,0:T(8,128)(2,1)S(1)} collective-permute-done((bf16[32,3072]{1,0:T(8,128)(2,1)S(1)}, bf16[32,3072]{1,0:T(8,128)(2,1)S(1)}, u32[]{:S(2)}, u32[]{:S(2)}) %collective-permute-start.23) | collective-permute-done | bytes 196640 | tf_op jit(solution)/shard_map/ppermute | solution.py:337
  113.6 1.9 %collective-permute-start.24 = (bf16[4,2,2,32,128]{4,3,2,1,0:T(8,128)(2,1)S(1)}, bf16[4,2,2,32,128]{4,3,2,1,0:T(8,128)(2,1)S(1)}, u32[]{:S(2)}, u32[]{:S(2)}) collective-permute-start(bf16[4,2,2,32,128]{4,3,2,1,0:T(8,128)(2,1)S(1)} %fusion.3), channel_id=1, source_target_pairs={{32,0},{40,8},{48,16},{56,24},{64,32},{72,40},{80,48},{88,56},{96,... | collective-permute-start | bytes 393224 | tf_op jit(solution)/shard_map/ppermute | solution.py:360
  115.5 6.8 %collective-permute-done.24 = bf16[4,2,2,32,128]{4,3,2,1,0:T(8,128)(2,1)S(1)} collective-permute-done((bf16[4,2,2,32,128]{4,3,2,1,0:T(8,128)(2,1)S(1)}, bf16[4,2,2,32,128]{4,3,2,1,0:T(8,128)(2,1)S(1)}, u32[]{:S(2)}, u32[]{:S(2)}) %collective-permute-start.24) | collective-permute-done | bytes 131104 | tf_op jit(solution)/shard_map/ppermute | solution.py:360
  126.4 1.6 %collective-permute-done.26.refs_10_ = bf16[2,2,32,128]{3,2,1,0:T(8,128)(2,1)S(1)} collective-permute-done((bf16[2,2,32,128]{3,2,1,0:T(8,128)(2,1)S(1)}, bf16[2,2,32,128]{3,2,1,0:T(8,128)(2,1)S(1)}, u32[]{:S(2)}, u32[]{:S(2)}) %collective-permute-start.26) | collective-permute-done | bytes 32800 | tf_op jit(solution)/shard_map/ppermute | solution.py:337
  128.6 2.9 %shard_map.105 = (bf16[32,12288]{1,0:T(8,128)(2,1)}, bf16[32,12288]{1,0:T(8,128)(2,1)}, bf16[32,1024]{1,0:T(8,128)(2,1)}, bf16[32,1024]{1,0:T(8,128)(2,1)}) custom-call(s32[3]{0:T(128)} %pad_add_fusion.meta, bf16[32,3072]{1,0:T(8,128)(2,1)} %copy-done.2, bf16[32,3072]{1,0:T(8,128)(2,1)} %copy-done.3, bf16[32,3072]{1,0:T(8,128)(2,1)} %copy-done.8, ...), custom_call_target="tpu_custom_call" | custom-call | tf_op jit(solution)/shard_map/pallas_call | solution.py:327
  (85 shorter events, 14.1 us)
Async XLA Ops:
  3.6 5.6 %collective-permute-start = (bf16[2,2,32,128]{3,2,1,0:T(8,128)(2,1)}, bf16[2,2,32,128]{3,2,1,0:T(8,128)(2,1)S(1)}, u32[]{:S(2)}, u32[]{:S(2)}) collective-permute-start(bf16[2,2,32,128]{3,2,1,0:T(8,128)(2,1)} %get-tuple-element.51), channel_id=1, source_target_pairs={{0,8},{8,0},{16,24},{24,16},{32,40},{40,32},{48,56},{56,48},{64,72... | collective-permute-start | bytes 98312 | tf_op jit(solution)/shard_map/ppermute | solution.py:337
  4.3 4.8 %collective-permute-start.1 = (bf16[2,2,32,128]{3,2,1,0:T(8,128)(2,1)}, bf16[2,2,32,128]{3,2,1,0:T(8,128)(2,1)S(1)}, u32[]{:S(2)}, u32[]{:S(2)}) collective-permute-start(bf16[2,2,32,128]{3,2,1,0:T(8,128)(2,1)} %get-tuple-element.52), channel_id=1, source_target_pairs={{0,16},{8,24},{16,0},{24,8},{32,48},{40,56},{48,32},{56,40},{64,80... | collective-permute-start | bytes 98312 | tf_op jit(solution)/shard_map/ppermute | solution.py:337
  4.8 4.4 %collective-permute-start.2 = (bf16[2,2,32,128]{3,2,1,0:T(8,128)(2,1)}, bf16[2,2,32,128]{3,2,1,0:T(8,128)(2,1)S(1)}, u32[]{:S(2)}, u32[]{:S(2)}) collective-permute-start(bf16[2,2,32,128]{3,2,1,0:T(8,128)(2,1)} %get-tuple-element.53), channel_id=1, source_target_pairs={{0,24},{8,16},{16,8},{24,0},{32,56},{40,48},{48,40},{56,32},{64,88... | collective-permute-start | bytes 98312 | tf_op jit(solution)/shard_map/ppermute | solution.py:337
  9.2 8.5 %collective-permute-start.3 = (bf16[4,2,2,32,128]{4,3,2,1,0:T(8,128)(2,1)S(1)}, bf16[4,2,2,32,128]{4,3,2,1,0:T(8,128)(2,1)S(1)}, u32[]{:S(2)}, u32[]{:S(2)}) collective-permute-start(bf16[4,2,2,32,128]{4,3,2,1,0:T(8,128)(2,1)S(1)} %pad_maximum_fusion.1), channel_id=1, source_target_pairs={{0,32},{8,40},{16,48},{24,56},{32,64},{40,72},{48,80},{56,88},{64,... | collective-permute-start | bytes 393224 | tf_op jit(solution)/shard_map/ppermute | solution.py:360
  13.2 4.6 %collective-permute-start.4 = (bf16[32,3072]{1,0:T(8,128)(2,1)}, bf16[32,3072]{1,0:T(8,128)(2,1)S(1)}, u32[]{:S(2)}, u32[]{:S(2)}) collective-permute-start(bf16[32,3072]{1,0:T(8,128)(2,1)} %get-tuple-element.61), channel_id=1, source_target_pairs={{0,8},{8,0},{16,24},{24,16},{32,40},{40,32},{48,56},{56,48},{64,72... | collective-permute-start | bytes 589832 | tf_op jit(solution)/shard_map/ppermute | solution.py:337
  17.8 9.4 %collective-permute-start.6 = (bf16[1,2,4,2,2,32,128]{6,5,4,3,2,1,0:T(8,128)(2,1)S(1)}, bf16[1,2,4,2,2,32,128]{6,5,4,3,2,1,0:T(8,128)(2,1)S(1)}, u32[]{:S(2)}, u32[]{:S(2)}) collective-permute-start(bf16[1,2,4,2,2,32,128]{6,5,4,3,2,1,0:T(8,128)(2,1)S(1)} %maximum_bitcast_fusion.refs_6_), channel_id=1, source_target_pairs={{0,1},{1,0},{2,3},{3,2},{4,5},{5,4},{6,7},{7,6},{8,15},{9,10},{10,... | collective-permute-start | bytes 786440 | tf_op jit(solution)/shard_map/ppermute | solution.py:346
  27.3 8.4 %collective-permute-start.7 = (bf16[2,2,4,2,2,32,128]{6,5,4,3,2,1,0:T(8,128)(2,1)S(1)}, bf16[2,2,4,2,2,32,128]{6,5,4,3,2,1,0:T(8,128)(2,1)S(1)}, u32[]{:S(2)}, u32[]{:S(2)}) collective-permute-start(bf16[2,2,4,2,2,32,128]{6,5,4,3,2,1,0:T(8,128)(2,1)S(1)} %pad_maximum_fusion), channel_id=1, source_target_pairs={{0,7},{1,2},{2,1},{3,4},{4,3},{5,6},{6,5},{7,0},{8,9},{9,8},{10,11... | collective-permute-start | bytes 1572872 | tf_op jit(solution)/shard_map/ppermute | solution.py:346
  27.4 5.1 %collective-permute-start.8 = (bf16[32,3072]{1,0:T(8,128)(2,1)}, bf16[32,3072]{1,0:T(8,128)(2,1)S(1)}, u32[]{:S(2)}, u32[]{:S(2)}) collective-permute-start(bf16[32,3072]{1,0:T(8,128)(2,1)} %get-tuple-element.65), channel_id=1, source_target_pairs={{0,16},{8,24},{16,0},{24,8},{32,48},{40,56},{48,32},{56,40},{64,80... | collective-permute-start | bytes 589832 | tf_op jit(solution)/shard_map/ppermute | solution.py:337
  35.7 9.7 %collective-permute-start.9 = (bf16[2,2,4,2,2,32,128]{6,5,4,3,2,1,0:T(8,128)(2,1)S(1)}, bf16[2,2,4,2,2,32,128]{6,5,4,3,2,1,0:T(8,128)(2,1)S(1)}, u32[]{:S(2)}, u32[]{:S(2)}) collective-permute-start(bf16[2,2,4,2,2,32,128]{6,5,4,3,2,1,0:T(8,128)(2,1)S(1)} %collective-permute-done.7.refs_8_), channel_id=1, source_target_pairs={{0,1},{1,0},{2,3},{3,2},{4,5},{5,4},{6,7},{7,6},{8,15},{9,10},{10,... | collective-permute-start | bytes 1572872 | tf_op jit(solution)/shard_map/ppermute | solution.py:346
  38.4 7.0 %collective-permute-start.10 = (bf16[32,3072]{1,0:T(8,128)(2,1)}, bf16[32,3072]{1,0:T(8,128)(2,1)S(1)}, u32[]{:S(2)}, u32[]{:S(2)}) collective-permute-start(bf16[32,3072]{1,0:T(8,128)(2,1)} %get-tuple-element.68), channel_id=1, source_target_pairs={{0,24},{8,16},{16,8},{24,0},{32,56},{40,48},{48,40},{56,32},{64,88... | collective-permute-start | bytes 589832 | tf_op jit(solution)/shard_map/ppermute | solution.py:337
  45.4 14.8 %collective-permute-start.13 = (bf16[2,2,4,2,2,32,128]{6,5,4,3,2,1,0:T(8,128)(2,1)S(1)}, bf16[2,2,4,2,2,32,128]{6,5,4,3,2,1,0:T(8,128)(2,1)S(1)}, u32[]{:S(2)}, u32[]{:S(2)}) collective-permute-start(bf16[2,2,4,2,2,32,128]{6,5,4,3,2,1,0:T(8,128)(2,1)S(1)} %collective-permute-done.9.refs_9_), channel_id=1, source_target_pairs={{0,7},{1,2},{2,1},{3,4},{4,3},{5,6},{6,5},{7,0},{8,9},{9,8},{10,11... | collective-permute-start | bytes 1572872 | tf_op jit(solution)/shard_map/ppermute | solution.py:346
  45.8 6.7 %collective-permute-start.11 = (bf16[32,3072]{1,0:T(8,128)(2,1)}, bf16[32,3072]{1,0:T(8,128)(2,1)S(1)}, u32[]{:S(2)}, u32[]{:S(2)}) collective-permute-start(bf16[32,3072]{1,0:T(8,128)(2,1)} %get-tuple-element.71), channel_id=1, source_target_pairs={{0,16},{8,24},{16,0},{24,8},{32,48},{40,56},{48,32},{56,40},{64,80... | collective-permute-start | bytes 589832 | tf_op jit(solution)/shard_map/ppermute | solution.py:337
  47.3 12.9 %collective-permute-start.12 = (bf16[32,3072]{1,0:T(8,128)(2,1)S(1)}, bf16[32,3072]{1,0:T(8,128)(2,1)S(1)}, u32[]{:S(2)}, u32[]{:S(2)}) collective-permute-start(bf16[32,3072]{1,0:T(8,128)(2,1)S(1)} %copy-done.18), channel_id=1, source_target_pairs={{0,24},{8,16},{16,8},{24,0},{32,56},{40,48},{48,40},{56,32},{64,88... | collective-permute-start | bytes 589832 | tf_op jit(solution)/shard_map/ppermute | solution.py:337
  77.2 8.4 %collective-permute-start.14 = (bf16[2,2,4,2,2,32,128]{6,5,4,3,2,1,0:T(8,128)(2,1)S(1)}, bf16[2,2,4,2,2,32,128]{6,5,4,3,2,1,0:T(8,128)(2,1)S(1)}, u32[]{:S(2)}, u32[]{:S(2)}) collective-permute-start(bf16[2,2,4,2,2,32,128]{6,5,4,3,2,1,0:T(8,128)(2,1)S(1)} %get-tuple-element.77), channel_id=1, source_target_pairs={{0,7},{1,2},{2,1},{3,4},{4,3},{5,6},{6,5},{7,0},{8,9},{9,8},{10,11... | collective-permute-start | bytes 1572872 | tf_op jit(solution)/shard_map/ppermute | solution.py:346
  77.3 8.5 %collective-permute-start.15 = (bf16[32,3072]{1,0:T(8,128)(2,1)S(1)}, bf16[32,3072]{1,0:T(8,128)(2,1)S(1)}, u32[]{:S(2)}, u32[]{:S(2)}) collective-permute-start(bf16[32,3072]{1,0:T(8,128)(2,1)S(1)} %get-tuple-element.78), channel_id=1, source_target_pairs={{0,8},{8,0},{16,24},{24,16},{32,40},{40,32},{48,56},{56,48},{64,72... | collective-permute-start | bytes 589832 | tf_op jit(solution)/shard_map/ppermute | solution.py:337
  77.4 8.5 %collective-permute-start.16 = (bf16[32,3072]{1,0:T(8,128)(2,1)S(1)}, bf16[32,3072]{1,0:T(8,128)(2,1)S(1)}, u32[]{:S(2)}, u32[]{:S(2)}) collective-permute-start(bf16[32,3072]{1,0:T(8,128)(2,1)S(1)} %get-tuple-element.79), channel_id=1, source_target_pairs={{0,8},{8,0},{16,24},{24,16},{32,40},{40,32},{48,56},{56,48},{64,72... | collective-permute-start | bytes 589832 | tf_op jit(solution)/shard_map/ppermute | solution.py:337
  77.9 8.0 %collective-permute-start.17 = (bf16[32,3072]{1,0:T(8,128)(2,1)S(1)}, bf16[32,3072]{1,0:T(8,128)(2,1)S(1)}, u32[]{:S(2)}, u32[]{:S(2)}) collective-permute-start(bf16[32,3072]{1,0:T(8,128)(2,1)S(1)} %get-tuple-element.80), channel_id=1, source_target_pairs={{0,16},{8,24},{16,0},{24,8},{32,48},{40,56},{48,32},{56,40},{64,80... | collective-permute-start | bytes 589832 | tf_op jit(solution)/shard_map/ppermute | solution.py:337
  85.9 9.3 %collective-permute-start.18 = (bf16[2,2,4,2,2,32,128]{6,5,4,3,2,1,0:T(8,128)(2,1)S(1)}, bf16[2,2,4,2,2,32,128]{6,5,4,3,2,1,0:T(8,128)(2,1)S(1)}, u32[]{:S(2)}, u32[]{:S(2)}) collective-permute-start(bf16[2,2,4,2,2,32,128]{6,5,4,3,2,1,0:T(8,128)(2,1)S(1)} %add_convert_fusion.1), channel_id=1, source_target_pairs={{0,1},{1,0},{2,3},{3,2},{4,5},{5,4},{6,7},{7,6},{8,15},{9,10},{10,... | collective-permute-start | bytes 1572872 | tf_op jit(solution)/shard_map/ppermute | solution.py:346
  86.0 9.5 %collective-permute-start.19 = (bf16[32,3072]{1,0:T(8,128)(2,1)S(1)}, bf16[32,3072]{1,0:T(8,128)(2,1)S(1)}, u32[]{:S(2)}, u32[]{:S(2)}) collective-permute-start(bf16[32,3072]{1,0:T(8,128)(2,1)S(1)} %get-tuple-element.87), channel_id=1, source_target_pairs={{0,24},{8,16},{16,8},{24,0},{32,56},{40,48},{48,40},{56,32},{64,88... | collective-permute-start | bytes 589832 | tf_op jit(solution)/shard_map/ppermute | solution.py:337
  95.5 8.4 %collective-permute-start.20 = (bf16[2,2,4,2,2,32,128]{6,5,4,3,2,1,0:T(8,128)(2,1)S(1)}, bf16[2,2,4,2,2,32,128]{6,5,4,3,2,1,0:T(8,128)(2,1)S(1)}, u32[]{:S(2)}, u32[]{:S(2)}) collective-permute-start(bf16[2,2,4,2,2,32,128]{6,5,4,3,2,1,0:T(8,128)(2,1)S(1)} %add_convert_fusion), channel_id=1, source_target_pairs={{0,7},{1,2},{2,1},{3,4},{4,3},{5,6},{6,5},{7,0},{8,9},{9,8},{10,11... | collective-permute-start | bytes 1572872 | tf_op jit(solution)/shard_map/ppermute | solution.py:346
  95.6 8.4 %collective-permute-start.21 = (bf16[32,3072]{1,0:T(8,128)(2,1)S(1)}, bf16[32,3072]{1,0:T(8,128)(2,1)S(1)}, u32[]{:S(2)}, u32[]{:S(2)}) collective-permute-start(bf16[32,3072]{1,0:T(8,128)(2,1)S(1)} %get-tuple-element.89), channel_id=1, source_target_pairs={{0,16},{8,24},{16,0},{24,8},{32,48},{40,56},{48,32},{56,40},{64,80... | collective-permute-start | bytes 589832 | tf_op jit(solution)/shard_map/ppermute | solution.py:337
  104.0 6.5 %collective-permute-start.22 = (bf16[2,4,2,2,32,128]{5,4,3,2,1,0:T(8,128)(2,1)S(1)}, bf16[2,4,2,2,32,128]{5,4,3,2,1,0:T(8,128)(2,1)S(1)}, u32[]{:S(2)}, u32[]{:S(2)}) collective-permute-start(bf16[2,4,2,2,32,128]{5,4,3,2,1,0:T(8,128)(2,1)S(1)} %fusion), channel_id=1, source_target_pairs={{0,1},{1,0},{2,3},{3,2},{4,5},{5,4},{6,7},{7,6},{8,15},{9,10},{10,... | collective-permute-start | bytes 786440 | tf_op jit(solution)/shard_map/ppermute | solution.py:346
  104.1 9.5 %collective-permute-start.23 = (bf16[32,3072]{1,0:T(8,128)(2,1)S(1)}, bf16[32,3072]{1,0:T(8,128)(2,1)S(1)}, u32[]{:S(2)}, u32[]{:S(2)}) collective-permute-start(bf16[32,3072]{1,0:T(8,128)(2,1)S(1)} %get-tuple-element.93), channel_id=1, source_target_pairs={{0,24},{8,16},{16,8},{24,0},{32,56},{40,48},{48,40},{56,32},{64,88... | collective-permute-start | bytes 589832 | tf_op jit(solution)/shard_map/ppermute | solution.py:337
  113.6 8.7 %collective-permute-start.24 = (bf16[4,2,2,32,128]{4,3,2,1,0:T(8,128)(2,1)S(1)}, bf16[4,2,2,32,128]{4,3,2,1,0:T(8,128)(2,1)S(1)}, u32[]{:S(2)}, u32[]{:S(2)}) collective-permute-start(bf16[4,2,2,32,128]{4,3,2,1,0:T(8,128)(2,1)S(1)} %fusion.3), channel_id=1, source_target_pairs={{32,0},{40,8},{48,16},{56,24},{64,32},{72,40},{80,48},{88,56},{96,... | collective-permute-start | bytes 393224 | tf_op jit(solution)/shard_map/ppermute | solution.py:360
  (23 other events, 383.0 us)

commit v3 on v2

v3 whole, which is shorter than its diff:
```python
import functools

import jax
import jax.numpy as jnp
from jax import lax
from jax.experimental import pallas as pl
from jax.experimental.pallas import tpu as pltpu
from jax.sharding import PartitionSpec as P

HD = 128
QPK = 12
TB = 32
GROUP = 4
ROWS = QPK * TB
CHUNK = 256
SCALE = HD ** (-0.5)
LOG2E = 1.4426950408889634
NEG = -1e30
GATHERED = (0, 1, -1, -2, 2, 3, -3, 4)
ARRIVALS = (
    ((0, 0, 0, 1),),
    ((1, 0, 0, 1),),
    ((1, 0, 1, 1),),
    ((1, 0, 2, 2), (0, 2, 1, 1)),
    ((1, 0, 4, 2), (0, 2, 2, 2)),
    ((1, 0, 6, 2), (0, 2, 4, 2)),
    ((0, 0, 6, 2),),
)
HW = 2 * QPK * HD
KW = 2 * HD

ANY = pl.BlockSpec(memory_space=pl.ANY)
SMEM = pl.BlockSpec(memory_space=pltpu.SMEM)
VMEM = pl.BlockSpec(memory_space=pltpu.VMEM)
TN = (((0,), (0,)), ((), ()))
NN = (((1,), (0,)), ((), ()))


def bf16(*shape):
    return jax.ShapeDtypeStruct(shape, jnp.bfloat16)


def columns(start, width):
    return pl.ds(pl.multiple_of(start, 128), width)


def run_copies(copies):
    for copy in copies:
        copy.start()
    for copy in copies:
        copy.wait()


def split_kv_body(meta, keys, values, *refs):
    outs, sem = refs[:GROUP], refs[GROUP]
    group_at = meta[0]
    copies = []
    for d in range(GROUP):
        for n, source in enumerate((keys, values)):
            for head in range(2):
                at = (group_at ^ d) * KW + head * HD
                copies.append(
                    pltpu.make_async_copy(
                        source.at[:, columns(at, HD)], outs[d].at[n, head], sem.at[len(copies)]
                    )
                )
    run_copies(copies)


def split_kv(meta, keys, values):
    return pl.pallas_call(
        split_kv_body,
        in_specs=[SMEM, ANY, ANY],
        out_specs=[VMEM] * GROUP,
        out_shape=[bf16(2, 2, TB, HD)] * GROUP,
        scratch_shapes=[pltpu.SemaphoreType.DMA((4 * GROUP,))],
    )(meta, keys, values)


def split_queries_body(meta, queries, grads, *refs):
    outs, sem = refs[: 2 * (GROUP - 1)], refs[2 * (GROUP - 1)]
    group_at = meta[0]
    copies = []
    for d in range(1, GROUP):
        for n, source in enumerate((queries, grads)):
            copies.append(
                pltpu.make_async_copy(
                    source.at[:, columns((group_at ^ d) * HW, HW)],
                    outs[n * (GROUP - 1) + d - 1],
                    sem.at[len(copies)],
                )
            )
    run_copies(copies)


def split_queries(meta, queries, grads):
    return pl.pallas_call(
        split_queries_body,
        in_specs=[SMEM, ANY, ANY],
        out_specs=[VMEM] * (2 * (GROUP - 1)),
        out_shape=[bf16(TB, HW)] * (2 * (GROUP - 1)),
        scratch_shapes=[pltpu.SemaphoreType.DMA((2 * GROUP,))],
    )(meta, queries, grads)


def attention_body(meta, doc_starts, doc_tenant, tenant_weight, queries, grads, *refs):
    sent, refs = refs[:6], refs[6:]
    gathered, refs = refs[:7], refs[7:]
    partials, refs = refs[:8], refs[8:]
    outs, refs = refs[:8], refs[8:]
    kv, acc_k, acc_v, scores, head_q, head_w, head_qt, head_wn = (refs[0],) + tuple(
        refs[1 + 2 * i : 3 + 2 * i] for i in range(7)
    )
    qs, gs, wide, sem_kv, sem_q, sem_out = refs[15:]
    group_at, z_at, pair_at = meta[0], meta[1], meta[2]
    n_docs = doc_starts.shape[0]
    side = (1 - 2 * (z_at & 1)) * (1 - 2 * (group_at & 1))

    copies = []
    for n, part in enumerate(gathered):
        for chain, source, target, blocks in ARRIVALS[n]:
            copies.append(
                pltpu.make_async_copy(
                    part.at[pl.ds(source, blocks)], kv.at[chain, pl.ds(target, blocks)], sem_kv
                )
            )
    own = columns(group_at * HW, HW)
    copies += [
        pltpu.make_async_copy(queries.at[:, own], qs.at[0], sem_q),
        pltpu.make_async_copy(grads.at[:, own], gs.at[0], sem_q),
    ]
    for d in range(3):
        copies.append(pltpu.make_async_copy(sent[d], qs.at[d + 1], sem_q))
        copies.append(pltpu.make_async_copy(sent[3 + d], gs.at[d + 1], sem_q))
    kv_copies = len(copies) - 8
    for copy in copies[kv_copies:] + copies[:kv_copies]:
        copy.start()
    for h in range(2):
        acc_k[h][...] = jnp.zeros_like(acc_k[h])
        acc_v[h][...] = jnp.zeros_like(acc_v[h])
    for copy in copies[kv_copies:]:
        copy.wait()

    def dot(a, b, dims):
        return lax.dot_general(a, b, dims, preferred_element_type=jnp.float32)

    def flip(x):
        return jnp.concatenate(
            [x[:, i * 128 : (i + 1) * 128].T for i in range(x.shape[1] // 128)], axis=0
        )

    def flip_back(x):
        return jnp.concatenate(
            [x[i * 128 : (i + 1) * 128].T for i in range(x.shape[0] // 128)], axis=1
        )

    def head_columns(h, m):
        return slice((h * QPK + m) * HD, (h * QPK + m + 1) * HD)

    for d in range(4):
        token = 1024 * pair_at + CHUNK * (group_at ^ d) + TB * z_at
        token = token + lax.broadcasted_iota(jnp.int32, (TB, HD), 0)
        scaling = jnp.zeros((TB, HD), jnp.float32)
        for n in range(n_docs):
            scaling = jnp.where(doc_starts[n] <= token, tenant_weight[doc_tenant[n]], scaling)
        for h in range(2):
            raw = [qs[d, :, head_columns(h, m)] for m in range(QPK)]
            head_q[h][d] = jnp.concatenate(raw, axis=0)
            head_qt[h][d] = flip_back(jnp.concatenate(raw, axis=0))
            raw = [gs[d, :, head_columns(h, m)].astype(jnp.float32) * scaling for m in range(QPK)]
            raw = jnp.concatenate([part.astype(jnp.bfloat16) for part in raw], axis=0)
            head_wn[h][d] = raw
            head_w[h][d] = flip_back(raw)
    for copy in copies[:kv_copies]:
        copy.wait()

    window_at = 1024 * (pair_at - 1)
    c_scale = SCALE * LOG2E

    def block(d, carry):
        sub = group_at ^ d
        first = 1024 * pair_at + CHUNK * sub + TB * z_at
        lowest = jnp.int32(0)
        for n in range(n_docs):
            lowest = jnp.where(doc_starts[n] <= first, doc_starts[n], lowest)
        chunk_lo = jnp.maximum((lowest - window_at) >> 8, 0)
        chunk_hi = 4 + sub + 1
        lane = lax.broadcasted_iota(jnp.int32, (1, 128), 1)
        token = first + (lane & (TB - 1))
        start = jnp.zeros((1, 128), jnp.int32)
        for n in range(n_docs):
            inside = doc_starts[n] <= token
            start = jnp.where(inside, doc_starts[n], start)

        def first_pass(c, tops):
            base = window_at + c * CHUNK
            row = lax.broadcasted_iota(jnp.int32, (TB, 128), 0)
            bias = []
            turn = jnp.where(c < 4, -side, side)
            for off in GATHERED:
                key = base + TB * ((z_at + turn * off + 8) & 7) + row
                bias.append(jnp.where((key >= start) & (key <= token), 0.0, NEG))
            bias = jnp.concatenate(bias, axis=0)
            bias = jnp.concatenate([bias] * 3, axis=1)
            new = []
            for h in range(2):
                k = kv[c >> 2, :, (c & 3) ^ group_at, 0, h].reshape(CHUNK, HD)
                s = dot(k, head_qt[h][d], NN) + bias
                scores[h][c] = s
                new.append(jnp.maximum(tops[h], jnp.max(s.reshape(CHUNK // 8, 8, ROWS), axis=0)))
            return tuple(new)

        held = ([], [])

        def joined(held):
            totals = []
            for one in held:
                left, right = (jnp.concatenate(part, axis=0) for part in zip(*one))
                totals.append(dot(left, right, TN))
                one.clear()
            return totals

        def work(chunks):
            def static_loop(f, carry):
                for i in range(chunks):
                    carry = f(chunk_lo + i, carry)
                return carry

            top = jnp.full((8, ROWS), NEG, jnp.float32)
            tops = static_loop(first_pass, (top, top))
            tops = [jnp.max(t, axis=0, keepdims=True) for t in tops]

            for h in range(2):
                held[h].clear()

            def second_pass(c, sums):
                new = []
                for h in range(2):
                    p = jnp.exp2((scores[h][c] - tops[h]) * c_scale)
                    scores[h][c] = p
                    new.append(sums[h] + jnp.sum(p.reshape(CHUNK // 8, 8, ROWS), axis=0))
                    v = kv[c >> 2, :, (c & 3) ^ group_at, 1, h].reshape(CHUNK, HD)
                    held[h].append((v, p.astype(jnp.bfloat16)))
                return tuple(new)

            zero = jnp.zeros((8, ROWS), jnp.float32)
            sums = static_loop(second_pass, (zero, zero))
            attended = joined(held)
            inverse = [1.0 / jnp.sum(s, axis=0, keepdims=True) for s in sums]
            deltas = []
            for h in range(2):
                rounded = (attended[h] * inverse[h]).astype(jnp.bfloat16)
                product = rounded.astype(jnp.float32) * head_w[h][d].astype(jnp.float32)
                deltas.append(jnp.sum(product, axis=0, keepdims=True))
                out = flip(rounded).astype(jnp.bfloat16)
                for m in range(QPK):
                    wide[d, 0, :, head_columns(h, m)] = out[m * TB : (m + 1) * TB]

            def third_pass(c, carry):
                for h in range(2):
                    k = kv[c >> 2, :, (c & 3) ^ group_at, 0, h].reshape(CHUNK, HD)
                    v = kv[c >> 2, :, (c & 3) ^ group_at, 1, h].reshape(CHUNK, HD)
                    p = scores[h][c] * inverse[h]
                    push = dot(v, head_w[h][d], NN)
                    ds = (p * (push - deltas[h])).astype(jnp.bfloat16)
                    at = (c >> 2, slice(None), (c & 3) ^ group_at)
                    acc_v[h][at] += dot(p.astype(jnp.bfloat16), head_wn[h][d], NN).reshape(8, TB, HD)
                    acc_k[h][at] += dot(ds, head_q[h][d], NN).reshape(8, TB, HD)
                    held[h].append((k, ds))
                return carry

            static_loop(third_pass, 0)
            query = joined(held)
            for h in range(2):
                out = flip((query[h] * SCALE).astype(jnp.bfloat16)).astype(jnp.bfloat16)
                for m in range(QPK):
                    wide[d, 1, :, head_columns(h, m)] = out[m * TB : (m + 1) * TB]

        for chunks in range(1, 6):
            pl.when(chunk_hi - chunk_lo == chunks)(functools.partial(work, chunks))
        for n in range(4):

            @pl.when(d == n)
            def _():
                for i in range(2):
                    pltpu.make_async_copy(wide.at[n, i], outs[2 * n + i], sem_out).start()

        return carry

    lax.fori_loop(0, 4, block, 0)

    for chain in range(2):
        for at in range(8):
            target = partials[chain * 4 + at // 2]
            for h in range(2):
                target[at % 2, :, 0, h] = (acc_k[h][chain, at] * SCALE).astype(jnp.bfloat16)
                target[at % 2, :, 1, h] = acc_v[h][chain, at].astype(jnp.bfloat16)
    for n in range(4):
        for i in range(2):
            pltpu.make_async_copy(wide.at[n, i], outs[2 * n + i], sem_out).wait()


def attention(meta, doc_starts, doc_tenant, tenant_weight, queries, grads, sent, gathered):
    def vmem(dtype, *shape):
        return pltpu.VMEM(shape, dtype)

    part = bf16(2, 4, 2, 2, TB, HD)
    return pl.pallas_call(
        attention_body,
        in_specs=[SMEM] * 4 + [ANY] * 2 + [VMEM] * 13,
        out_specs=[VMEM] * 16,
        out_shape=[part] * 8 + [bf16(TB, HW)] * 8,
        scratch_shapes=[vmem(jnp.bfloat16, 2, 8, 4, 2, 2, TB, HD)]
        + [vmem(jnp.float32, 2, 8, 4, TB, HD)] * 4
        + [vmem(jnp.float32, 8, CHUNK, ROWS)] * 2
        + [vmem(jnp.bfloat16, 4, ROWS, HD)] * 2
        + [vmem(jnp.bfloat16, 4, HD, ROWS)] * 4
        + [vmem(jnp.bfloat16, 4, ROWS, HD)] * 2
        + [vmem(jnp.bfloat16, 4, TB, HW)] * 2
        + [vmem(jnp.bfloat16, 4, 2, TB, HW)]
        + [pltpu.SemaphoreType.DMA] * 3,
        compiler_params=pltpu.CompilerParams(vmem_limit_bytes=40 * 1024 * 1024),
        cost_estimate=pl.CostEstimate(flops=3 * 10**9, bytes_accessed=10**7, transcendentals=10**6),
    )(meta, doc_starts, doc_tenant, tenant_weight, queries, grads, *sent, *gathered)


def join_wide_body(meta, *refs):
    ins, outs, sem = refs[: 2 * GROUP], refs[2 * GROUP : 2 * GROUP + 2], refs[2 * GROUP + 2]
    group_at = meta[0]
    copies = []
    for d in range(GROUP):
        for n, target in enumerate(outs):
            target = target.at[:, columns((group_at ^ d) * HW, HW)]
            copies.append(pltpu.make_async_copy(ins[2 * d + n], target, sem.at[len(copies)]))
    run_copies(copies)


def join_wide(meta, pieces):
    return pl.pallas_call(
        join_wide_body,
        in_specs=[SMEM] + [VMEM] * (2 * GROUP),
        out_specs=[ANY] * 2,
        out_shape=[bf16(TB, 96 * HD)] * 2,
        scratch_shapes=[pltpu.SemaphoreType.DMA((2 * GROUP,))],
    )(meta, *pieces)


def join_narrow_body(meta, *refs):
    ins, outs = refs[:GROUP], refs[GROUP:]
    group_at = meta[0]
    for d in range(GROUP):
        for n, target in enumerate(outs):
            for head in range(2):
                target[:, columns((group_at ^ d) * KW + head * HD, HD)] = ins[d][n, head]


def join_narrow(meta, pieces):
    return pl.pallas_call(
        join_narrow_body,
        in_specs=[SMEM] + [VMEM] * GROUP,
        out_specs=[VMEM] * 2,
        out_shape=[bf16(TB, 8 * HD)] * 2,
    )(meta, *pieces)


def swap_in_group(x, d):
    return lax.ppermute(x, "ctx", [(i, i ^ d) for i in range(lax.axis_size("ctx"))])


def swap_on_z(x, phase):
    pairs = []
    for i in range(lax.axis_size("ctx")):
        for z in range(8):
            up = (z + phase + i) % 2 == 0
            pairs.append((8 * i + z, 8 * i + (z + 1 if up else z - 1) % 8))
    return lax.ppermute(x, ("ctx", "hg"), pairs)


def arrived(x, *beside):
    return lax.optimization_barrier((x, *beside))


def add(a, b):
    return (a.astype(jnp.float32) + b.astype(jnp.float32)).astype(jnp.bfloat16)


def shift_pairs(x, by):
    devices = lax.axis_size("ctx")
    pairs = [(i, i + by) for i in range(devices) if 0 <= i + by < devices]
    return lax.ppermute(x, "ctx", pairs)


def local(query_states, key_states, value_states, out_grad, doc_starts, doc_tenant, tenant_weight):
    ctx_at = lax.axis_index("ctx")
    z_at = lax.axis_index("hg")
    meta = jnp.stack([ctx_at & 3, z_at, ctx_at >> 2]).astype(jnp.int32)

    kv = split_kv(meta, key_states, value_states)
    own = jnp.stack([kv[0]] + [swap_in_group(kv[d], d) for d in range(1, GROUP)])
    sent = split_queries(meta, query_states, out_grad)
    own, sent = lax.optimization_barrier((own, sent))
    q1, q2, q3, g1, g2, g3 = [swap_in_group(x, i % 3 + 1) for i, x in enumerate(sent)]
    own = own[None]
    earlier = shift_pairs(own, GROUP)
    first = swap_on_z(own, 0)
    message, q1, g1 = arrived(jnp.concatenate([own, first, earlier]), q1, g1)
    second = swap_on_z(message, 1)
    message, q2 = arrived(jnp.concatenate([second[:2], earlier, second[2:]]), q2)
    third = swap_on_z(message, 0)
    third, q3 = arrived(third, q3)
    fourth = swap_on_z(third, 1)
    fourth, g2 = arrived(fourth, g2)
    fifth = swap_on_z(fourth[2:], 0)

    results = attention(
        meta,
        doc_starts,
        doc_tenant,
        tenant_weight,
        query_states,
        out_grad,
        (q1, q2, q3, g1, g2, g3),
        (earlier, own, first, second, third, fourth, fifth),
    )
    before, parts, wide = results[:4], results[4:8], list(results[8:])

    for d in range(1, GROUP):
        for i in range(2):
            wide[2 * d + i] = swap_in_group(wide[2 * d + i], d)
    moved = swap_on_z(before[3], 0)
    moved, wide[2], wide[3] = arrived(
        jnp.concatenate([parts[3], add(before[2], moved)]), wide[2], wide[3]
    )
    moved = swap_on_z(moved, 1)
    moved = jnp.concatenate([add(parts[2], moved[:2]), add(before[1], moved[2:])])
    moved, wide[4], wide[6] = arrived(moved, wide[4], wide[6])
    moved = swap_on_z(moved, 0)
    kept = before[0][0].astype(jnp.float32) + moved[2].astype(jnp.float32)
    moved = jnp.concatenate([add(parts[1], moved[:2]), add(before[0][1:], moved[3:])])
    moved, wide[5] = arrived(moved, wide[5])
    moved = swap_on_z(moved, 1)
    earlier_sum = (kept + moved[2].astype(jnp.float32)).astype(jnp.bfloat16)
    kept = parts[0][0].astype(jnp.float32) + moved[0].astype(jnp.float32)
    moved, earlier_sum, wide[7] = arrived(add(parts[0][1], moved[1]), earlier_sum, wide[7])
    moved = swap_on_z(moved, 0)
    earlier_sum = shift_pairs(earlier_sum, -GROUP)
    total = kept + moved.astype(jnp.float32) + earlier_sum.astype(jnp.float32)
    total, *wide = arrived(total.astype(jnp.bfloat16), *join_wide(meta, wide))
    narrow = [total[0]] + [swap_in_group(total[d], d) for d in range(1, GROUP)]
    return tuple(wide) + tuple(join_narrow(meta, narrow))


def solution(mesh):
    row = P(("ctx", "hg"), None)
    return jax.shard_map(
        local,
        mesh=mesh,
        in_specs=(row, row, row, row, P(), P(), P()),
        out_specs=(row, row, row, row),
        check_vma=False,
    )
```

time: 133 us -> 129 us (0.970); the launches traced: 132 us -> 126 us
  waiting for transfers between devices: 66.3 us -> 57.6 us
  starting transfers between devices: 36.2 us -> 39.4 us
    ppermute x8 -> x10, starting transfers between devices: 9.17 us -> 16.5 us  [swap_on_z(): return lax.ppermute(x, ('ctx', 'hg'), pairs)]
    ppermute x2, waiting for transfers between devices: 10.7 us -> 4.73 us  [shift_pairs(): return lax.ppermute(x, 'ctx', pairs)]
    ppermute x18, starting transfers between devices: 21.2 us -> 16.9 us  [swap_in_group(): lax.ppermute(x, 'ctx', [(i, i ^ d) for i in range(lax.axis_size('ctx'))])]
    ppermute x18, waiting for transfers between devices: 24 us -> 21.2 us  [swap_in_group(): lax.ppermute(x, 'ctx', [(i, i ^ d) for i in range(lax.axis_size('ctx'))])]
    pallas_call x1 -> x2, Pallas kernels: 2.88 us -> 4.17 us  [the longest x1 2.67 us: join_wide(): pl.pallas_call(join_wide_body, in_specs=[SMEM] + [VMEM] * (2 * GROUP), ou...]
    ppermute x8 -> x10, waiting for transfers between devices: 31.6 us -> 31.7 us  [swap_on_z(): return lax.ppermute(x, ('ctx', 'hg'), pairs)]
  transfers between devices with their start and end apart: 28 -> 30, of which waited for: 14 -> 15; matrix products, arithmetic and copies ran while one was open for 0% -> 1% of each run, Pallas kernels for 2% -> 5%
where the time goes in v3:
time: 129 us; the launch traced here: 126 us
  waiting for transfers between devices  57.6 us (45%)
  starting transfers between devices  39.4 us (31%)
  Pallas kernels  25.2 us (20%)
  other arithmetic  1.43 us (1%)
  local copies, waits for them, and re-layouts  1.38 us (1%)
    ppermute x10, waiting for transfers between devices, swap_on_z(): return lax.ppermute(x, ('ctx', 'hg'), pairs)  31.7 us
    ppermute x18, waiting for transfers between devices, swap_in_group(): lax.ppermute(x, 'ctx', [(i, i ^ d) for i in range(lax.axis_size('ctx'))])  21.2 us
    ppermute x18, starting transfers between devices, swap_in_group(): lax.ppermute(x, 'ctx', [(i, i ^ d) for i in range(lax.axis_size('ctx'))])  16.9 us
    ppermute x10, starting transfers between devices, swap_on_z(): return lax.ppermute(x, ('ctx', 'hg'), pairs)  16.5 us
    pallas_call x1, Pallas kernels, attention(): pl.pallas_call(attention_body, in_specs=[SMEM] * 4 + [ANY] * 2 + [VMEM] *...  15.7 us
    ppermute x2, starting transfers between devices, shift_pairs(): return lax.ppermute(x, 'ctx', pairs)  6.03 us
    ppermute x2, waiting for transfers between devices, shift_pairs(): return lax.ppermute(x, 'ctx', pairs)  4.73 us
    pallas_call x1, Pallas kernels, split_queries(): pl.pallas_call(split_queries_body, in_specs=[SMEM, ANY, ANY], out_specs=[...  3.08 us
  transfers between devices with their start and end apart: 30, of which 15 were waited for; matrix products, arithmetic and copies ran while one was open for 1% of the time, Pallas kernels for 5%

profile of v3, /device:TPU:25, one launch (start us, length us, event | category | flops | bytes accessed | tf_op | source)
XLA Modules:
  0.0 126.2 jit_solution(7252599578054350928)
XLA Ops:
  1.2 2.3 %shard_map.102 = (bf16[2,2,32,128]{3,2,1,0:T(8,128)(2,1)}, bf16[2,2,32,128]{3,2,1,0:T(8,128)(2,1)}, bf16[2,2,32,128]{3,2,1,0:T(8,128)(2,1)}, bf16[2,2,32,128]{3,2,1,0:T(8,128)(2,1)}) custom-call(s32[3]{0:T(128)} %pad_add_fusion.meta, bf16[32,1024]{1,0:T(8,128)(2,1)} %keys.1, bf16[32,1024]{1,0:T(8,128)(2,1)} %values.1), custom_call_target="tpu_custom_call" | custom-call | tf_op jit(solution)/shard_map/pallas_call | solution.py:71
  6.0 3.1 %shard_map.103 = (bf16[32,3072]{1,0:T(8,128)(2,1)}, bf16[32,3072]{1,0:T(8,128)(2,1)}, bf16[32,3072]{1,0:T(8,128)(2,1)}, bf16[32,3072]{1,0:T(8,128)(2,1)}, bf16[3...) custom-call(s32[3]{0:T(128)} %pad_add_fusion.meta, bf16[32,12288]{1,0:T(8,128)(2,1)} %queries.3, bf16[32,12288]{1,0:T(8,128)(2,1)} %grads.3), custom_call_target="tpu_custom_call" | custom-call | tf_op jit(solution)/shard_map/pallas_call | solution.py:97
  9.2 3.9 %collective-permute-start.4 = (bf16[1,4,2,2,32,128]{5,4,3,2,1,0:T(8,128)(2,1)S(1)}, bf16[1,4,2,2,32,128]{5,4,3,2,1,0:T(8,128)(2,1)S(1)}, u32[]{:S(2)}, u32[]{:S(2)}) collective-permute-start(bf16[1,4,2,2,32,128]{5,4,3,2,1,0:T(8,128)(2,1)S(1)} %bitcast.26), channel_id=1, source_target_pairs={{0,32},{8,40},{16,48},{24,56},{32,64},{40,72},{48,80},{56,88},{64,... | collective-permute-start | bytes 393224 | tf_op jit(solution)/shard_map/ppermute | solution.py:390
  13.2 5.7 %collective-permute-start.3 = (bf16[1,4,2,2,32,128]{5,4,3,2,1,0:T(8,128)(2,1)S(1)}, bf16[1,4,2,2,32,128]{5,4,3,2,1,0:T(8,128)(2,1)S(1)}, u32[]{:S(2)}, u32[]{:S(2)}) collective-permute-start(bf16[1,4,2,2,32,128]{5,4,3,2,1,0:T(8,128)(2,1)S(1)} %bitcast.27), channel_id=1, source_target_pairs={{0,1},{1,0},{2,3},{3,2},{4,5},{5,4},{6,7},{7,6},{8,15},{9,10},{10,... | collective-permute-start | bytes 393224 | tf_op jit(solution)/shard_map/ppermute | solution.py:376
  19.3 1.8 %collective-permute-done.3.refs_8_ = bf16[1,4,2,2,32,128]{5,4,3,2,1,0:T(8,128)(2,1)S(1)} collective-permute-done((bf16[1,4,2,2,32,128]{5,4,3,2,1,0:T(8,128)(2,1)S(1)}, bf16[1,4,2,2,32,128]{5,4,3,2,1,0:T(8,128)(2,1)S(1)}, u32[]{:S(2)}, u32[]{:S(2)}) %collective-permute-start.3) | collective-permute-done | bytes 131104 | tf_op jit(solution)/shard_map/ppermute | solution.py:376
  21.5 6.8 %collective-permute-done.7.refs_9_ = bf16[3,4,2,2,32,128]{5,4,3,2,1,0:T(8,128)(2,1)S(1)} collective-permute-done((bf16[3,4,2,2,32,128]{5,4,3,2,1,0:T(8,128)(2,1)S(1)}, bf16[3,4,2,2,32,128]{5,4,3,2,1,0:T(8,128)(2,1)S(1)}, u32[]{:S(2)}, u32[]{:S(2)}) %collective-permute-start.7) | collective-permute-done | bytes 393248 | tf_op jit(solution)/shard_map/ppermute | solution.py:376
  28.5 2.8 %collective-permute-start.9 = (bf16[4,4,2,2,32,128]{5,4,3,2,1,0:T(8,128)(2,1)S(1)}, bf16[4,4,2,2,32,128]{5,4,3,2,1,0:T(8,128)(2,1)S(1)}, u32[]{:S(2)}, u32[]{:S(2)}) collective-permute-start(bf16[4,4,2,2,32,128]{5,4,3,2,1,0:T(8,128)(2,1)S(1)} %pad_maximum_fusion), channel_id=1, source_target_pairs={{0,1},{1,0},{2,3},{3,2},{4,5},{5,4},{6,7},{7,6},{8,15},{9,10},{10,... | collective-permute-start | bytes 1572872 | tf_op jit(solution)/shard_map/ppermute | solution.py:376
  31.7 6.5 %collective-permute-done.10.refs_2_ = bf16[32,3072]{1,0:T(8,128)(2,1)S(1)} collective-permute-done((bf16[32,3072]{1,0:T(8,128)(2,1)S(1)}, bf16[32,3072]{1,0:T(8,128)(2,1)S(1)}, u32[]{:S(2)}, u32[]{:S(2)}) %collective-permute-start.10) | collective-permute-done | bytes 196640 | tf_op jit(solution)/shard_map/ppermute | solution.py:367
  39.4 3.4 %collective-permute-done.12.refs_4_ = bf16[32,3072]{1,0:T(8,128)(2,1)S(1)} collective-permute-done((bf16[32,3072]{1,0:T(8,128)(2,1)S(1)}, bf16[32,3072]{1,0:T(8,128)(2,1)S(1)}, u32[]{:S(2)}, u32[]{:S(2)}) %collective-permute-start.12) | collective-permute-done | bytes 196640 | tf_op jit(solution)/shard_map/ppermute | solution.py:367
  42.8 3.7 %collective-permute-done.11.refs_11_ = bf16[4,4,2,2,32,128]{5,4,3,2,1,0:T(8,128)(2,1)S(1)} collective-permute-done((bf16[4,4,2,2,32,128]{5,4,3,2,1,0:T(8,128)(2,1)S(1)}, bf16[4,4,2,2,32,128]{5,4,3,2,1,0:T(8,128)(2,1)S(1)}, u32[]{:S(2)}, u32[]{:S(2)}) %collective-permute-start.11) | collective-permute-done | bytes 524320 | tf_op jit(solution)/shard_map/ppermute | solution.py:376
  46.5 2.4 %collective-permute-start.14 = (bf16[2,4,2,2,32,128]{5,4,3,2,1,0:T(8,128)(2,1)S(1)}, bf16[2,4,2,2,32,128]{5,4,3,2,1,0:T(8,128)(2,1)S(1)}, u32[]{:S(2)}, u32[]{:S(2)}) collective-permute-start(bf16[2,4,2,2,32,128]{5,4,3,2,1,0:T(8,128)(2,1)S(1)} %slice.59), channel_id=1, source_target_pairs={{0,1},{1,0},{2,3},{3,2},{4,5},{5,4},{6,7},{7,6},{8,15},{9,10},{10,... | collective-permute-start | bytes 786440 | tf_op jit(solution)/shard_map/ppermute | solution.py:376
  48.9 2.0 %collective-permute-start.13 = (bf16[32,3072]{1,0:T(8,128)(2,1)S(1)}, bf16[32,3072]{1,0:T(8,128)(2,1)S(1)}, u32[]{:S(2)}, u32[]{:S(2)}) collective-permute-start(bf16[32,3072]{1,0:T(8,128)(2,1)S(1)} %copy-done.18), channel_id=1, source_target_pairs={{0,24},{8,16},{16,8},{24,0},{32,56},{40,48},{48,40},{56,32},{64,88... | collective-permute-start | bytes 589832 | tf_op jit(solution)/shard_map/ppermute | solution.py:367
  50.9 5.1 %collective-permute-done.13.refs_5_ = bf16[32,3072]{1,0:T(8,128)(2,1)S(1)} collective-permute-done((bf16[32,3072]{1,0:T(8,128)(2,1)S(1)}, bf16[32,3072]{1,0:T(8,128)(2,1)S(1)}, u32[]{:S(2)}, u32[]{:S(2)}) %collective-permute-start.13) | collective-permute-done | bytes 196640 | tf_op jit(solution)/shard_map/ppermute | solution.py:367
  56.0 15.7 %shard_map.104 = (bf16[2,4,2,2,32,128]{5,4,3,2,1,0:T(8,128)(2,1)S(1)}, bf16[2,4,2,2,32,128]{5,4,3,2,1,0:T(8,128)(2,1)S(1)}, bf16[2,4,2,2,32,128]{5,4,3,2,1,0:T(8...) custom-call(s32[3]{0:T(128)S(1)} %copy-done.4, ...), custom_call_target="tpu_custom_call" | custom-call | flops 3000000000 | bytes 10000000 | tf_op jit(solution)/shard_map/pallas_call | solution.py:308
  72.7 2.1 %collective-permute-start.16 = (bf16[32,3072]{1,0:T(8,128)(2,1)S(1)}, bf16[32,3072]{1,0:T(8,128)(2,1)S(1)}, u32[]{:S(2)}, u32[]{:S(2)}) collective-permute-start(bf16[32,3072]{1,0:T(8,128)(2,1)S(1)} %get-tuple-element.96), channel_id=1, source_target_pairs={{0,8},{8,0},{16,24},{24,16},{32,40},{40,32},{48,56},{56,48},{64,72... | collective-permute-start | bytes 589832 | tf_op jit(solution)/shard_map/ppermute | solution.py:367
  74.8 3.5 %collective-permute-done.15 = bf16[2,4,2,2,32,128]{5,4,3,2,1,0:T(8,128)(2,1)S(1)} collective-permute-done((bf16[2,4,2,2,32,128]{5,4,3,2,1,0:T(8,128)(2,1)S(1)}, bf16[2,4,2,2,32,128]{5,4,3,2,1,0:T(8,128)(2,1)S(1)}, u32[]{:S(2)}, u32[]{:S(2)}) %collective-permute-start.15) | collective-permute-done | bytes 262176 | tf_op jit(solution)/shard_map/ppermute | solution.py:376
  82.3 4.5 %collective-permute-done.18 = bf16[4,4,2,2,32,128]{5,4,3,2,1,0:T(8,128)(2,1)S(1)} collective-permute-done((bf16[4,4,2,2,32,128]{5,4,3,2,1,0:T(8,128)(2,1)S(1)}, bf16[4,4,2,2,32,128]{5,4,3,2,1,0:T(8,128)(2,1)S(1)}, u32[]{:S(2)}, u32[]{:S(2)}) %collective-permute-start.18) | collective-permute-done | bytes 524320 | tf_op jit(solution)/shard_map/ppermute | solution.py:376
  87.2 3.0 %collective-permute-done.20.refs_6_ = bf16[32,3072]{1,0:T(8,128)(2,1)S(1)} collective-permute-done((bf16[32,3072]{1,0:T(8,128)(2,1)S(1)}, bf16[32,3072]{1,0:T(8,128)(2,1)S(1)}, u32[]{:S(2)}, u32[]{:S(2)}) %collective-permute-start.20) | collective-permute-done | bytes 196640 | tf_op jit(solution)/shard_map/ppermute | solution.py:367
  92.7 6.7 %collective-permute-done.21 = bf16[4,4,2,2,32,128]{5,4,3,2,1,0:T(8,128)(2,1)S(1)} collective-permute-done((bf16[4,4,2,2,32,128]{5,4,3,2,1,0:T(8,128)(2,1)S(1)}, bf16[4,4,2,2,32,128]{5,4,3,2,1,0:T(8,128)(2,1)S(1)}, u32[]{:S(2)}, u32[]{:S(2)}) %collective-permute-start.21) | collective-permute-done | bytes 524320 | tf_op jit(solution)/shard_map/ppermute | solution.py:376
  100.0 1.9 %collective-permute-start.24 = (bf16[32,3072]{1,0:T(8,128)(2,1)S(1)}, bf16[32,3072]{1,0:T(8,128)(2,1)S(1)}, u32[]{:S(2)}, u32[]{:S(2)}) collective-permute-start(bf16[32,3072]{1,0:T(8,128)(2,1)S(1)} %get-tuple-element.106), channel_id=1, source_target_pairs={{0,24},{8,16},{16,8},{24,0},{32,56},{40,48},{48,40},{56,32},{64,88... | collective-permute-start | bytes 589832 | tf_op jit(solution)/shard_map/ppermute | solution.py:367
  101.9 4.7 %collective-permute-done.23 = bf16[3,4,2,2,32,128]{5,4,3,2,1,0:T(8,128)(2,1)S(1)} collective-permute-done((bf16[3,4,2,2,32,128]{5,4,3,2,1,0:T(8,128)(2,1)S(1)}, bf16[3,4,2,2,32,128]{5,4,3,2,1,0:T(8,128)(2,1)S(1)}, u32[]{:S(2)}, u32[]{:S(2)}) %collective-permute-start.23) | collective-permute-done | bytes 393248 | tf_op jit(solution)/shard_map/ppermute | solution.py:376
  109.3 2.1 %collective-permute-start.26 = (bf16[4,2,2,32,128]{4,3,2,1,0:T(8,128)(2,1)S(1)}, bf16[4,2,2,32,128]{4,3,2,1,0:T(8,128)(2,1)S(1)}, u32[]{:S(2)}, u32[]{:S(2)}) collective-permute-start(bf16[4,2,2,32,128]{4,3,2,1,0:T(8,128)(2,1)S(1)} %get-tuple-element.108), channel_id=1, source_target_pairs={{32,0},{40,8},{48,16},{56,24},{64,32},{72,40},{80,48},{88,56},{96,... | collective-permute-start | bytes 393224 | tf_op jit(solution)/shard_map/ppermute | solution.py:390
  111.4 2.7 %shard_map.105 = (bf16[32,12288]{1,0:T(8,128)(2,1)}, bf16[32,12288]{1,0:T(8,128)(2,1)}) custom-call(s32[3]{0:T(128)} %pad_add_fusion.meta, bf16[32,3072]{1,0:T(8,128)(2,1)} %copy-done.2, bf16[32,3072]{1,0:T(8,128)(2,1)} %copy-done.3, bf16[32,3072]{1,0:T(8,128)(2,1)} %copy-done.8, bf16[32,3072]{1,0:T(8,128)(2,1)} %copy-done.9, bf16[32,3072]{1,0:T(8,128)(2,1)} %copy-done.10, ...), custom_call_target="tpu_custom_call" | custom-call | tf_op jit(solution)/shard_map/pallas_call | solution.py:339
  114.1 4.7 %collective-permute-done.26 = bf16[4,2,2,32,128]{4,3,2,1,0:T(8,128)(2,1)S(1)} collective-permute-done((bf16[4,2,2,32,128]{4,3,2,1,0:T(8,128)(2,1)S(1)}, bf16[4,2,2,32,128]{4,3,2,1,0:T(8,128)(2,1)S(1)}, u32[]{:S(2)}, u32[]{:S(2)}) %collective-permute-start.26) | collective-permute-done | bytes 131104 | tf_op jit(solution)/shard_map/ppermute | solution.py:390
  (104 shorter events, 24.3 us)
Async XLA Ops:
  3.6 5.6 %collective-permute-start = (bf16[2,2,32,128]{3,2,1,0:T(8,128)(2,1)}, bf16[2,2,32,128]{3,2,1,0:T(8,128)(2,1)S(1)}, u32[]{:S(2)}, u32[]{:S(2)}) collective-permute-start(bf16[2,2,32,128]{3,2,1,0:T(8,128)(2,1)} %get-tuple-element.65), channel_id=1, source_target_pairs={{0,8},{8,0},{16,24},{24,16},{32,40},{40,32},{48,56},{56,48},{64,72... | collective-permute-start | bytes 98312 | tf_op jit(solution)/shard_map/ppermute | solution.py:367
  4.3 4.8 %collective-permute-start.1 = (bf16[2,2,32,128]{3,2,1,0:T(8,128)(2,1)}, bf16[2,2,32,128]{3,2,1,0:T(8,128)(2,1)S(1)}, u32[]{:S(2)}, u32[]{:S(2)}) collective-permute-start(bf16[2,2,32,128]{3,2,1,0:T(8,128)(2,1)} %get-tuple-element.66), channel_id=1, source_target_pairs={{0,16},{8,24},{16,0},{24,8},{32,48},{40,56},{48,32},{56,40},{64,80... | collective-permute-start | bytes 98312 | tf_op jit(solution)/shard_map/ppermute | solution.py:367
  4.8 4.4 %collective-permute-start.2 = (bf16[2,2,32,128]{3,2,1,0:T(8,128)(2,1)}, bf16[2,2,32,128]{3,2,1,0:T(8,128)(2,1)S(1)}, u32[]{:S(2)}, u32[]{:S(2)}) collective-permute-start(bf16[2,2,32,128]{3,2,1,0:T(8,128)(2,1)} %get-tuple-element.67), channel_id=1, source_target_pairs={{0,24},{8,16},{16,8},{24,0},{32,56},{40,48},{48,40},{56,32},{64,88... | collective-permute-start | bytes 98312 | tf_op jit(solution)/shard_map/ppermute | solution.py:367
  9.2 10.1 %collective-permute-start.4 = (bf16[1,4,2,2,32,128]{5,4,3,2,1,0:T(8,128)(2,1)S(1)}, bf16[1,4,2,2,32,128]{5,4,3,2,1,0:T(8,128)(2,1)S(1)}, u32[]{:S(2)}, u32[]{:S(2)}) collective-permute-start(bf16[1,4,2,2,32,128]{5,4,3,2,1,0:T(8,128)(2,1)S(1)} %bitcast.26), channel_id=1, source_target_pairs={{0,32},{8,40},{16,48},{24,56},{32,64},{40,72},{48,80},{56,88},{64,... | collective-permute-start | bytes 393224 | tf_op jit(solution)/shard_map/ppermute | solution.py:390
  13.2 8.0 %collective-permute-start.3 = (bf16[1,4,2,2,32,128]{5,4,3,2,1,0:T(8,128)(2,1)S(1)}, bf16[1,4,2,2,32,128]{5,4,3,2,1,0:T(8,128)(2,1)S(1)}, u32[]{:S(2)}, u32[]{:S(2)}) collective-permute-start(bf16[1,4,2,2,32,128]{5,4,3,2,1,0:T(8,128)(2,1)S(1)} %bitcast.27), channel_id=1, source_target_pairs={{0,1},{1,0},{2,3},{3,2},{4,5},{5,4},{6,7},{7,6},{8,15},{9,10},{10,... | collective-permute-start | bytes 393224 | tf_op jit(solution)/shard_map/ppermute | solution.py:376
  21.2 7.0 %collective-permute-start.7 = (bf16[3,4,2,2,32,128]{5,4,3,2,1,0:T(8,128)(2,1)S(1)}, bf16[3,4,2,2,32,128]{5,4,3,2,1,0:T(8,128)(2,1)S(1)}, u32[]{:S(2)}, u32[]{:S(2)}) collective-permute-start(bf16[3,4,2,2,32,128]{5,4,3,2,1,0:T(8,128)(2,1)S(1)} %pad_maximum_fusion.3), channel_id=1, source_target_pairs={{0,7},{1,2},{2,1},{3,4},{4,3},{5,6},{6,5},{7,0},{8,9},{9,8},{10,11... | collective-permute-start | bytes 1179656 | tf_op jit(solution)/shard_map/ppermute | solution.py:376
  21.4 7.1 %collective-permute-start.8 = (bf16[32,3072]{1,0:T(8,128)(2,1)S(1)}, bf16[32,3072]{1,0:T(8,128)(2,1)S(1)}, u32[]{:S(2)}, u32[]{:S(2)}) collective-permute-start(bf16[32,3072]{1,0:T(8,128)(2,1)S(1)} %copy-done.21), channel_id=1, source_target_pairs={{0,16},{8,24},{16,0},{24,8},{32,48},{40,56},{48,32},{56,40},{64,80... | collective-permute-start | bytes 589832 | tf_op jit(solution)/shard_map/ppermute | solution.py:367
  28.5 9.7 %collective-permute-start.9 = (bf16[4,4,2,2,32,128]{5,4,3,2,1,0:T(8,128)(2,1)S(1)}, bf16[4,4,2,2,32,128]{5,4,3,2,1,0:T(8,128)(2,1)S(1)}, u32[]{:S(2)}, u32[]{:S(2)}) collective-permute-start(bf16[4,4,2,2,32,128]{5,4,3,2,1,0:T(8,128)(2,1)S(1)} %pad_maximum_fusion), channel_id=1, source_target_pairs={{0,1},{1,0},{2,3},{3,2},{4,5},{5,4},{6,7},{7,6},{8,15},{9,10},{10,... | collective-permute-start | bytes 1572872 | tf_op jit(solution)/shard_map/ppermute | solution.py:376
  31.2 7.0 %collective-permute-start.10 = (bf16[32,3072]{1,0:T(8,128)(2,1)S(1)}, bf16[32,3072]{1,0:T(8,128)(2,1)S(1)}, u32[]{:S(2)}, u32[]{:S(2)}) collective-permute-start(bf16[32,3072]{1,0:T(8,128)(2,1)S(1)} %copy-done.20), channel_id=1, source_target_pairs={{0,24},{8,16},{16,8},{24,0},{32,56},{40,48},{48,40},{56,32},{64,88... | collective-permute-start | bytes 589832 | tf_op jit(solution)/shard_map/ppermute | solution.py:367
  38.2 8.3 %collective-permute-start.11 = (bf16[4,4,2,2,32,128]{5,4,3,2,1,0:T(8,128)(2,1)S(1)}, bf16[4,4,2,2,32,128]{5,4,3,2,1,0:T(8,128)(2,1)S(1)}, u32[]{:S(2)}, u32[]{:S(2)}) collective-permute-start(bf16[4,4,2,2,32,128]{5,4,3,2,1,0:T(8,128)(2,1)S(1)} %collective-permute-done.9.refs_10_), channel_id=1, source_target_pairs={{0,7},{1,2},{2,1},{3,4},{4,3},{5,6},{6,5},{7,0},{8,9},{9,8},{10,11... | collective-permute-start | bytes 1572872 | tf_op jit(solution)/shard_map/ppermute | solution.py:376
  38.2 4.6 %collective-permute-start.12 = (bf16[32,3072]{1,0:T(8,128)(2,1)S(1)}, bf16[32,3072]{1,0:T(8,128)(2,1)S(1)}, u32[]{:S(2)}, u32[]{:S(2)}) collective-permute-start(bf16[32,3072]{1,0:T(8,128)(2,1)S(1)} %copy-done.19), channel_id=1, source_target_pairs={{0,16},{8,24},{16,0},{24,8},{32,48},{40,56},{48,32},{56,40},{64,80... | collective-permute-start | bytes 589832 | tf_op jit(solution)/shard_map/ppermute | solution.py:367
  46.5 9.4 %collective-permute-start.14 = (bf16[2,4,2,2,32,128]{5,4,3,2,1,0:T(8,128)(2,1)S(1)}, bf16[2,4,2,2,32,128]{5,4,3,2,1,0:T(8,128)(2,1)S(1)}, u32[]{:S(2)}, u32[]{:S(2)}) collective-permute-start(bf16[2,4,2,2,32,128]{5,4,3,2,1,0:T(8,128)(2,1)S(1)} %slice.59), channel_id=1, source_target_pairs={{0,1},{1,0},{2,3},{3,2},{4,5},{5,4},{6,7},{7,6},{8,15},{9,10},{10,... | collective-permute-start | bytes 786440 | tf_op jit(solution)/shard_map/ppermute | solution.py:376
  48.9 7.1 %collective-permute-start.13 = (bf16[32,3072]{1,0:T(8,128)(2,1)S(1)}, bf16[32,3072]{1,0:T(8,128)(2,1)S(1)}, u32[]{:S(2)}, u32[]{:S(2)}) collective-permute-start(bf16[32,3072]{1,0:T(8,128)(2,1)S(1)} %copy-done.18), channel_id=1, source_target_pairs={{0,24},{8,16},{16,8},{24,0},{32,56},{40,48},{48,40},{56,32},{64,88... | collective-permute-start | bytes 589832 | tf_op jit(solution)/shard_map/ppermute | solution.py:367
  71.7 6.5 %collective-permute-start.15 = (bf16[2,4,2,2,32,128]{5,4,3,2,1,0:T(8,128)(2,1)S(1)}, bf16[2,4,2,2,32,128]{5,4,3,2,1,0:T(8,128)(2,1)S(1)}, u32[]{:S(2)}, u32[]{:S(2)}) collective-permute-start(bf16[2,4,2,2,32,128]{5,4,3,2,1,0:T(8,128)(2,1)S(1)} %get-tuple-element.95), channel_id=1, source_target_pairs={{0,1},{1,0},{2,3},{3,2},{4,5},{5,4},{6,7},{7,6},{8,15},{9,10},{10,... | collective-permute-start | bytes 786440 | tf_op jit(solution)/shard_map/ppermute | solution.py:376
  72.7 5.7 %collective-permute-start.16 = (bf16[32,3072]{1,0:T(8,128)(2,1)S(1)}, bf16[32,3072]{1,0:T(8,128)(2,1)S(1)}, u32[]{:S(2)}, u32[]{:S(2)}) collective-permute-start(bf16[32,3072]{1,0:T(8,128)(2,1)S(1)} %get-tuple-element.96), channel_id=1, source_target_pairs={{0,8},{8,0},{16,24},{24,16},{32,40},{40,32},{48,56},{56,48},{64,72... | collective-permute-start | bytes 589832 | tf_op jit(solution)/shard_map/ppermute | solution.py:367
  78.4 8.4 %collective-permute-start.18 = (bf16[4,4,2,2,32,128]{5,4,3,2,1,0:T(8,128)(2,1)S(1)}, bf16[4,4,2,2,32,128]{5,4,3,2,1,0:T(8,128)(2,1)S(1)}, u32[]{:S(2)}, u32[]{:S(2)}) collective-permute-start(bf16[4,4,2,2,32,128]{5,4,3,2,1,0:T(8,128)(2,1)S(1)} %pad_maximum_fusion.1), channel_id=1, source_target_pairs={{0,7},{1,2},{2,1},{3,4},{4,3},{5,6},{6,5},{7,0},{8,9},{9,8},{10,11... | collective-permute-start | bytes 1572872 | tf_op jit(solution)/shard_map/ppermute | solution.py:376
  79.2 7.9 %collective-permute-start.19 = (bf16[32,3072]{1,0:T(8,128)(2,1)S(1)}, bf16[32,3072]{1,0:T(8,128)(2,1)S(1)}, u32[]{:S(2)}, u32[]{:S(2)}) collective-permute-start(bf16[32,3072]{1,0:T(8,128)(2,1)S(1)} %get-tuple-element.100), channel_id=1, source_target_pairs={{0,16},{8,24},{16,0},{24,8},{32,48},{40,56},{48,32},{56,40},{64,80... | collective-permute-start | bytes 589832 | tf_op jit(solution)/shard_map/ppermute | solution.py:367
  80.7 9.4 %collective-permute-start.20 = (bf16[32,3072]{1,0:T(8,128)(2,1)S(1)}, bf16[32,3072]{1,0:T(8,128)(2,1)S(1)}, u32[]{:S(2)}, u32[]{:S(2)}) collective-permute-start(bf16[32,3072]{1,0:T(8,128)(2,1)S(1)} %get-tuple-element.101), channel_id=1, source_target_pairs={{0,24},{8,16},{16,8},{24,0},{32,56},{40,48},{48,40},{56,32},{64,88... | collective-permute-start | bytes 589832 | tf_op jit(solution)/shard_map/ppermute | solution.py:367
  90.1 9.2 %collective-permute-start.21 = (bf16[4,4,2,2,32,128]{5,4,3,2,1,0:T(8,128)(2,1)S(1)}, bf16[4,4,2,2,32,128]{5,4,3,2,1,0:T(8,128)(2,1)S(1)}, u32[]{:S(2)}, u32[]{:S(2)}) collective-permute-start(bf16[4,4,2,2,32,128]{5,4,3,2,1,0:T(8,128)(2,1)S(1)} %pad_maximum_fusion.2), channel_id=1, source_target_pairs={{0,1},{1,0},{2,3},{3,2},{4,5},{5,4},{6,7},{7,6},{8,15},{9,10},{10,... | collective-permute-start | bytes 1572872 | tf_op jit(solution)/shard_map/ppermute | solution.py:376
  91.7 7.9 %collective-permute-start.22 = (bf16[32,3072]{1,0:T(8,128)(2,1)S(1)}, bf16[32,3072]{1,0:T(8,128)(2,1)S(1)}, u32[]{:S(2)}, u32[]{:S(2)}) collective-permute-start(bf16[32,3072]{1,0:T(8,128)(2,1)S(1)} %get-tuple-element.104), channel_id=1, source_target_pairs={{0,16},{8,24},{16,0},{24,8},{32,48},{40,56},{48,32},{56,40},{64,80... | collective-permute-start | bytes 589832 | tf_op jit(solution)/shard_map/ppermute | solution.py:367
  99.6 7.0 %collective-permute-start.23 = (bf16[3,4,2,2,32,128]{5,4,3,2,1,0:T(8,128)(2,1)S(1)}, bf16[3,4,2,2,32,128]{5,4,3,2,1,0:T(8,128)(2,1)S(1)}, u32[]{:S(2)}, u32[]{:S(2)}) collective-permute-start(bf16[3,4,2,2,32,128]{5,4,3,2,1,0:T(8,128)(2,1)S(1)} %pad_maximum_fusion.4), channel_id=1, source_target_pairs={{0,7},{1,2},{2,1},{3,4},{4,3},{5,6},{6,5},{7,0},{8,9},{9,8},{10,11... | collective-permute-start | bytes 1179656 | tf_op jit(solution)/shard_map/ppermute | solution.py:376
  100.0 7.4 %collective-permute-start.24 = (bf16[32,3072]{1,0:T(8,128)(2,1)S(1)}, bf16[32,3072]{1,0:T(8,128)(2,1)S(1)}, u32[]{:S(2)}, u32[]{:S(2)}) collective-permute-start(bf16[32,3072]{1,0:T(8,128)(2,1)S(1)} %get-tuple-element.106), channel_id=1, source_target_pairs={{0,24},{8,16},{16,8},{24,0},{32,56},{40,48},{48,40},{56,32},{64,88... | collective-permute-start | bytes 589832 | tf_op jit(solution)/shard_map/ppermute | solution.py:367
  107.5 6.6 %collective-permute-start.25 = (bf16[4,2,2,32,128]{4,3,2,1,0:T(8,128)(2,1)S(1)}, bf16[4,2,2,32,128]{4,3,2,1,0:T(8,128)(2,1)S(1)}, u32[]{:S(2)}, u32[]{:S(2)}) collective-permute-start(bf16[4,2,2,32,128]{4,3,2,1,0:T(8,128)(2,1)S(1)} %get-tuple-element.107), channel_id=1, source_target_pairs={{0,1},{1,0},{2,3},{3,2},{4,5},{5,4},{6,7},{7,6},{8,15},{9,10},{10,... | collective-permute-start | bytes 393224 | tf_op jit(solution)/shard_map/ppermute | solution.py:376
  109.3 9.6 %collective-permute-start.26 = (bf16[4,2,2,32,128]{4,3,2,1,0:T(8,128)(2,1)S(1)}, bf16[4,2,2,32,128]{4,3,2,1,0:T(8,128)(2,1)S(1)}, u32[]{:S(2)}, u32[]{:S(2)}) collective-permute-start(bf16[4,2,2,32,128]{4,3,2,1,0:T(8,128)(2,1)S(1)} %get-tuple-element.108), channel_id=1, source_target_pairs={{32,0},{40,8},{48,16},{56,24},{64,32},{72,40},{80,48},{88,56},{96,... | collective-permute-start | bytes 393224 | tf_op jit(solution)/shard_map/ppermute | solution.py:390
  (29 other events, 309.9 us)

commit v4 on v3

--- a/solution.py
+++ b/solution.py
@@ -51,9 +51,9 @@
         copy.wait()
 
 
-def split_kv_body(meta, keys, values, *refs):
+def split_kv_body(keys, values, *refs):
     outs, sem = refs[:GROUP], refs[GROUP]
-    group_at = meta[0]
+    group_at = lax.axis_index("ctx") & 3
     copies = []
     for d in range(GROUP):
         for n, source in enumerate((keys, values)):
@@ -67,14 +67,14 @@
     run_copies(copies)
 
 
-def split_kv(meta, keys, values):
+def split_kv(keys, values):
     return pl.pallas_call(
         split_kv_body,
-        in_specs=[SMEM, ANY, ANY],
+        in_specs=[ANY, ANY],
         out_specs=[VMEM] * GROUP,
         out_shape=[bf16(2, 2, TB, HD)] * GROUP,
         scratch_shapes=[pltpu.SemaphoreType.DMA((4 * GROUP,))],
-    )(meta, keys, values)
+    )(keys, values)
 
 
 def split_queries_body(meta, queries, grads, *refs):
@@ -125,21 +125,15 @@
                 )
             )
     own = columns(group_at * HW, HW)
-    copies += [
-        pltpu.make_async_copy(queries.at[:, own], qs.at[0], sem_q),
-        pltpu.make_async_copy(grads.at[:, own], gs.at[0], sem_q),
+    own_copies = [
+        pltpu.make_async_copy(queries.at[:, own], qs, sem_q),
+        pltpu.make_async_copy(grads.at[:, own], gs, sem_q),
     ]
-    for d in range(3):
-        copies.append(pltpu.make_async_copy(sent[d], qs.at[d + 1], sem_q))
-        copies.append(pltpu.make_async_copy(sent[3 + d], gs.at[d + 1], sem_q))
-    kv_copies = len(copies) - 8
-    for copy in copies[kv_copies:] + copies[:kv_copies]:
+    for copy in own_copies + copies:
         copy.start()
     for h in range(2):
         acc_k[h][...] = jnp.zeros_like(acc_k[h])
         acc_v[h][...] = jnp.zeros_like(acc_v[h])
-    for copy in copies[kv_copies:]:
-        copy.wait()
 
     def dot(a, b, dims):
         return lax.dot_general(a, b, dims, preferred_element_type=jnp.float32)
@@ -157,21 +151,25 @@
     def head_columns(h, m):
         return slice((h * QPK + m) * HD, (h * QPK + m + 1) * HD)
 
-    for d in range(4):
+    for d in (1, 2, 3, 0):
+        from_q, from_g = (sent[d - 1], sent[d + 2]) if d else (qs, gs)
+        if d == 0:
+            for copy in own_copies:
+                copy.wait()
         token = 1024 * pair_at + CHUNK * (group_at ^ d) + TB * z_at
         token = token + lax.broadcasted_iota(jnp.int32, (TB, HD), 0)
         scaling = jnp.zeros((TB, HD), jnp.float32)
         for n in range(n_docs):
             scaling = jnp.where(doc_starts[n] <= token, tenant_weight[doc_tenant[n]], scaling)
         for h in range(2):
-            raw = [qs[d, :, head_columns(h, m)] for m in range(QPK)]
+            raw = [from_q[:, head_columns(h, m)] for m in range(QPK)]
             head_q[h][d] = jnp.concatenate(raw, axis=0)
             head_qt[h][d] = flip_back(jnp.concatenate(raw, axis=0))
-            raw = [gs[d, :, head_columns(h, m)].astype(jnp.float32) * scaling for m in range(QPK)]
+            raw = [from_g[:, head_columns(h, m)].astype(jnp.float32) * scaling for m in range(QPK)]
             raw = jnp.concatenate([part.astype(jnp.bfloat16) for part in raw], axis=0)
             head_wn[h][d] = raw
             head_w[h][d] = flip_back(raw)
-    for copy in copies[:kv_copies]:
+    for copy in copies:
         copy.wait()
 
     window_at = 1024 * (pair_at - 1)
@@ -316,7 +314,7 @@
         + [vmem(jnp.bfloat16, 4, ROWS, HD)] * 2
         + [vmem(jnp.bfloat16, 4, HD, ROWS)] * 4
         + [vmem(jnp.bfloat16, 4, ROWS, HD)] * 2
-        + [vmem(jnp.bfloat16, 4, TB, HW)] * 2
+        + [vmem(jnp.bfloat16, TB, HW)] * 2
         + [vmem(jnp.bfloat16, 4, 2, TB, HW)]
         + [pltpu.SemaphoreType.DMA] * 3,
         compiler_params=pltpu.CompilerParams(vmem_limit_bytes=40 * 1024 * 1024),
@@ -395,7 +393,7 @@
     z_at = lax.axis_index("hg")
     meta = jnp.stack([ctx_at & 3, z_at, ctx_at >> 2]).astype(jnp.int32)
 
-    kv = split_kv(meta, key_states, value_states)
+    kv = split_kv(key_states, value_states)
     own = jnp.stack([kv[0]] + [swap_in_group(kv[d], d) for d in range(1, GROUP)])
     sent = split_queries(meta, query_states, out_grad)
     own, sent = lax.optimization_barrier((own, sent))

time: 129 us -> 128 us (level)
  the two profiles are of different devices: /device:TPU:25 before, /device:TPU:2 now
where the time goes in v4:
time: 128 us
  waiting for transfers between devices  62.7 us (49%)
  starting transfers between devices  34.4 us (27%)
  Pallas kernels  26 us (20%)
  local copies, waits for them, and re-layouts  1.99 us (2%)
  other arithmetic  1.43 us (1%)
    ppermute x10, waiting for transfers between devices, swap_on_z(): return lax.ppermute(x, ('ctx', 'hg'), pairs)  36.8 us
    ppermute x18, waiting for transfers between devices, swap_in_group(): lax.ppermute(x, 'ctx', [(i, i ^ d) for i in range(lax.axis_size('ctx'))])  22.4 us
    pallas_call x1, Pallas kernels, attention(): pl.pallas_call(attention_body, in_specs=[SMEM] * 4 + [ANY] * 2 + [VMEM] *...  17 us
    ppermute x18, starting transfers between devices, swap_in_group(): lax.ppermute(x, 'ctx', [(i, i ^ d) for i in range(lax.axis_size('ctx'))])  15 us
    ppermute x10, starting transfers between devices, swap_on_z(): return lax.ppermute(x, ('ctx', 'hg'), pairs)  12.2 us
    ppermute x2, starting transfers between devices, shift_pairs(): return lax.ppermute(x, 'ctx', pairs)  7.17 us
    ppermute x2, waiting for transfers between devices, shift_pairs(): return lax.ppermute(x, 'ctx', pairs)  3.44 us
    pallas_call x1, Pallas kernels, split_queries(): pl.pallas_call(split_queries_body, in_specs=[SMEM, ANY, ANY], out_specs=[...  3.21 us
  transfers between devices with their start and end apart: 30, of which 16 were waited for; matrix products, arithmetic and copies ran while one was open for 1% of the time, Pallas kernels for 5%

profile of v4, /device:TPU:2, one launch (start us, length us, event | category | flops | bytes accessed | tf_op | source)
XLA Modules:
  0.0 127.6 jit_solution(8682740613240856770)
XLA Ops:
  0.6 1.7 %shard_map.102 = (bf16[2,2,32,128]{3,2,1,0:T(8,128)(2,1)}, bf16[2,2,32,128]{3,2,1,0:T(8,128)(2,1)}, bf16[2,2,32,128]{3,2,1,0:T(8,128)(2,1)}, bf16[2,2,32,128]{3,2,1,0:T(8,128)(2,1)}) custom-call(bf16[32,1024]{1,0:T(8,128)(2,1)} %keys.1, bf16[32,1024]{1,0:T(8,128)(2,1)} %values.1), custom_call_target="tpu_custom_call" | custom-call | tf_op jit(solution)/shard_map/pallas_call | solution.py:71
  2.4 1.7 %collective-permute-start.1 = (bf16[2,2,32,128]{3,2,1,0:T(8,128)(2,1)}, bf16[2,2,32,128]{3,2,1,0:T(8,128)(2,1)S(1)}, u32[]{:S(2)}, u32[]{:S(2)}) collective-permute-start(bf16[2,2,32,128]{3,2,1,0:T(8,128)(2,1)} %get-tuple-element.66), channel_id=1, source_target_pairs={{0,16},{8,24},{16,0},{24,8},{32,48},{40,56},{48,32},{56,40},{64,80... | collective-permute-start | bytes 98312 | tf_op jit(solution)/shard_map/ppermute | solution.py:365
  4.9 3.2 %shard_map.103 = (bf16[32,3072]{1,0:T(8,128)(2,1)}, bf16[32,3072]{1,0:T(8,128)(2,1)}, bf16[32,3072]{1,0:T(8,128)(2,1)}, bf16[32,3072]{1,0:T(8,128)(2,1)}, bf16[3...) custom-call(s32[3]{0:T(128)} %pad_add_fusion.meta, bf16[32,12288]{1,0:T(8,128)(2,1)} %queries.3, bf16[32,12288]{1,0:T(8,128)(2,1)} %grads.3), custom_call_target="tpu_custom_call" | custom-call | tf_op jit(solution)/shard_map/pallas_call | solution.py:97
  8.2 5.2 %collective-permute-start.4 = (bf16[1,4,2,2,32,128]{5,4,3,2,1,0:T(8,128)(2,1)S(1)}, bf16[1,4,2,2,32,128]{5,4,3,2,1,0:T(8,128)(2,1)S(1)}, u32[]{:S(2)}, u32[]{:S(2)}) collective-permute-start(bf16[1,4,2,2,32,128]{5,4,3,2,1,0:T(8,128)(2,1)S(1)} %bitcast.26), channel_id=1, source_target_pairs={{0,32},{8,40},{16,48},{24,56},{32,64},{40,72},{48,80},{56,88},{64,... | collective-permute-start | bytes 393224 | tf_op jit(solution)/shard_map/ppermute | solution.py:388
  13.4 2.0 %collective-permute-start.3 = (bf16[1,4,2,2,32,128]{5,4,3,2,1,0:T(8,128)(2,1)S(1)}, bf16[1,4,2,2,32,128]{5,4,3,2,1,0:T(8,128)(2,1)S(1)}, u32[]{:S(2)}, u32[]{:S(2)}) collective-permute-start(bf16[1,4,2,2,32,128]{5,4,3,2,1,0:T(8,128)(2,1)S(1)} %bitcast.27), channel_id=1, source_target_pairs={{0,1},{1,0},{2,3},{3,2},{4,5},{5,4},{6,7},{7,6},{8,15},{9,10},{10,... | collective-permute-start | bytes 393224 | tf_op jit(solution)/shard_map/ppermute | solution.py:374
  15.4 3.7 %collective-permute-start.5 = (bf16[32,3072]{1,0:T(8,128)(2,1)}, bf16[32,3072]{1,0:T(8,128)(2,1)S(1)}, u32[]{:S(2)}, u32[]{:S(2)}) collective-permute-start(bf16[32,3072]{1,0:T(8,128)(2,1)} %get-tuple-element.75), channel_id=1, source_target_pairs={{0,8},{8,0},{16,24},{24,16},{32,40},{40,32},{48,56},{56,48},{64,72... | collective-permute-start | bytes 589832 | tf_op jit(solution)/shard_map/ppermute | solution.py:365
  20.7 3.8 %collective-permute-start.7 = (bf16[3,4,2,2,32,128]{5,4,3,2,1,0:T(8,128)(2,1)S(1)}, bf16[3,4,2,2,32,128]{5,4,3,2,1,0:T(8,128)(2,1)S(1)}, u32[]{:S(2)}, u32[]{:S(2)}) collective-permute-start(bf16[3,4,2,2,32,128]{5,4,3,2,1,0:T(8,128)(2,1)S(1)} %pad_maximum_fusion.3), channel_id=1, source_target_pairs={{0,7},{1,2},{2,1},{3,4},{4,3},{5,6},{6,5},{7,0},{8,9},{9,8},{10,11... | collective-permute-start | bytes 1179656 | tf_op jit(solution)/shard_map/ppermute | solution.py:374
  26.0 4.3 %collective-permute-done.7.refs_9_ = bf16[3,4,2,2,32,128]{5,4,3,2,1,0:T(8,128)(2,1)S(1)} collective-permute-done((bf16[3,4,2,2,32,128]{5,4,3,2,1,0:T(8,128)(2,1)S(1)}, bf16[3,4,2,2,32,128]{5,4,3,2,1,0:T(8,128)(2,1)S(1)}, u32[]{:S(2)}, u32[]{:S(2)}) %collective-permute-start.7) | collective-permute-done | bytes 393248 | tf_op jit(solution)/shard_map/ppermute | solution.py:374
  32.1 5.8 %collective-permute-done.10.refs_2_ = bf16[32,3072]{1,0:T(8,128)(2,1)S(1)} collective-permute-done((bf16[32,3072]{1,0:T(8,128)(2,1)S(1)}, bf16[32,3072]{1,0:T(8,128)(2,1)S(1)}, u32[]{:S(2)}, u32[]{:S(2)}) %collective-permute-start.10) | collective-permute-done | bytes 196640 | tf_op jit(solution)/shard_map/ppermute | solution.py:365
  37.9 1.8 %collective-permute-done.9.refs_10_ = bf16[4,4,2,2,32,128]{5,4,3,2,1,0:T(8,128)(2,1)S(1)} collective-permute-done((bf16[4,4,2,2,32,128]{5,4,3,2,1,0:T(8,128)(2,1)S(1)}, bf16[4,4,2,2,32,128]{5,4,3,2,1,0:T(8,128)(2,1)S(1)}, u32[]{:S(2)}, u32[]{:S(2)}) %collective-permute-start.9) | collective-permute-done | bytes 524320 | tf_op jit(solution)/shard_map/ppermute | solution.py:374
  39.7 3.2 %collective-permute-start.11 = (bf16[4,4,2,2,32,128]{5,4,3,2,1,0:T(8,128)(2,1)S(1)}, bf16[4,4,2,2,32,128]{5,4,3,2,1,0:T(8,128)(2,1)S(1)}, u32[]{:S(2)}, u32[]{:S(2)}) collective-permute-start(bf16[4,4,2,2,32,128]{5,4,3,2,1,0:T(8,128)(2,1)S(1)} %collective-permute-done.9.refs_10_), channel_id=1, source_target_pairs={{0,7},{1,2},{2,1},{3,4},{4,3},{5,6},{6,5},{7,0},{8,9},{9,8},{10,11... | collective-permute-start | bytes 1572872 | tf_op jit(solution)/shard_map/ppermute | solution.py:374
  44.4 4.2 %collective-permute-done.12.refs_4_ = bf16[32,3072]{1,0:T(8,128)(2,1)S(1)} collective-permute-done((bf16[32,3072]{1,0:T(8,128)(2,1)S(1)}, bf16[32,3072]{1,0:T(8,128)(2,1)S(1)}, u32[]{:S(2)}, u32[]{:S(2)}) %collective-permute-start.12) | collective-permute-done | bytes 196640 | tf_op jit(solution)/shard_map/ppermute | solution.py:365
  48.6 1.5 %collective-permute-done.11.refs_11_ = bf16[4,4,2,2,32,128]{5,4,3,2,1,0:T(8,128)(2,1)S(1)} collective-permute-done((bf16[4,4,2,2,32,128]{5,4,3,2,1,0:T(8,128)(2,1)S(1)}, bf16[4,4,2,2,32,128]{5,4,3,2,1,0:T(8,128)(2,1)S(1)}, u32[]{:S(2)}, u32[]{:S(2)}) %collective-permute-start.11) | collective-permute-done | bytes 524320 | tf_op jit(solution)/shard_map/ppermute | solution.py:374
  50.4 7.2 %collective-permute-done.13.refs_5_ = bf16[32,3072]{1,0:T(8,128)(2,1)S(1)} collective-permute-done((bf16[32,3072]{1,0:T(8,128)(2,1)S(1)}, bf16[32,3072]{1,0:T(8,128)(2,1)S(1)}, u32[]{:S(2)}, u32[]{:S(2)}) %collective-permute-start.13) | collective-permute-done | bytes 196640 | tf_op jit(solution)/shard_map/ppermute | solution.py:365
  57.6 17.0 %shard_map.104 = (bf16[2,4,2,2,32,128]{5,4,3,2,1,0:T(8,128)(2,1)S(1)}, bf16[2,4,2,2,32,128]{5,4,3,2,1,0:T(8,128)(2,1)S(1)}, bf16[2,4,2,2,32,128]{5,4,3,2,1,0:T(8...) custom-call(s32[3]{0:T(128)S(1)} %copy-done.4, ...), custom_call_target="tpu_custom_call" | custom-call | flops 3000000000 | bytes 10000000 | tf_op jit(solution)/shard_map/pallas_call | solution.py:306
  74.6 2.0 %collective-permute-start.15 = (bf16[2,4,2,2,32,128]{5,4,3,2,1,0:T(8,128)(2,1)S(1)}, bf16[2,4,2,2,32,128]{5,4,3,2,1,0:T(8,128)(2,1)S(1)}, u32[]{:S(2)}, u32[]{:S(2)}) collective-permute-start(bf16[2,4,2,2,32,128]{5,4,3,2,1,0:T(8,128)(2,1)S(1)} %get-tuple-element.95), channel_id=1, source_target_pairs={{0,1},{1,0},{2,3},{3,2},{4,5},{5,4},{6,7},{7,6},{8,15},{9,10},{10,... | collective-permute-start | bytes 786440 | tf_op jit(solution)/shard_map/ppermute | solution.py:374
  77.1 3.9 %collective-permute-done.15 = bf16[2,4,2,2,32,128]{5,4,3,2,1,0:T(8,128)(2,1)S(1)} collective-permute-done((bf16[2,4,2,2,32,128]{5,4,3,2,1,0:T(8,128)(2,1)S(1)}, bf16[2,4,2,2,32,128]{5,4,3,2,1,0:T(8,128)(2,1)S(1)}, u32[]{:S(2)}, u32[]{:S(2)}) %collective-permute-start.15) | collective-permute-done | bytes 262176 | tf_op jit(solution)/shard_map/ppermute | solution.py:374
  83.6 8.1 %collective-permute-done.18 = bf16[4,4,2,2,32,128]{5,4,3,2,1,0:T(8,128)(2,1)S(1)} collective-permute-done((bf16[4,4,2,2,32,128]{5,4,3,2,1,0:T(8,128)(2,1)S(1)}, bf16[4,4,2,2,32,128]{5,4,3,2,1,0:T(8,128)(2,1)S(1)}, u32[]{:S(2)}, u32[]{:S(2)}) %collective-permute-start.18) | collective-permute-done | bytes 524320 | tf_op jit(solution)/shard_map/ppermute | solution.py:374
  93.8 8.4 %collective-permute-done.21 = bf16[4,4,2,2,32,128]{5,4,3,2,1,0:T(8,128)(2,1)S(1)} collective-permute-done((bf16[4,4,2,2,32,128]{5,4,3,2,1,0:T(8,128)(2,1)S(1)}, bf16[4,4,2,2,32,128]{5,4,3,2,1,0:T(8,128)(2,1)S(1)}, u32[]{:S(2)}, u32[]{:S(2)}) %collective-permute-start.21) | collective-permute-done | bytes 524320 | tf_op jit(solution)/shard_map/ppermute | solution.py:374
  103.2 8.3 %collective-permute-done.23 = bf16[3,4,2,2,32,128]{5,4,3,2,1,0:T(8,128)(2,1)S(1)} collective-permute-done((bf16[3,4,2,2,32,128]{5,4,3,2,1,0:T(8,128)(2,1)S(1)}, bf16[3,4,2,2,32,128]{5,4,3,2,1,0:T(8,128)(2,1)S(1)}, u32[]{:S(2)}, u32[]{:S(2)}) %collective-permute-start.23) | collective-permute-done | bytes 393248 | tf_op jit(solution)/shard_map/ppermute | solution.py:374
  111.8 1.9 %collective-permute-start.26 = (bf16[4,2,2,32,128]{4,3,2,1,0:T(8,128)(2,1)S(1)}, bf16[4,2,2,32,128]{4,3,2,1,0:T(8,128)(2,1)S(1)}, u32[]{:S(2)}, u32[]{:S(2)}) collective-permute-start(bf16[4,2,2,32,128]{4,3,2,1,0:T(8,128)(2,1)S(1)} %get-tuple-element.108), channel_id=1, source_target_pairs={{32,0},{40,8},{48,16},{56,24},{64,32},{72,40},{80,48},{88,56},{96,... | collective-permute-start | bytes 393224 | tf_op jit(solution)/shard_map/ppermute | solution.py:388
  113.7 2.7 %shard_map.105 = (bf16[32,12288]{1,0:T(8,128)(2,1)}, bf16[32,12288]{1,0:T(8,128)(2,1)}) custom-call(s32[3]{0:T(128)} %pad_add_fusion.meta, bf16[32,3072]{1,0:T(8,128)(2,1)} %copy-done.2, bf16[32,3072]{1,0:T(8,128)(2,1)} %copy-done.3, bf16[32,3072]{1,0:T(8,128)(2,1)} %copy-done.8, bf16[32,3072]{1,0:T(8,128)(2,1)} %copy-done.9, bf16[32,3072]{1,0:T(8,128)(2,1)} %copy-done.10, ...), custom_call_target="tpu_custom_call" | custom-call | tf_op jit(solution)/shard_map/pallas_call | solution.py:337
  116.7 3.4 %collective-permute-done.26 = bf16[4,2,2,32,128]{4,3,2,1,0:T(8,128)(2,1)S(1)} collective-permute-done((bf16[4,2,2,32,128]{4,3,2,1,0:T(8,128)(2,1)S(1)}, bf16[4,2,2,32,128]{4,3,2,1,0:T(8,128)(2,1)S(1)}, u32[]{:S(2)}, u32[]{:S(2)}) %collective-permute-start.26) | collective-permute-done | bytes 131104 | tf_op jit(solution)/shard_map/ppermute | solution.py:388
  126.2 1.5 %shard_map.106 = (bf16[32,1024]{1,0:T(8,128)(2,1)}, bf16[32,1024]{1,0:T(8,128)(2,1)}) custom-call(s32[3]{0:T(128)} %pad_add_fusion.meta, bf16[2,2,32,128]{3,2,1,0:T(8,128)(2,1)} %get-tuple-element.131.refs_0_, bf16[2,2,32,128]{3,2,1,0:T(8,128)(2,1)} %copy-done.16, bf16[2,2,32,128]{3,2,1,0:T(8,128)(2,1)} %copy-done.15, bf16[2,2,32,128]{3,2,1,0:T(8,128)(2,1)} %copy-done.14), custom_call_target="tpu_custom_call" | custom-call | tf_op jit(solution)/shard_map/pallas_call | solution.py:356
  (104 shorter events, 19.8 us)
Async XLA Ops:
  2.3 5.8 %collective-permute-start = (bf16[2,2,32,128]{3,2,1,0:T(8,128)(2,1)}, bf16[2,2,32,128]{3,2,1,0:T(8,128)(2,1)S(1)}, u32[]{:S(2)}, u32[]{:S(2)}) collective-permute-start(bf16[2,2,32,128]{3,2,1,0:T(8,128)(2,1)} %get-tuple-element.65), channel_id=1, source_target_pairs={{0,8},{8,0},{16,24},{24,16},{32,40},{40,32},{48,56},{56,48},{64,72... | collective-permute-start | bytes 98312 | tf_op jit(solution)/shard_map/ppermute | solution.py:365
  2.4 5.7 %collective-permute-start.1 = (bf16[2,2,32,128]{3,2,1,0:T(8,128)(2,1)}, bf16[2,2,32,128]{3,2,1,0:T(8,128)(2,1)S(1)}, u32[]{:S(2)}, u32[]{:S(2)}) collective-permute-start(bf16[2,2,32,128]{3,2,1,0:T(8,128)(2,1)} %get-tuple-element.66), channel_id=1, source_target_pairs={{0,16},{8,24},{16,0},{24,8},{32,48},{40,56},{48,32},{56,40},{64,80... | collective-permute-start | bytes 98312 | tf_op jit(solution)/shard_map/ppermute | solution.py:365
  8.2 11.0 %collective-permute-start.4 = (bf16[1,4,2,2,32,128]{5,4,3,2,1,0:T(8,128)(2,1)S(1)}, bf16[1,4,2,2,32,128]{5,4,3,2,1,0:T(8,128)(2,1)S(1)}, u32[]{:S(2)}, u32[]{:S(2)}) collective-permute-start(bf16[1,4,2,2,32,128]{5,4,3,2,1,0:T(8,128)(2,1)S(1)} %bitcast.26), channel_id=1, source_target_pairs={{0,32},{8,40},{16,48},{24,56},{32,64},{40,72},{48,80},{56,88},{64,... | collective-permute-start | bytes 393224 | tf_op jit(solution)/shard_map/ppermute | solution.py:388
  13.4 5.7 %collective-permute-start.3 = (bf16[1,4,2,2,32,128]{5,4,3,2,1,0:T(8,128)(2,1)S(1)}, bf16[1,4,2,2,32,128]{5,4,3,2,1,0:T(8,128)(2,1)S(1)}, u32[]{:S(2)}, u32[]{:S(2)}) collective-permute-start(bf16[1,4,2,2,32,128]{5,4,3,2,1,0:T(8,128)(2,1)S(1)} %bitcast.27), channel_id=1, source_target_pairs={{0,1},{1,0},{2,3},{3,2},{4,5},{5,4},{6,7},{7,6},{8,15},{9,10},{10,... | collective-permute-start | bytes 393224 | tf_op jit(solution)/shard_map/ppermute | solution.py:374
  15.4 5.2 %collective-permute-start.5 = (bf16[32,3072]{1,0:T(8,128)(2,1)}, bf16[32,3072]{1,0:T(8,128)(2,1)S(1)}, u32[]{:S(2)}, u32[]{:S(2)}) collective-permute-start(bf16[32,3072]{1,0:T(8,128)(2,1)} %get-tuple-element.75), channel_id=1, source_target_pairs={{0,8},{8,0},{16,24},{24,16},{32,40},{40,32},{48,56},{56,48},{64,72... | collective-permute-start | bytes 589832 | tf_op jit(solution)/shard_map/ppermute | solution.py:365
  20.7 9.6 %collective-permute-start.7 = (bf16[3,4,2,2,32,128]{5,4,3,2,1,0:T(8,128)(2,1)S(1)}, bf16[3,4,2,2,32,128]{5,4,3,2,1,0:T(8,128)(2,1)S(1)}, u32[]{:S(2)}, u32[]{:S(2)}) collective-permute-start(bf16[3,4,2,2,32,128]{5,4,3,2,1,0:T(8,128)(2,1)S(1)} %pad_maximum_fusion.3), channel_id=1, source_target_pairs={{0,7},{1,2},{2,1},{3,4},{4,3},{5,6},{6,5},{7,0},{8,9},{9,8},{10,11... | collective-permute-start | bytes 1179656 | tf_op jit(solution)/shard_map/ppermute | solution.py:374
  24.5 6.0 %collective-permute-start.8 = (bf16[32,3072]{1,0:T(8,128)(2,1)S(1)}, bf16[32,3072]{1,0:T(8,128)(2,1)S(1)}, u32[]{:S(2)}, u32[]{:S(2)}) collective-permute-start(bf16[32,3072]{1,0:T(8,128)(2,1)S(1)} %copy-done.21), channel_id=1, source_target_pairs={{0,16},{8,24},{16,0},{24,8},{32,48},{40,56},{48,32},{56,40},{64,80... | collective-permute-start | bytes 589832 | tf_op jit(solution)/shard_map/ppermute | solution.py:365
  30.5 9.3 %collective-permute-start.9 = (bf16[4,4,2,2,32,128]{5,4,3,2,1,0:T(8,128)(2,1)S(1)}, bf16[4,4,2,2,32,128]{5,4,3,2,1,0:T(8,128)(2,1)S(1)}, u32[]{:S(2)}, u32[]{:S(2)}) collective-permute-start(bf16[4,4,2,2,32,128]{5,4,3,2,1,0:T(8,128)(2,1)S(1)} %pad_maximum_fusion), channel_id=1, source_target_pairs={{0,1},{1,0},{2,3},{3,2},{4,5},{5,4},{6,7},{7,6},{8,15},{9,10},{10,... | collective-permute-start | bytes 1572872 | tf_op jit(solution)/shard_map/ppermute | solution.py:374
  31.2 6.8 %collective-permute-start.10 = (bf16[32,3072]{1,0:T(8,128)(2,1)S(1)}, bf16[32,3072]{1,0:T(8,128)(2,1)S(1)}, u32[]{:S(2)}, u32[]{:S(2)}) collective-permute-start(bf16[32,3072]{1,0:T(8,128)(2,1)S(1)} %copy-done.20), channel_id=1, source_target_pairs={{0,24},{8,16},{16,8},{24,0},{32,56},{40,48},{48,40},{56,32},{64,88... | collective-permute-start | bytes 589832 | tf_op jit(solution)/shard_map/ppermute | solution.py:365
  39.7 10.4 %collective-permute-start.11 = (bf16[4,4,2,2,32,128]{5,4,3,2,1,0:T(8,128)(2,1)S(1)}, bf16[4,4,2,2,32,128]{5,4,3,2,1,0:T(8,128)(2,1)S(1)}, u32[]{:S(2)}, u32[]{:S(2)}) collective-permute-start(bf16[4,4,2,2,32,128]{5,4,3,2,1,0:T(8,128)(2,1)S(1)} %collective-permute-done.9.refs_10_), channel_id=1, source_target_pairs={{0,7},{1,2},{2,1},{3,4},{4,3},{5,6},{6,5},{7,0},{8,9},{9,8},{10,11... | collective-permute-start | bytes 1572872 | tf_op jit(solution)/shard_map/ppermute | solution.py:374
  43.0 5.7 %collective-permute-start.12 = (bf16[32,3072]{1,0:T(8,128)(2,1)S(1)}, bf16[32,3072]{1,0:T(8,128)(2,1)S(1)}, u32[]{:S(2)}, u32[]{:S(2)}) collective-permute-start(bf16[32,3072]{1,0:T(8,128)(2,1)S(1)} %copy-done.19), channel_id=1, source_target_pairs={{0,16},{8,24},{16,0},{24,8},{32,48},{40,56},{48,32},{56,40},{64,80... | collective-permute-start | bytes 589832 | tf_op jit(solution)/shard_map/ppermute | solution.py:365
  50.2 7.4 %collective-permute-start.14 = (bf16[2,4,2,2,32,128]{5,4,3,2,1,0:T(8,128)(2,1)S(1)}, bf16[2,4,2,2,32,128]{5,4,3,2,1,0:T(8,128)(2,1)S(1)}, u32[]{:S(2)}, u32[]{:S(2)}) collective-permute-start(bf16[2,4,2,2,32,128]{5,4,3,2,1,0:T(8,128)(2,1)S(1)} %slice.59), channel_id=1, source_target_pairs={{0,1},{1,0},{2,3},{3,2},{4,5},{5,4},{6,7},{7,6},{8,15},{9,10},{10,... | collective-permute-start | bytes 786440 | tf_op jit(solution)/shard_map/ppermute | solution.py:374
  50.3 7.3 %collective-permute-start.13 = (bf16[32,3072]{1,0:T(8,128)(2,1)S(1)}, bf16[32,3072]{1,0:T(8,128)(2,1)S(1)}, u32[]{:S(2)}, u32[]{:S(2)}) collective-permute-start(bf16[32,3072]{1,0:T(8,128)(2,1)S(1)} %copy-done.18), channel_id=1, source_target_pairs={{0,24},{8,16},{16,8},{24,0},{32,56},{40,48},{48,40},{56,32},{64,88... | collective-permute-start | bytes 589832 | tf_op jit(solution)/shard_map/ppermute | solution.py:365
  74.6 6.5 %collective-permute-start.15 = (bf16[2,4,2,2,32,128]{5,4,3,2,1,0:T(8,128)(2,1)S(1)}, bf16[2,4,2,2,32,128]{5,4,3,2,1,0:T(8,128)(2,1)S(1)}, u32[]{:S(2)}, u32[]{:S(2)}) collective-permute-start(bf16[2,4,2,2,32,128]{5,4,3,2,1,0:T(8,128)(2,1)S(1)} %get-tuple-element.95), channel_id=1, source_target_pairs={{0,1},{1,0},{2,3},{3,2},{4,5},{5,4},{6,7},{7,6},{8,15},{9,10},{10,... | collective-permute-start | bytes 786440 | tf_op jit(solution)/shard_map/ppermute | solution.py:374
  76.6 4.6 %collective-permute-start.17 = (bf16[32,3072]{1,0:T(8,128)(2,1)S(1)}, bf16[32,3072]{1,0:T(8,128)(2,1)S(1)}, u32[]{:S(2)}, u32[]{:S(2)}) collective-permute-start(bf16[32,3072]{1,0:T(8,128)(2,1)S(1)} %get-tuple-element.97), channel_id=1, source_target_pairs={{0,8},{8,0},{16,24},{24,16},{32,40},{40,32},{48,56},{56,48},{64,72... | collective-permute-start | bytes 589832 | tf_op jit(solution)/shard_map/ppermute | solution.py:365
  81.2 10.5 %collective-permute-start.18 = (bf16[4,4,2,2,32,128]{5,4,3,2,1,0:T(8,128)(2,1)S(1)}, bf16[4,4,2,2,32,128]{5,4,3,2,1,0:T(8,128)(2,1)S(1)}, u32[]{:S(2)}, u32[]{:S(2)}) collective-permute-start(bf16[4,4,2,2,32,128]{5,4,3,2,1,0:T(8,128)(2,1)S(1)} %pad_maximum_fusion.1), channel_id=1, source_target_pairs={{0,7},{1,2},{2,1},{3,4},{4,3},{5,6},{6,5},{7,0},{8,9},{9,8},{10,11... | collective-permute-start | bytes 1572872 | tf_op jit(solution)/shard_map/ppermute | solution.py:374
  81.4 10.6 %collective-permute-start.19 = (bf16[32,3072]{1,0:T(8,128)(2,1)S(1)}, bf16[32,3072]{1,0:T(8,128)(2,1)S(1)}, u32[]{:S(2)}, u32[]{:S(2)}) collective-permute-start(bf16[32,3072]{1,0:T(8,128)(2,1)S(1)} %get-tuple-element.100), channel_id=1, source_target_pairs={{0,16},{8,24},{16,0},{24,8},{32,48},{40,56},{48,32},{56,40},{64,80... | collective-permute-start | bytes 589832 | tf_op jit(solution)/shard_map/ppermute | solution.py:365
  82.7 10.4 %collective-permute-start.20 = (bf16[32,3072]{1,0:T(8,128)(2,1)S(1)}, bf16[32,3072]{1,0:T(8,128)(2,1)S(1)}, u32[]{:S(2)}, u32[]{:S(2)}) collective-permute-start(bf16[32,3072]{1,0:T(8,128)(2,1)S(1)} %get-tuple-element.101), channel_id=1, source_target_pairs={{0,24},{8,16},{16,8},{24,0},{32,56},{40,48},{48,40},{56,32},{64,88... | collective-permute-start | bytes 589832 | tf_op jit(solution)/shard_map/ppermute | solution.py:365
  93.1 9.2 %collective-permute-start.21 = (bf16[4,4,2,2,32,128]{5,4,3,2,1,0:T(8,128)(2,1)S(1)}, bf16[4,4,2,2,32,128]{5,4,3,2,1,0:T(8,128)(2,1)S(1)}, u32[]{:S(2)}, u32[]{:S(2)}) collective-permute-start(bf16[4,4,2,2,32,128]{5,4,3,2,1,0:T(8,128)(2,1)S(1)} %pad_maximum_fusion.2), channel_id=1, source_target_pairs={{0,1},{1,0},{2,3},{3,2},{4,5},{5,4},{6,7},{7,6},{8,15},{9,10},{10,... | collective-permute-start | bytes 1572872 | tf_op jit(solution)/shard_map/ppermute | solution.py:374
  93.1 9.4 %collective-permute-start.22 = (bf16[32,3072]{1,0:T(8,128)(2,1)S(1)}, bf16[32,3072]{1,0:T(8,128)(2,1)S(1)}, u32[]{:S(2)}, u32[]{:S(2)}) collective-permute-start(bf16[32,3072]{1,0:T(8,128)(2,1)S(1)} %get-tuple-element.104), channel_id=1, source_target_pairs={{0,16},{8,24},{16,0},{24,8},{32,48},{40,56},{48,32},{56,40},{64,80... | collective-permute-start | bytes 589832 | tf_op jit(solution)/shard_map/ppermute | solution.py:365
  102.5 9.1 %collective-permute-start.23 = (bf16[3,4,2,2,32,128]{5,4,3,2,1,0:T(8,128)(2,1)S(1)}, bf16[3,4,2,2,32,128]{5,4,3,2,1,0:T(8,128)(2,1)S(1)}, u32[]{:S(2)}, u32[]{:S(2)}) collective-permute-start(bf16[3,4,2,2,32,128]{5,4,3,2,1,0:T(8,128)(2,1)S(1)} %pad_maximum_fusion.4), channel_id=1, source_target_pairs={{0,7},{1,2},{2,1},{3,4},{4,3},{5,6},{6,5},{7,0},{8,9},{9,8},{10,11... | collective-permute-start | bytes 1179656 | tf_op jit(solution)/shard_map/ppermute | solution.py:374
  103.2 8.4 %collective-permute-start.24 = (bf16[32,3072]{1,0:T(8,128)(2,1)S(1)}, bf16[32,3072]{1,0:T(8,128)(2,1)S(1)}, u32[]{:S(2)}, u32[]{:S(2)}) collective-permute-start(bf16[32,3072]{1,0:T(8,128)(2,1)S(1)} %get-tuple-element.106), channel_id=1, source_target_pairs={{0,24},{8,16},{16,8},{24,0},{32,56},{40,48},{48,40},{56,32},{64,88... | collective-permute-start | bytes 589832 | tf_op jit(solution)/shard_map/ppermute | solution.py:365
  111.7 5.1 %collective-permute-start.25 = (bf16[4,2,2,32,128]{4,3,2,1,0:T(8,128)(2,1)S(1)}, bf16[4,2,2,32,128]{4,3,2,1,0:T(8,128)(2,1)S(1)}, u32[]{:S(2)}, u32[]{:S(2)}) collective-permute-start(bf16[4,2,2,32,128]{4,3,2,1,0:T(8,128)(2,1)S(1)} %get-tuple-element.107), channel_id=1, source_target_pairs={{0,1},{1,0},{2,3},{3,2},{4,5},{5,4},{6,7},{7,6},{8,15},{9,10},{10,... | collective-permute-start | bytes 393224 | tf_op jit(solution)/shard_map/ppermute | solution.py:374
  111.8 8.4 %collective-permute-start.26 = (bf16[4,2,2,32,128]{4,3,2,1,0:T(8,128)(2,1)S(1)}, bf16[4,2,2,32,128]{4,3,2,1,0:T(8,128)(2,1)S(1)}, u32[]{:S(2)}, u32[]{:S(2)}) collective-permute-start(bf16[4,2,2,32,128]{4,3,2,1,0:T(8,128)(2,1)S(1)} %get-tuple-element.108), channel_id=1, source_target_pairs={{32,0},{40,8},{48,16},{56,24},{64,32},{72,40},{80,48},{88,56},{96,... | collective-permute-start | bytes 393224 | tf_op jit(solution)/shard_map/ppermute | solution.py:388
  (29 other events, 316.6 us)
